TPU v7x, 32 devices: a whole 2x2x4 slice. The times are simulated.
32 devices in a mesh: group: 2 (over x), dp: 2 (over core), tensor: 8 (over z, y).
Axes of the slice: x: 2, y: 2, z: 4, core: 2. Of those that a mesh axis runs over, the one named last changes fastest.
Arguments:
- hidden: bfloat16 [1024, 8192], P(('group', 'dp'), 'tensor'), parts along dimension 0, may hold values from -6 to 6
- norm_gain: float32 [2, 8192], replicated, may hold values from 0.1 to 1.9
- w_query: bfloat16 [2, 8192, 4096], P(None, None, 'tensor'), may hold values from -0.0625 to 0.0625
- w_kv: bfloat16 [2, 8192, 1024], P(None, None, 'tensor'), may hold values from -0.0625 to 0.0625
- w_out: bfloat16 [2, 4096, 8192], P(None, 'tensor'), may hold values from -0.125 to 0.125
- cache: bfloat16 [2, 1024, 64, 1024], P(None, ('group', 'dp', 'tensor')), parts along dimension 1, may hold values from -1000 to 1000
- lengths: int32 [1024], P(('group', 'dp')), parts along dimension 0, may hold values from 1 to 64, as said below
- exits: int32 [1024], P(('group', 'dp')), parts along dimension 0, may hold values from 1 to 2, as said below
Outputs:
- result: bfloat16 [1024, 8192], P(('group', 'dp'), 'tensor'), parts along dimension 0
There are 2 independent parts, one for each index of `group`. A program takes and returns all parts, laid end to end along the dimension named above; an argument that names none is the same for every part. Nothing has to cross between parts.
Inputs may be any that keep to these rules, and one draw needn't show every extreme that they name: `exits`: A row passes both layers where 2. Group the rows of every index of dp by place q // 32; over all indices of dp, exactly 32 rows of each such group pass both. How many of them stand on each index of dp varies. `lengths`: the new token stands at this position.
All inputs are finite; a program needn't handle non-finite values.
Results may differ from a plain program's by a relative error of at most 0.023.
Values may be sent and summed in bfloat16 or wider, within the bound.
No kernel may reach another device: no remote copies, remote signals or barrier semaphores. Data moves between devices by JAX's collectives and lax.ppermute only.
A program may use at most 192 MiB of HBM per device.

v0:
```python
import jax
import jax.numpy as jnp
from jax import lax
from jax.sharding import PartitionSpec as P

QH = 32
KVH = 4
HEAD_DIM = 128


EPS = 1e-05
ROPE_BASE = 500000.0
NEGATIVE = -1e30


def rotate(values, position):
    half = values.shape[-1] // 2
    freqs = ROPE_BASE ** (-jnp.arange(half, dtype=jnp.float32) / half)
    angle = position.astype(jnp.float32)[:, None] * freqs[None, :]
    cosine = jnp.cos(angle)[:, None, :]
    sine = jnp.sin(angle)[:, None, :]
    front = values[..., :half]
    back = values[..., half:]
    return jnp.concatenate([front * cosine - back * sine, back * cosine + front * sine], axis=-1)


def layer(level, share, stored_cache, lengths, norm_gain, w_query, w_kv, w_out):
    count, piece_width = share.shape
    parts = lax.axis_size("tensor")
    place_index = lax.axis_index("tensor")
    width = piece_width * parts
    gain = norm_gain[level]
    query_weight = w_query[level]
    fresh_weight = w_kv[level]
    values = lax.all_gather(share, "tensor", axis=1, tiled=True).astype(jnp.float32)
    scaled = (values * gain[None, :]).astype(jnp.bfloat16)
    query_sum = jnp.dot(scaled, query_weight, preferred_element_type=jnp.float32)
    fresh_sum = jnp.dot(scaled, fresh_weight, preferred_element_type=jnp.float32)
    query_sum, fresh_sum, squared_values = (query_sum, fresh_sum, jnp.sum(values * values, axis=1))
    factor = lax.rsqrt(squared_values / width + EPS)[:, None]
    heads_dev = query_weight.shape[1] // HEAD_DIM
    query_own = (
        rotate((query_sum * factor).reshape(count, heads_dev, HEAD_DIM), lengths)
        .astype(jnp.bfloat16)
        .reshape(count, heads_dev * HEAD_DIM)
    )
    fresh_own = (fresh_sum * factor).astype(jnp.bfloat16)
    queries, fresh = (
        lax.all_to_all(query_own, "tensor", split_axis=0, concat_axis=1, tiled=True),
        lax.all_to_all(fresh_own, "tensor", split_axis=0, concat_axis=1, tiled=True),
    )
    local_rows = stored_cache.shape[0]
    local_len = lax.dynamic_slice_in_dim(lengths, place_index * local_rows, local_rows)
    queries = queries.reshape(local_rows, KVH, QH // KVH, HEAD_DIM)
    new_keys = rotate(
        fresh[:, : KVH * HEAD_DIM].reshape(local_rows, KVH, HEAD_DIM).astype(jnp.float32), local_len
    ).astype(jnp.bfloat16)
    new_values = fresh[:, KVH * HEAD_DIM :].reshape(local_rows, KVH, HEAD_DIM).astype(jnp.float32)
    slots = stored_cache.shape[1]
    stored_cache = stored_cache.reshape(local_rows, slots, KVH, 2, HEAD_DIM)
    keys = stored_cache[:, :, :, 0]
    values = stored_cache[:, :, :, 1].astype(jnp.float32)
    scale = HEAD_DIM ** (-0.5)
    scores = (
        jnp.einsum("rkgd,rpkd->rkgp", queries, keys, preferred_element_type=jnp.float32) * scale
    )
    own_score = (
        jnp.einsum("rkgd,rkd->rkg", queries, new_keys, preferred_element_type=jnp.float32) * scale
    )
    valid = (jnp.arange(slots)[None, :] < local_len[:, None])[:, None, None, :]
    highest = jnp.maximum(jnp.max(jnp.where(valid, scores, NEGATIVE), axis=-1), own_score)
    weights = jnp.where(valid, jnp.exp(scores - highest[..., None]), 0.0)
    own_weight = jnp.exp(own_score - highest)
    total = jnp.sum(weights, axis=-1) + own_weight
    mixed = (
        jnp.einsum("rkgp,rpkd->rkgd", weights, values)
        + own_weight[..., None] * new_values[:, :, None, :]
    )
    attended_rows = (
        (mixed / total[..., None]).astype(jnp.bfloat16).reshape(local_rows, QH * HEAD_DIM)
    )
    attended = lax.all_to_all(attended_rows, "tensor", split_axis=1, concat_axis=0, tiled=True)
    branch_part = jnp.dot(attended, w_out[level], preferred_element_type=jnp.float32)
    summed = lax.psum(branch_part.astype(jnp.bfloat16), "tensor").astype(jnp.float32)
    own_branch = lax.dynamic_slice_in_dim(summed, place_index * piece_width, piece_width, 1)
    return (share.astype(jnp.float32) + own_branch).astype(jnp.bfloat16)


def local(hidden, norm_gain, w_query, w_kv, w_out, cache, lengths, exits):
    first = layer(0, hidden, cache[0], lengths, norm_gain, w_query, w_kv, w_out)
    second = layer(1, first, cache[1], lengths, norm_gain, w_query, w_kv, w_out)
    output = jnp.where(exits[:, None] == 2, second, first)
    return output


def solution(mesh):
    in_specs = (
        P(("group", "dp"), "tensor"),
        P(),
        P(None, None, "tensor"),
        P(None, None, "tensor"),
        P(None, "tensor", None),
        P(None, ("group", "dp", "tensor"), None, None),
        P(("group", "dp")),
        P(("group", "dp")),
    )
    out_specs = P(("group", "dp"), "tensor")
    return jax.shard_map(local, mesh=mesh, in_specs=in_specs, out_specs=out_specs, check_vma=False)
```

profile of v0, /device:TPU:0, one launch (start us, length us, event | category | flops | bytes accessed | tf_op | source)
XLA Modules:
  0.0 596.5 jit_solution(17378224672155107828)
XLA Ops:
  6.5 0.7 all-gather.3.cloned.1.call-update
  7.3 0.7 convert_element_type.107
  7.9 6.2 %fusion.84 = (bf16[1,32,64,1024]{3,2,1,0:T(8,128)(2,1)}, bf16[1,32,64,1024]{3,2,1,0:T(8,128)(2,1)}) fusion(bf16[2,32,64,1024]{3,2,1,0:T(8,128)(2,1)} %param.13), kind=kLoop, calls=%fused_computation.103 | loop fusion | bytes 16777216 | tf_op jit(solution)/shard_map/slice | solution.py:91
  14.1 7.8 %reshape_squeeze.6 = bf16[32,64,4,2,128]{4,3,2,1,0:T(2,128)(2,1)} reshape(bf16[1,32,64,1024]{3,2,1,0:T(8,128)(2,1)} %get-tuple-element.12) | data formatting | bytes 8388608 | tf_op jit(solution)/shard_map/reshape;squeeze | solution.py:60
  22.3 0.5 multiply_cosine_fusion
  22.8 10.2 %fusion.86 = (bf16[32,64,4,1,128]{4,3,2,1,0:T(2,128)(2,1)}, bf16[32,64,4,1,128]{4,3,2,1,0:T(2,128)(2,1)}) fusion(bf16[32,64,4,2,128]{4,3,2,1,0:T(2,128)(2,1)} %reshape_squeeze.6), kind=kLoop, calls=%fused_computation.105 | loop fusion | bytes 8388608 | tf_op jit(solution)/shard_map/slice | solution.py:61
  33.1 52.6 %all-gather.3.cloned.1.call-done = bf16[256,8192]{1,0:T(8,128)(2,1)} async-done(((bf16[256,1024]{1,0:T(8,128)(2,1)}), bf16[256,8192]{1,0:T(8,128)(2,1)}) %all-gather.3.cloned.1.call-update) | async-done | bytes 4194320 | tf_op jit(solution)/shard_map/all_gather | solution.py:35
  85.7 3.3 fusion.1
  88.9 0.2 copy-done.1
  89.1 3.5 fusion.61
  92.6 3.3 all-to-all-start.1
  95.9 7.0 %fusion.34 = f32[256,512]{1,0:T(8,128)S(1)} fusion(bf16[2,8192,512]{2,1,0:T(8,128)(2,1)} %param.10, bf16[256,8192]{1,0:T(8,128)(2,1)} %all-gather.3.cloned.1.call-done, f32[8192]{0:T(1024)S(1)} %bitcast.119, f32[256]{0:T(256)S(1)} %add_rsqrt_fusion.1), kind=kOutput, calls=%fused_computation.40 | convolution fusion | flops 2153906176 | bytes 13140992 | tf_op jit(solution)/shard_map/dot_general | solution.py:37
  103.1 0.5 subtract_convert_fusion.1
  103.6 0.4 pad_maximum_fusion
  104.0 0.8 convert_element_type.108
  104.8 5.9 all-to-all-start
  111.0 7.9 %all-to-all-done = bf16[8,32,512]{2,1,0:T(8,128)(2,1)S(1)} async-done(((bf16[8,32,512]{2,1,0:T(8,128)(2,1)}), bf16[8,32,512]{2,1,0:T(8,128)(2,1)S(1)}, u32[]{:S(2)}, u32[]{:S(2)}) %all-to-all-start) | async-done | bytes 262176 | tf_op jit(solution)/shard_map/all_to_all | solution.py:49
  119.3 0.3 fusion.77
  119.6 3.6 select_reduce_fusion.1
  123.2 0.5 fusion.67
  123.8 0.7 fusion.45
  124.7 11.7 %all_to_all.102 = bf16[32,8,512]{2,0,1:T(8,128)(2,1)S(1)} all-to-all(bf16[32,8,512]{2,0,1:T(8,128)(2,1)S(1)} %copy.25), channel_id=1, replica_groups=mesh['group'=2,'dp'=2,'tensor'=8] {'tensor'}, dimensions={1} | all-to-all | bytes 524288 | tf_op jit(solution)/shard_map/all_to_all | solution.py:82
  136.4 7.7 %convolution_convert_fusion.1 = bf16[256,8192]{1,0:T(8,128)(2,1)} fusion(bf16[256,512]{1,0:T(8,128)(2,1)S(1)} %bitcast.114, bf16[2,512,8192]{2,1,0:T(8,128)(2,1)} %param.12), kind=kOutput, calls=%fused_computation.5 | convolution fusion | flops 2149580800 | bytes 12845056 | tf_op jit(solution)/shard_map/dot_general | solution.py:83
  144.2 155.2 %all-reduce.3.cloned.1.call-done = bf16[256,8192]{1,0:T(8,128)(2,1)} async-done(((bf16[256,8192]{1,0:T(8,128)(2,1)}), bf16[256,8192]{1,0:T(8,128)(2,1)}) %all-reduce.3.cloned.1.call-update) | async-done | bytes 4194320 | tf_op jit(solution)/shard_map/psum | solution.py:84
  299.4 2.0 add_convert_fusion.1
  301.5 7.8 %reshape_squeeze.7 = bf16[32,64,4,2,128]{4,3,2,1,0:T(2,128)(2,1)} reshape(bf16[1,32,64,1024]{3,2,1,0:T(8,128)(2,1)} %get-tuple-element.11) | data formatting | bytes 8388608 | tf_op jit(solution)/shard_map/reshape;squeeze | solution.py:60
  309.3 10.3 %fusion.85 = (bf16[32,64,4,1,128]{4,3,2,1,0:T(2,128)(2,1)}, bf16[32,64,4,1,128]{4,3,2,1,0:T(2,128)(2,1)}) fusion(bf16[32,64,4,2,128]{4,3,2,1,0:T(2,128)(2,1)} %reshape_squeeze.7), kind=kLoop, calls=%fused_computation.104 | loop fusion | bytes 8388608 | tf_op jit(solution)/shard_map/slice | solution.py:61
  319.5 54.5 %all-gather.5.cloned.1.call-done = bf16[256,8192]{1,0:T(8,128)(2,1)} async-done(((bf16[256,1024]{1,0:T(8,128)(2,1)}), bf16[256,8192]{1,0:T(8,128)(2,1)}) %all-gather.5.cloned.1.call-update) | async-done | bytes 4194320 | tf_op jit(solution)/shard_map/all_gather | solution.py:35
  374.0 3.3 fusion.3
  377.3 0.2 copy-done.2
  377.5 3.5 fusion.56
  381.0 3.3 all-to-all-start.4
  384.3 7.0 %fusion.39 = f32[256,512]{1,0:T(8,128)S(1)} fusion(bf16[2,8192,512]{2,1,0:T(8,128)(2,1)} %param.10, bf16[256,8192]{1,0:T(8,128)(2,1)} %all-gather.5.cloned.1.call-done, f32[8192]{0:T(1024)S(1)} %bitcast.117, f32[256]{0:T(256)S(1)} %add_rsqrt_fusion), kind=kOutput, calls=%fused_computation.41 | convolution fusion | flops 2153906176 | bytes 13140992 | tf_op jit(solution)/shard_map/dot_general | solution.py:37
  391.5 0.5 subtract_convert_fusion
  392.0 0.4 pad_maximum_fusion.1
  392.4 0.8 convert_element_type.122
  393.2 5.9 all-to-all-start.3
  399.1 0.3 all-reduce.5.cloned.1.call-start
  399.7 7.7 %all-to-all-done.3 = bf16[8,32,512]{2,1,0:T(8,128)(2,1)S(1)} async-done(((bf16[8,32,512]{2,1,0:T(8,128)(2,1)}), bf16[8,32,512]{2,1,0:T(8,128)(2,1)S(1)}, u32[]{:S(2)}, u32[]{:S(2)}) %all-to-all-start.3) | async-done | bytes 262176 | tf_op jit(solution)/shard_map/all_to_all | solution.py:49
  407.7 0.3 fusion.75
  408.0 3.6 select_reduce_fusion
  411.6 0.4 fusion.68
  412.1 0.7 fusion.44
  413.1 11.7 %all_to_all.103 = bf16[32,8,512]{2,0,1:T(8,128)(2,1)S(1)} all-to-all(bf16[32,8,512]{2,0,1:T(8,128)(2,1)S(1)} %copy.30), channel_id=1, replica_groups=mesh['group'=2,'dp'=2,'tensor'=8] {'tensor'}, dimensions={1} | all-to-all | bytes 524288 | tf_op jit(solution)/shard_map/all_to_all | solution.py:82
  424.8 7.7 %convolution_convert_fusion = bf16[256,8192]{1,0:T(8,128)(2,1)} fusion(bf16[256,512]{1,0:T(8,128)(2,1)S(1)} %bitcast.115, bf16[2,512,8192]{2,1,0:T(8,128)(2,1)} %param.12), kind=kOutput, calls=%fused_computation.4 | convolution fusion | flops 2149580800 | bytes 12845056 | tf_op jit(solution)/shard_map/dot_general | solution.py:83
  432.6 0.7 copy-done.8
  433.2 154.7 %all-reduce.5.cloned.1.call-done = bf16[256,8192]{1,0:T(8,128)(2,1)} async-done(((bf16[256,8192]{1,0:T(8,128)(2,1)}), bf16[256,8192]{1,0:T(8,128)(2,1)}) %all-reduce.5.cloned.1.call-update) | async-done | bytes 4194320 | tf_op jit(solution)/shard_map/psum | solution.py:84
  587.9 2.1 fusion.66
  (57 shorter events, 2.7 us)
Async XLA Ops:
  6.5 79.1 %all-gather.3.cloned.1.call-start = ((), (), s32[]{:S(2)}) async-start(), calls=%async_computation.6 | async-start | bytes 4718592 | tf_op jit(solution)/shard_map/all_gather | solution.py:35
  14.1 7.8 %copy-start.7 = (s32[256]{0:T(256)S(1)}, s32[256]{0:T(256)}, u32[]{:S(2)}) copy-start(s32[256]{0:T(256)} %param.14) | copy-start | bytes 3076
  22.8 10.2 %copy-start.6 = (f32[2,8192]{1,0:T(2,128)S(1)}, f32[2,8192]{1,0:T(2,128)}, u32[]{:S(2)}) copy-start(f32[2,8192]{1,0:T(2,128)} %param.9) | copy-start | bytes 196612
  85.7 3.4 copy-start.1
  92.6 12.2 %all-to-all-start.1 = ((bf16[8,32,128]{2,1,0:T(8,128)(2,1)}), bf16[8,32,128]{2,1,0:T(8,128)(2,1)S(1)}, u32[]{:S(2)}, u32[]{:S(2)}) async-start(bf16[8,32,128]{2,1,0:T(8,128)(2,1)} %bitcast.5), calls=%async_computation.1 | async-start | bytes 131072 | tf_op jit(solution)/shard_map/all_to_all | solution.py:50
  104.8 14.2 %all-to-all-start = ((bf16[8,32,512]{2,1,0:T(8,128)(2,1)}), bf16[8,32,512]{2,1,0:T(8,128)(2,1)S(1)}, u32[]{:S(2)}, u32[]{:S(2)}) async-start(bf16[8,32,512]{2,1,0:T(8,128)(2,1)} %convert_element_type.108), calls=%async_computation | async-start | bytes 524288 | tf_op jit(solution)/shard_map/all_to_all | solution.py:49
  110.7 188.7 %all-reduce.3.cloned.1.call-start = ((), (), s32[]{:S(2)}) async-start(), calls=%async_computation.7 | async-start | bytes 8388608 | tf_op jit(solution)/shard_map/psum | solution.py:84
  119.3 4.5 copy-start.4
  144.1 155.3 %copy-start.5 = (bf16[256,1024]{1,0:T(8,128)(2,1)S(1)}, bf16[256,1024]{1,0:T(8,128)(2,1)}, u32[]{:S(2)}) copy-start(bf16[256,1024]{1,0:T(8,128)(2,1)} %param.8) | copy-start | bytes 1572868
  144.2 229.9 %all-gather.5.cloned.1.call-start = ((), (), s32[]{:S(2)}) async-start(), calls=%async_computation.8 | async-start | bytes 4718592 | tf_op jit(solution)/shard_map/all_gather | solution.py:35
  374.0 3.4 copy-start.2
  381.0 12.2 %all-to-all-start.4 = ((bf16[8,32,128]{2,1,0:T(8,128)(2,1)}), bf16[8,32,128]{2,1,0:T(8,128)(2,1)S(1)}, u32[]{:S(2)}, u32[]{:S(2)}) async-start(bf16[8,32,128]{2,1,0:T(8,128)(2,1)} %bitcast.19), calls=%async_computation.4 | async-start | bytes 131072 | tf_op jit(solution)/shard_map/all_to_all | solution.py:50
  393.2 14.2 %all-to-all-start.3 = ((bf16[8,32,512]{2,1,0:T(8,128)(2,1)}), bf16[8,32,512]{2,1,0:T(8,128)(2,1)S(1)}, u32[]{:S(2)}, u32[]{:S(2)}) async-start(bf16[8,32,512]{2,1,0:T(8,128)(2,1)} %convert_element_type.122), calls=%async_computation.3 | async-start | bytes 524288 | tf_op jit(solution)/shard_map/all_to_all | solution.py:49
  399.1 188.8 %all-reduce.5.cloned.1.call-start = ((), (), s32[]{:S(2)}) async-start(), calls=%async_computation.9 | async-start | bytes 8388608 | tf_op jit(solution)/shard_map/psum | solution.py:84
  407.7 4.5 copy-start.3
  432.5 0.7 copy-start.8
  432.5 155.4 %copy-start = (bf16[256,1024]{1,0:T(8,128)(2,1)S(1)}, bf16[256,1024]{1,0:T(8,128)(2,1)}, u32[]{:S(2)}) copy-start(bf16[256,1024]{1,0:T(8,128)(2,1)} %add_convert_fusion.1) | copy-start | bytes 1572868
Sparse Core Ops, SparseCore 0:
  9.5 76.0 all-gather.2
  144.3 155.0 all-reduce.2
  301.6 72.3 all-gather.4
  432.7 155.1 all-reduce.4
where the time goes:
time: 598 us; the launch traced here: 597 us
  waiting for transfers between devices  433 us (72%)
  local copies, waits for them, and re-layouts  46.6 us (8%)
  matrix products  45.7 us (8%)
  blocking collectives  23.3 us (4%)
  starting transfers between devices  18.9 us (3%)
  other arithmetic  15.3 us (3%)
  between operations  13.5 us (2%)
    psum x2, waiting for transfers between devices, layer(): lax.psum(branch_part.astype(jnp.bfloat16), 'tensor').astype(jnp.float32)  310 us
    all_gather x2, waiting for transfers between devices, layer(): lax.all_gather(share, 'tensor', axis=1, tiled=True).astype(jnp.float32)  107 us
    all_to_all x2, blocking collectives, layer(): lax.all_to_all(attended_rows, 'tensor', split_axis=1, concat_axis=0, tile...  23.3 us
    slice x2, local copies, waits for them, and re-layouts, layer(): keys = stored_cache[:, :, :, 0]  20.4 us
    another operation x2, local copies, waits for them, and re-layouts, layer(): stored_cache = stored_cache.reshape(local_rows, slots, KVH, 2, HEAD_DIM)  15.6 us
    all_to_all x2, waiting for transfers between devices, layer(): lax.all_to_all(query_own, 'tensor', split_axis=0, concat_axis=1, tiled=True)  15.5 us
    dot_general x2, matrix products, layer(): jnp.dot(attended, w_out[level], preferred_element_type=jnp.float32)  15.4 us
    dot_general x2, matrix products, layer(): jnp.dot(scaled, query_weight, preferred_element_type=jnp.float32)  14 us
  transfers between devices with their start and end apart: 8, of which 6 were waited for; matrix products, arithmetic and copies ran while one was open for 10% of the time, Pallas kernels for 0%

commit v1 on v0

v1 whole, which is shorter than its diff:
```python
import functools

import jax
import jax.numpy as jnp
from jax import lax
from jax.experimental import pallas as pl
from jax.experimental.pallas import tpu as pltpu
from jax.sharding import PartitionSpec as P

QH = 32
KVH = 4
HEAD_DIM = 128

EPS = 1e-05
ROPE_BASE = 500000.0
NEGATIVE = -1e30
VMEM_LIMIT = 40 * 1024 * 1024


def ring_order(mesh):
    count = mesh.shape["tensor"]
    natural = list(range(count))
    if count % 2 or count < 4:
        return natural
    axis = mesh.axis_names.index("tensor")
    places = [getattr(d, "coords", None) for d in jnp_line(mesh, axis)]
    if all(place is not None for place in places):
        steps = [sum(abs(a - b) for a, b in zip(p, q)) for p, q in zip(places, places[1:])]
        if max(steps) <= 1:
            return natural
    return natural[0::2] + natural[1::2][::-1]


def jnp_line(mesh, axis):
    devices = mesh.devices
    index = [0] * devices.ndim
    index[axis] = slice(None)
    return list(devices[tuple(index)])


def params():
    return pltpu.CompilerParams(vmem_limit_bytes=VMEM_LIMIT)


def whole(*shape):
    return pl.BlockSpec(shape, lambda *_: (0,) * len(shape))


def deal_kernel(block_rows, marks_ref, spans_ref, own_ref, other_ref, first_ref, second_ref, stay_ref, leave_ref, span_ref, source_ref):
    rows = own_ref.shape[0]
    half = block_rows // 2
    part = rows // 2
    marks = marks_ref[...]
    down = lax.broadcasted_iota(jnp.int32, (rows, rows), 0)
    across = lax.broadcasted_iota(jnp.int32, (rows, rows), 1)
    same = (down // block_rows) == (across // block_rows)
    before = same & (down < across)
    marks16 = marks.astype(jnp.bfloat16)
    ranks = jnp.dot(marks16, before.astype(jnp.bfloat16), preferred_element_type=jnp.float32)
    totals = jnp.dot(marks16, same.astype(jnp.bfloat16), preferred_element_type=jnp.float32)

    def listed(which):
        count = totals[which : which + 1]
        place = jnp.where(marks[which : which + 1] > 0.5, ranks[which : which + 1], count + ranks[which + 2 : which + 3])
        low = jnp.minimum(count, float(half))
        high = jnp.maximum(count, float(half))
        return place, low, (place >= low) & (place < high)

    place, low, goes = listed(0)
    other_place, other_low, comes = listed(1)
    group = (lax.broadcasted_iota(jnp.int32, (1, rows), 1) // block_rows).astype(jnp.float32) * float(half)

    def slot(position):
        return jnp.where(position < float(half), group + position, group + position + float(part - half))

    stays_at = jnp.where(goes, -1.0, slot(place))
    comes_to = jnp.where(comes, slot(low + other_place - other_low), -1.0)
    leaves_to = jnp.where(goes, slot(other_low + place - low), -1.0)
    slots = down.astype(jnp.float32)
    stay = slots == stays_at
    come = slots == comes_to
    leave = slots == leaves_to
    stay16 = stay.astype(jnp.bfloat16)
    come16 = come.astype(jnp.bfloat16)
    moved = jnp.dot(stay16, own_ref[...], preferred_element_type=jnp.float32) + jnp.dot(
        come16, other_ref[...], preferred_element_type=jnp.float32
    )
    moved = moved.astype(jnp.bfloat16)
    first_ref[...] = moved[:part]
    second_ref[...] = moved[part:]
    stay_ref[...] = stay16
    leave_ref[...] = leave.astype(jnp.bfloat16)
    spans = spans_ref[...]
    local = (across % block_rows).astype(jnp.float32)
    span_ref[...] = jnp.sum(jnp.where(stay, spans[0:1], 0.0) + jnp.where(come, spans[1:2], 0.0), axis=1, keepdims=True)
    source_ref[...] = jnp.sum(jnp.where(stay, local, 0.0) + jnp.where(come, local + float(block_rows), 0.0), axis=1, keepdims=True)


def deal(block_rows, marks, spans, own, other):
    rows, width = own.shape
    shapes = [
        ((rows // 2, width), jnp.bfloat16),
        ((rows // 2, width), jnp.bfloat16),
        ((rows, rows), jnp.bfloat16),
        ((rows, rows), jnp.bfloat16),
        ((rows, 1), jnp.float32),
        ((rows, 1), jnp.float32),
    ]
    return pl.pallas_call(
        functools.partial(deal_kernel, block_rows),
        out_shape=[jax.ShapeDtypeStruct(*s) for s in shapes],
        compiler_params=params(),
        name="deal",
    )(marks, spans, own, other)


def restore_kernel(stay_ref, leave_ref, first_ref, second_ref, other_first_ref, other_second_ref, out_ref):
    part = first_ref.shape[0]

    def back(chosen, values):
        return lax.dot_general(chosen, values, (((0,), (0,)), ((), ())), preferred_element_type=jnp.float32)

    stay = stay_ref[...]
    leave = leave_ref[...]
    total = back(stay[:part], first_ref[...]) + back(stay[part:], second_ref[...])
    total = total + back(leave[:part], other_first_ref[...]) + back(leave[part:], other_second_ref[...])
    out_ref[...] = total.astype(jnp.bfloat16)


def restore(stay, leave, first, second, other_first, other_second):
    return pl.pallas_call(
        restore_kernel,
        out_shape=jax.ShapeDtypeStruct((stay.shape[1], first.shape[1]), jnp.bfloat16),
        compiler_params=params(),
        name="restore",
    )(stay, leave, first, second, other_first, other_second)


def project_kernel(level, count, steps, width, has_sum, finish, table_ref, *refs):
    refs = list(refs)
    blocks = [refs[4 * i : 4 * i + 4] for i in range(count)]
    refs = refs[4 * count :]
    if has_sum:
        start, refs = refs[:3], refs[3:]
    if finish:
        cosine_ref, sine_ref, out_ref, query_ref, fresh_ref, square_ref = refs
    else:
        query_ref, fresh_ref, square_ref = refs
    step = pl.program_id(0)

    @pl.when(step == 0)
    def _():
        if has_sum:
            query_ref[...] = start[0][...]
            fresh_ref[...] = start[1][...]
            square_ref[...] = start[2][...]
        else:
            query_ref[...] = jnp.zeros_like(query_ref)
            fresh_ref[...] = jnp.zeros_like(fresh_ref)
            square_ref[...] = jnp.zeros_like(square_ref)

    query = query_ref[...]
    fresh = fresh_ref[...]
    square = square_ref[...]
    for value_ref, gain_ref, query_weight_ref, fresh_weight_ref in blocks:
        values = value_ref[...].astype(jnp.float32)
        scaled = (values * gain_ref[level : level + 1, :]).astype(jnp.bfloat16)
        query = query + jnp.dot(scaled, query_weight_ref[...], preferred_element_type=jnp.float32)
        fresh = fresh + jnp.dot(scaled, fresh_weight_ref[...], preferred_element_type=jnp.float32)
        squares = values * values
        for at in range(0, squares.shape[1], HEAD_DIM):
            square = square + squares[:, at : at + HEAD_DIM]
    query_ref[...] = query
    fresh_ref[...] = fresh
    square_ref[...] = square

    if finish:

        @pl.when(step == steps - 1)
        def _():
            factor = lax.rsqrt(jnp.sum(square, axis=1, keepdims=True) / width + EPS)
            cosine = cosine_ref[...]
            sine = sine_ref[...]
            columns = query.shape[1]
            for at in range(0, columns, HEAD_DIM):
                head = query[:, at : at + HEAD_DIM] * factor
                turned = head * cosine + pltpu.roll(head, HEAD_DIM // 2, 1) * sine
                out_ref[:, at : at + HEAD_DIM] = turned.astype(jnp.bfloat16)
            out_ref[:, columns:] = (fresh * factor).astype(jnp.bfloat16)


def project(level, table, gain, query_weight, fresh_weight, blocks, sums=None, rope=None):
    rows = blocks[0][0].shape[0]
    parts = table.shape[0]
    depth = query_weight.shape[1]
    tile = depth // parts // 2
    steps = blocks[0][0].shape[1] // tile
    columns = query_weight.shape[2]
    fresh_columns = fresh_weight.shape[2]
    in_specs = []
    operands = []
    for values, place, first in blocks:
        in_specs += [
            pl.BlockSpec((rows, tile), lambda k, t: (0, k)),
            pl.BlockSpec((2, tile), lambda k, t, place=place, first=first: (0, t[place] * 2 + first + k)),
            pl.BlockSpec((None, tile, columns), lambda k, t, place=place, first=first: (level, t[place] * 2 + first + k, 0)),
            pl.BlockSpec((None, tile, fresh_columns), lambda k, t, place=place, first=first: (level, t[place] * 2 + first + k, 0)),
        ]
        operands += [values, gain, query_weight, fresh_weight]
    sum_shapes = [(rows, columns), (rows, fresh_columns), (rows, HEAD_DIM)]
    if sums is not None:
        in_specs += [whole(*s) for s in sum_shapes]
        operands += list(sums)
    finish = rope is not None
    scratch = []
    if finish:
        in_specs += [whole(rows, HEAD_DIM)] * 2
        operands += list(rope)
        out_shape = jax.ShapeDtypeStruct((rows, columns + fresh_columns), jnp.bfloat16)
        out_specs = whole(rows, columns + fresh_columns)
        scratch = [pltpu.VMEM(s, jnp.float32) for s in sum_shapes]
    else:
        out_shape = [jax.ShapeDtypeStruct(s, jnp.float32) for s in sum_shapes]
        out_specs = [whole(*s) for s in sum_shapes]
    body = functools.partial(project_kernel, level, len(blocks), steps, depth, sums is not None, finish)
    flops = 2 * rows * tile * steps * len(blocks) * (columns + fresh_columns)
    return pl.pallas_call(
        body,
        out_shape=out_shape,
        grid_spec=pltpu.PrefetchScalarGridSpec(
            num_scalar_prefetch=1, grid=(steps,), in_specs=in_specs, out_specs=out_specs, scratch_shapes=scratch
        ),
        compiler_params=params(),
        cost_estimate=pl.CostEstimate(flops=flops, bytes_accessed=flops // rows, transcendentals=0),
        name="project",
    )(table, *operands)


def attend_kernel(level, block_rows, columns, source_ref, got_ref, cosine_ref, sine_ref, span_ref, own_ref, other_ref, out_ref, held, sems):
    parts, rows, _ = got_ref.shape
    slots = held.shape[1]
    copies = []
    for row in range(rows):
        source = source_ref[row]

        @pl.when(source < block_rows)
        def _():
            pltpu.make_async_copy(own_ref.at[level, source], held.at[row], sems.at[row]).start()

        @pl.when(source >= block_rows)
        def _():
            pltpu.make_async_copy(other_ref.at[level, source - block_rows], held.at[row], sems.at[row]).start()

    heads_dev = columns // HEAD_DIM
    group = QH // KVH
    fresh = jnp.concatenate([got_ref[s, :, columns:].astype(jnp.float32) for s in range(parts)], axis=1)
    cosine = cosine_ref[...]
    sine = sine_ref[...]
    scale = HEAD_DIM ** (-0.5)
    total_rows = group * rows
    down = lax.broadcasted_iota(jnp.int32, (total_rows, rows * slots), 0)
    across = lax.broadcasted_iota(jnp.int32, (total_rows, rows * slots), 1)
    valid = ((down % rows) == (across // slots)) & ((across % slots).astype(jnp.float32) < span_ref[...])
    for row in range(rows):
        pltpu.make_async_copy(own_ref.at[level, 0], held.at[row], sems.at[row]).wait()
    for j in range(KVH):
        tiles = []
        for head in range(j * group, (j + 1) * group):
            at = head % heads_dev * HEAD_DIM
            tiles.append(got_ref[head // heads_dev, :, at : at + HEAD_DIM].astype(jnp.float32))
        query = jnp.concatenate(tiles, axis=0)
        new_key = fresh[:, j * HEAD_DIM : (j + 1) * HEAD_DIM]
        new_key = new_key * cosine + pltpu.roll(new_key, HEAD_DIM // 2, 1) * sine
        new_key = new_key.astype(jnp.bfloat16).astype(jnp.float32)
        new_value = fresh[:, (KVH + j) * HEAD_DIM : (KVH + j + 1) * HEAD_DIM]
        keys = held[:, :, 2 * j * HEAD_DIM : (2 * j + 1) * HEAD_DIM].reshape(rows * slots, HEAD_DIM)
        values = held[:, :, (2 * j + 1) * HEAD_DIM : (2 * j + 2) * HEAD_DIM].reshape(rows * slots, HEAD_DIM)
        scores = lax.dot_general(
            query.astype(jnp.bfloat16), keys, (((1,), (1,)), ((), ())), preferred_element_type=jnp.float32
        )
        scores = jnp.where(valid, scores * scale, NEGATIVE)
        own = jnp.sum(query * jnp.concatenate([new_key] * group, axis=0), axis=1, keepdims=True) * scale
        highest = jnp.maximum(jnp.max(scores, axis=1, keepdims=True), own)
        weights = jnp.where(valid, jnp.exp(scores - highest), 0.0)
        own_weight = jnp.exp(own - highest)
        total = jnp.sum(weights, axis=1, keepdims=True) + own_weight
        mixed = jnp.dot(weights.astype(jnp.bfloat16), values, preferred_element_type=jnp.float32)
        mixed = (mixed + own_weight * jnp.concatenate([new_value] * group, axis=0)) / total
        for head in range(j * group, (j + 1) * group):
            at = head % heads_dev * HEAD_DIM
            tile = mixed[(head - j * group) * rows : (head - j * group + 1) * rows]
            out_ref[head // heads_dev, :, at : at + HEAD_DIM] = tile.astype(jnp.bfloat16)


def attend(level, got, columns, rope, span, source, own, other):
    parts, rows, _ = got.shape
    _, block_rows, slots, depth = own.shape
    return pl.pallas_call(
        functools.partial(attend_kernel, level, block_rows, columns),
        out_shape=jax.ShapeDtypeStruct((parts, rows, columns), jnp.bfloat16),
        in_specs=[
            pl.BlockSpec(memory_space=pltpu.SMEM),
            pl.BlockSpec(memory_space=pltpu.VMEM),
            pl.BlockSpec(memory_space=pltpu.VMEM),
            pl.BlockSpec(memory_space=pltpu.VMEM),
            pl.BlockSpec(memory_space=pltpu.VMEM),
            pl.BlockSpec(memory_space=pl.ANY),
            pl.BlockSpec(memory_space=pl.ANY),
        ],
        out_specs=pl.BlockSpec(memory_space=pltpu.VMEM),
        scratch_shapes=[pltpu.VMEM((rows, slots, depth), jnp.bfloat16), pltpu.SemaphoreType.DMA((rows,))],
        compiler_params=params(),
        cost_estimate=pl.CostEstimate(flops=10**8, bytes_accessed=rows * slots * depth * 2, transcendentals=0),
        name="attend",
    )(source, got, rope[0], rope[1], span, own, other)


def output_kernel(table_ref, value_ref, weight_ref, *out_refs):
    product = jnp.dot(value_ref[...], weight_ref[...], preferred_element_type=jnp.float32).astype(jnp.bfloat16)
    if len(out_refs) == 1:
        out_refs[0][...] = product
    else:
        width = product.shape[1] // 2
        out_refs[0][...] = product[:, :width]
        out_refs[1][...] = product[:, width:]


def output_blocks(level, table, values, weight, first, count):
    rows, depth = values.shape
    parts = table.shape[0]
    width = weight.shape[2] // parts
    if count == 1:
        out_shape = [jax.ShapeDtypeStruct((rows, width // 2), jnp.bfloat16)] * 2
        out_specs = [whole(rows, width // 2)] * 2
    else:
        out_shape = jax.ShapeDtypeStruct((count, rows, width), jnp.bfloat16)
        out_specs = pl.BlockSpec((None, rows, width), lambda k, t: (k, 0, 0))
    flops = 2 * rows * depth * width * count
    return pl.pallas_call(
        output_kernel,
        out_shape=out_shape,
        grid_spec=pltpu.PrefetchScalarGridSpec(
            num_scalar_prefetch=1,
            grid=(count,),
            in_specs=[
                whole(rows, depth),
                pl.BlockSpec((None, depth, width), lambda k, t: (level, 0, t[(first + k) % parts])),
            ],
            out_specs=out_specs,
        ),
        compiler_params=params(),
        cost_estimate=pl.CostEstimate(flops=flops, bytes_accessed=flops // rows, transcendentals=0),
        name="output",
    )(table, values, weight)


def layer(level, ring, table, share, rope, local_rope, span, source, own, other, gain, query_weight, fresh_weight, out_weight):
    parts = len(ring)
    half = parts // 2
    width = share.shape[1]
    rows = share.shape[0]
    forward = [(ring[i], ring[(i + 1) % parts]) for i in range(parts)]
    backward = [(ring[i], ring[(i - 1) % parts]) for i in range(parts)]

    def send(value, way):
        return lax.ppermute(value, "tensor", way)

    weights = (gain, query_weight, fresh_weight)
    sums = project(level, table, *weights, [(share, 0, 0)])
    ahead = behind = share
    for step in range(1, half):
        behind = send(behind, forward)
        ahead = send(ahead, backward)
        sums = project(level, table, *weights, [(behind, parts - step, 0), (ahead, step, 0)], sums)
    behind = send(behind[:, : width // 2], forward)
    ahead = send(ahead[:, width // 2 :], backward)
    mine = project(level, table, *weights, [(behind, half, 0), (ahead, half, 1)], sums, rope)

    columns = query_weight.shape[2]
    got = lax.all_to_all(
        mine.reshape(parts, rows // parts, mine.shape[1]), "tensor", split_axis=0, concat_axis=0, tiled=True
    )
    attended = attend(level, got, columns, local_rope, span, source, own, other)
    attended = lax.all_to_all(attended, "tensor", split_axis=0, concat_axis=0, tiled=True).reshape(rows, columns)

    to_front, to_back = output_blocks(level, table, attended, out_weight, half, 1)
    products = output_blocks(level, table, attended, out_weight, half + 1, parts - 1)

    def product(place):
        return products[(place - half - 1) % parts].astype(jnp.float32)

    from_back = send(to_front, forward).astype(jnp.float32)
    from_front = send(to_back, backward).astype(jnp.float32)
    for step in range(half - 1, 0, -1):
        to_front = product(step)
        to_back = product(-step)
        if step == half - 1:
            to_front = jnp.concatenate([to_front[:, : width // 2] + from_back, to_front[:, width // 2 :]], axis=1)
            to_back = jnp.concatenate([to_back[:, : width // 2], to_back[:, width // 2 :] + from_front], axis=1)
        else:
            to_front = to_front + from_back
            to_back = to_back + from_front
        from_back = send(to_front.astype(jnp.bfloat16), forward).astype(jnp.float32)
        from_front = send(to_back.astype(jnp.bfloat16), backward).astype(jnp.float32)
    total = product(0) + (from_back + from_front)
    return (share.astype(jnp.float32) + total).astype(jnp.bfloat16)


def local(ring, hidden, norm_gain, w_query, w_kv, w_out, cache, lengths, exits):
    parts = len(ring)
    rows, width = hidden.shape
    block_rows = rows // parts
    half = block_rows // 2
    part = rows // 2
    me = lax.axis_index("tensor")
    swap = [(0, 1), (1, 0)]
    places = [ring.index(i) for i in range(parts)]
    tables = jnp.array([[ring[(places[i] + r) % parts] for r in range(parts)] for i in range(parts)], jnp.int32)
    table = lax.dynamic_index_in_dim(tables, me, 0, False)

    facts = jnp.stack([exits, lengths])
    other_facts = lax.ppermute(facts, "dp", swap)
    other_hidden = lax.ppermute(hidden, "dp", swap)
    other_cache = lax.ppermute(cache, "dp", swap)
    marks = (jnp.stack([facts[0], other_facts[0]]) == 2).astype(jnp.float32)
    marks = jnp.concatenate([marks, 1.0 - marks, jnp.zeros((4, rows), jnp.float32)], axis=0)
    spans = jnp.stack([facts[1], other_facts[1]]).astype(jnp.float32)
    first, second, stay, leave, span, source = deal(block_rows, marks, spans, hidden, other_hidden)

    turns = HEAD_DIM // 2
    freqs = ROPE_BASE ** (-jnp.arange(turns, dtype=jnp.float32) / turns)
    angle = span * freqs[None, :]
    cosine = jnp.cos(angle)
    sine = jnp.sin(angle)
    cosine = jnp.concatenate([cosine, cosine], axis=1)
    sine = jnp.concatenate([-sine, sine], axis=1)
    slots = cache.shape[2]

    def facts_of(start):
        rope = (cosine[start : start + part], sine[start : start + part])
        at = start + me * half
        local_rope = tuple(lax.dynamic_slice_in_dim(v, at, half) for v in (cosine, sine))
        local_span = lax.dynamic_slice_in_dim(span, at, half)
        local_span = jnp.broadcast_to(local_span, (half, slots)).reshape(1, half * slots)
        local_source = lax.dynamic_slice_in_dim(source, at, half).reshape(half).astype(jnp.int32)
        return rope, local_rope, local_span, local_source, cache, other_cache

    weights = (norm_gain, w_query, w_kv, w_out)
    of_first = facts_of(0)
    of_second = facts_of(part)
    first = layer(0, ring, table, first, *of_first, *weights)
    second = layer(0, ring, table, second, *of_second, *weights)
    first = layer(1, ring, table, first, *of_first, *weights)
    other_second = lax.ppermute(second, "dp", swap)
    other_first = lax.ppermute(first, "dp", swap)
    return restore(stay, leave, first, second, other_first, other_second)


def solution(mesh):
    in_specs = (
        P(("group", "dp"), "tensor"),
        P(),
        P(None, None, "tensor"),
        P(None, None, "tensor"),
        P(None, "tensor", None),
        P(None, ("group", "dp", "tensor"), None, None),
        P(("group", "dp")),
        P(("group", "dp")),
    )
    out_specs = P(("group", "dp"), "tensor")
    body = functools.partial(local, ring_order(mesh))
    return jax.shard_map(body, mesh=mesh, in_specs=in_specs, out_specs=out_specs, check_vma=False)
```

time: 598 us -> 298 us (0.50)
  waiting for transfers between devices: 433 us -> 106 us
  Pallas kernels: 0 us -> 86.6 us
  starting transfers between devices: 18.9 us -> 75.2 us
  matrix products: 45.7 us -> 0 us
  local copies, waits for them, and re-layouts: 46.6 us -> 15.4 us
  blocking collectives: 23.3 us -> 0 us
  between operations: 13.5 us -> 0.73 us
    psum x2 -> x0, waiting for transfers between devices: 310 us -> none  [layer(): lax.psum(branch_part.astype(jnp.bfloat16), 'tensor').astype(jnp.float32)]
    all_gather x2 -> x0, waiting for transfers between devices: 107 us -> none  [layer(): lax.all_gather(share, 'tensor', axis=1, tiled=True).astype(jnp.float32)]
    pallas_call x0 -> x26, Pallas kernels: none -> 86.6 us  [the longest x15 39.5 us: project(): pl.pallas_call(body, out_shape=out_shape, grid_spec=pltpu.PrefetchScalarG...]
    ppermute x0 -> x53, waiting for transfers between devices: none -> 74.9 us  [the longest x48 62.4 us: send(): return lax.ppermute(value, 'tensor', way)]
    ppermute x0 -> x53, starting transfers between devices: none -> 51.7 us  [the longest x48 50.6 us: send(): return lax.ppermute(value, 'tensor', way)]
    dot_general x12 -> x0, matrix products: 45.7 us -> none  [the longest x2 15.4 us: layer(): jnp.dot(attended, w_out[level], preferred_element_type=jnp.float32)]
    slice x4 -> x13, local copies, waits for them, and re-layouts: 26.7 us -> 0.12 us  [the longest x3 0.03 us: layer(): to_front[:, width // 2:]]
    all_to_all x2 -> x0, blocking collectives: 23.3 us -> none  [layer(): lax.all_to_all(attended_rows, 'tensor', split_axis=1, concat_axis=0, tile...]
  transfers between devices with their start and end apart: 8 -> 59, of which waited for: 6 -> 25; matrix products, arithmetic and copies ran while one was open for 10% -> 4% of each run, Pallas kernels for 0% -> 27%
where the time goes in v1:
time: 298 us; the launch traced here: 295 us
  waiting for transfers between devices  106 us (36%)
  Pallas kernels  86.6 us (29%)
  starting transfers between devices  75.2 us (25%)
  local copies, waits for them, and re-layouts  15.4 us (5%)
  other arithmetic  11.3 us (4%)
    ppermute x48, waiting for transfers between devices, send(): return lax.ppermute(value, 'tensor', way)  62.4 us
    ppermute x48, starting transfers between devices, send(): return lax.ppermute(value, 'tensor', way)  50.6 us
    pallas_call x15, Pallas kernels, project(): pl.pallas_call(body, out_shape=out_shape, grid_spec=pltpu.PrefetchScalarG...  39.5 us
    pallas_call x6, Pallas kernels, output_blocks(): pl.pallas_call(output_kernel, out_shape=out_shape, grid_spec=pltpu.Prefet...  27.7 us
    pallas_call x3, Pallas kernels, attend(): pl.pallas_call(functools.partial(attend_kernel, level, block_rows, column...  17.2 us
    all_to_all x3, waiting for transfers between devices, layer(): lax.all_to_all(mine.reshape(parts, rows // parts, mine.shape[1]), 'tensor...  16.1 us
    all_to_all x3, waiting for transfers between devices, layer(): lax.all_to_all(attended, 'tensor', split_axis=0, concat_axis=0, tiled=True)  15 us
    unnamed x26, local copies, waits for them, and re-layouts  14 us
  transfers between devices with their start and end apart: 59, of which 25 were waited for; matrix products, arithmetic and copies ran while one was open for 4% of the time, Pallas kernels for 27%

profile of v1, /device:TPU:0, one launch (start us, length us, event | category | flops | bytes accessed | tf_op | source)
XLA Modules:
  0.0 295.2 jit_solution(14552145853432410735)
XLA Ops:
  1.7 11.0 %collective-permute-done = s32[2,256]{1,0:T(2,128)S(1)} collective-permute-done((s32[2,256]{1,0:T(2,128)S(1)}, s32[2,256]{1,0:T(2,128)S(1)}, u32[]{:S(2)}, u32[]{:S(2)}) %collective-permute-start) | collective-permute-done | bytes 2080 | tf_op jit(solution)/shard_map/ppermute | solution.py:422
  17.2 3.1 %collective-permute-start.2 = (bf16[128,1024]{1,0:T(8,128)(2,1)S(1)}, bf16[128,1024]{1,0:T(8,128)(2,1)S(1)}, u32[]{:S(2)}, u32[]{:S(2)}) collective-permute-start(bf16[128,1024]{1,0:T(8,128)(2,1)S(1)} %get-tuple-element.55.refs_0_), channel_id=1, source_target_pairs={{0,2},{2,4},{4,6},{6,7},{7,5},{5,3},{3,1},{1,0},{8,10},{10,12},{12... | collective-permute-start | bytes 786440 | tf_op jit(solution)/shard_map/ppermute | solution.py:366
  20.3 6.8 %collective-permute-done.2.refs_0_ = bf16[128,1024]{1,0:T(8,128)(2,1)S(1)} collective-permute-done((bf16[128,1024]{1,0:T(8,128)(2,1)S(1)}, bf16[128,1024]{1,0:T(8,128)(2,1)S(1)}, u32[]{:S(2)}, u32[]{:S(2)}) %collective-permute-start.2) | collective-permute-done | bytes 262176 | tf_op jit(solution)/shard_map/ppermute | solution.py:366
  29.1 6.0 %collective-permute-done.3.refs_0_ = bf16[128,1024]{1,0:T(8,128)(2,1)S(1)} collective-permute-done((bf16[128,1024]{1,0:T(8,128)(2,1)S(1)}, bf16[128,1024]{1,0:T(8,128)(2,1)S(1)}, u32[]{:S(2)}, u32[]{:S(2)}) %collective-permute-start.3) | collective-permute-done | bytes 262176 | tf_op jit(solution)/shard_map/ppermute | solution.py:366
  38.5 3.7 %collective-permute-done.4.refs_0_ = bf16[128,1024]{1,0:T(8,128)(2,1)S(1)} collective-permute-done((bf16[128,1024]{1,0:T(8,128)(2,1)S(1)}, bf16[128,1024]{1,0:T(8,128)(2,1)S(1)}, u32[]{:S(2)}, u32[]{:S(2)}) %collective-permute-start.4) | collective-permute-done | bytes 262176 | tf_op jit(solution)/shard_map/ppermute | solution.py:366
  46.7 2.5 project.15
  49.2 2.6 project.16
  51.9 2.6 project.17
  54.5 2.6 project.18
  57.2 2.9 project.19
  60.1 5.5 %all-to-all-start = ((bf16[8,16,640]{2,1,0:T(8,128)(2,1)}), bf16[8,16,640]{2,1,0:T(8,128)(2,1)S(1)}, u32[]{:S(2)}, u32[]{:S(2)}) async-start(bf16[8,16,640]{2,1,0:T(8,128)(2,1)} %bitcast.3), calls=%async_computation | async-start | bytes 327680 | tf_op jit(solution)/shard_map/all_to_all | solution.py:380
  66.1 7.1 %all-to-all-done.got_ref = bf16[8,16,640]{2,1,0:T(8,128)(2,1)S(1)} async-done(((bf16[8,16,640]{2,1,0:T(8,128)(2,1)}), bf16[8,16,640]{2,1,0:T(8,128)(2,1)S(1)}, u32[]{:S(2)}, u32[]{:S(2)}) %all-to-all-start) | async-done | bytes 163872 | tf_op jit(solution)/shard_map/all_to_all | solution.py:380
  73.2 3.4 %copy-done.4 = bf16[2,32,64,1024]{3,2,1,0:T(8,128)(2,1)S(1)} copy-done((bf16[2,32,64,1024]{3,2,1,0:T(8,128)(2,1)S(1)}, bf16[2,32,64,1024]{3,2,1,0:T(8,128)(2,1)}, u32[]{:S(2)}) %copy-start.4) | copy-done | bytes 8388632
  76.6 5.8 %attend.3 = bf16[8,16,512]{2,1,0:T(8,128)(2,1)} custom-call(s32[16]{0:T(128)S(1)} %get-tuple-element.104.source_ref, bf16[8,16,640]{2,1,0:T(8,128)(2,1)S(1)} %all-to-all-done.got_ref, f32[16,128]{1,0:T(8,128)S(1)} %get-tuple-element.130.cosine_ref, f32[16,128]{1,0:T(8,128)S(1)} %get-tuple-element.118.sine_ref, f32[1,1024]{1,0:T(1,128)S(1)} %reshape.77.span_ref, ...), custom_call_target="tpu_custom_call" | custom-call | flops 100000000 | bytes 2097152 | tf_op jit(solution)/shard_map/attend/pallas_call | solution.py:298
  82.3 3.4 %all-to-all-start.1 = ((bf16[8,16,512]{2,1,0:T(8,128)(2,1)}), bf16[8,16,512]{2,1,0:T(8,128)(2,1)S(1)}, u32[]{:S(2)}, u32[]{:S(2)}) async-start(bf16[8,16,512]{2,1,0:T(8,128)(2,1)} %attend.3), calls=%async_computation.1 | async-start | bytes 262144 | tf_op jit(solution)/shard_map/all_to_all | solution.py:384
  87.8 5.2 %all-to-all-done.1 = bf16[8,16,512]{2,1,0:T(8,128)(2,1)S(1)} async-done(((bf16[8,16,512]{2,1,0:T(8,128)(2,1)}), bf16[8,16,512]{2,1,0:T(8,128)(2,1)S(1)}, u32[]{:S(2)}, u32[]{:S(2)}) %all-to-all-start.1) | async-done | bytes 131104 | tf_op jit(solution)/shard_map/all_to_all | solution.py:384
  93.0 6.8 %output.6 = bf16[7,128,1024]{2,1,0:T(8,128)(2,1)S(1)} custom-call(s32[8]{0:T(128)S(1)} %fusion.27.table_ref, bf16[128,512]{1,0:T(8,128)(2,1)S(1)} %bitcast.101, bf16[2,512,8192]{2,1,0:T(8,128)(2,1)} %weight_ref.11), custom_call_target="tpu_custom_call" | custom-call | flops 939524096 | bytes 7340032 | tf_op jit(solution)/shard_map/output/pallas_call | solution.py:339
  104.2 3.7 %collective-permute-done.11 = bf16[128,512]{1,0:T(8,128)(2,1)S(1)} collective-permute-done((bf16[128,512]{1,0:T(8,128)(2,1)S(1)}, bf16[128,512]{1,0:T(8,128)(2,1)S(1)}, u32[]{:S(2)}, u32[]{:S(2)}) %collective-permute-start.11) | collective-permute-done | bytes 131104 | tf_op jit(solution)/shard_map/ppermute | solution.py:366
  110.2 7.1 %collective-permute-done.12 = bf16[128,1024]{1,0:T(8,128)(2,1)S(1)} collective-permute-done((bf16[128,1024]{1,0:T(8,128)(2,1)S(1)}, bf16[128,1024]{1,0:T(8,128)(2,1)S(1)}, u32[]{:S(2)}, u32[]{:S(2)}) %collective-permute-start.12) | collective-permute-done | bytes 262176 | tf_op jit(solution)/shard_map/ppermute | solution.py:366
  119.6 6.8 %collective-permute-done.13 = bf16[128,1024]{1,0:T(8,128)(2,1)S(1)} collective-permute-done((bf16[128,1024]{1,0:T(8,128)(2,1)S(1)}, bf16[128,1024]{1,0:T(8,128)(2,1)S(1)}, u32[]{:S(2)}, u32[]{:S(2)}) %collective-permute-start.13) | collective-permute-done | bytes 262176 | tf_op jit(solution)/shard_map/ppermute | solution.py:366
  127.7 4.4 %collective-permute-done.36.refs_0_ = bf16[128,1024]{1,0:T(8,128)(2,1)S(1)} collective-permute-done((bf16[128,1024]{1,0:T(8,128)(2,1)S(1)}, bf16[128,1024]{1,0:T(8,128)(2,1)S(1)}, u32[]{:S(2)}, u32[]{:S(2)}) %collective-permute-start.36) | collective-permute-done | bytes 262176 | tf_op jit(solution)/shard_map/ppermute | solution.py:366
  142.9 2.7 project.26
  145.6 2.6 project.27
  148.2 2.6 project.28
  150.9 2.9 project.29
  153.8 3.4 %all-to-all-start.4 = ((bf16[8,16,640]{2,1,0:T(8,128)(2,1)}), bf16[8,16,640]{2,1,0:T(8,128)(2,1)S(1)}, u32[]{:S(2)}, u32[]{:S(2)}) async-start(bf16[8,16,640]{2,1,0:T(8,128)(2,1)} %bitcast.21), calls=%async_computation.4 | async-start | bytes 327680 | tf_op jit(solution)/shard_map/all_to_all | solution.py:380
  160.5 4.3 %all-to-all-done.4.got_ref = bf16[8,16,640]{2,1,0:T(8,128)(2,1)S(1)} async-done(((bf16[8,16,640]{2,1,0:T(8,128)(2,1)}), bf16[8,16,640]{2,1,0:T(8,128)(2,1)S(1)}, u32[]{:S(2)}, u32[]{:S(2)}) %all-to-all-start.4) | async-done | bytes 163872 | tf_op jit(solution)/shard_map/all_to_all | solution.py:380
  164.8 3.4 %copy-done.5 = bf16[2,32,64,1024]{3,2,1,0:T(8,128)(2,1)S(1)} copy-done((bf16[2,32,64,1024]{3,2,1,0:T(8,128)(2,1)S(1)}, bf16[2,32,64,1024]{3,2,1,0:T(8,128)(2,1)}, u32[]{:S(2)}) %copy-start.5) | copy-done | bytes 8388632
  168.1 5.6 %attend.5 = bf16[8,16,512]{2,1,0:T(8,128)(2,1)} custom-call(s32[16]{0:T(128)S(1)} %get-tuple-element.103.source_ref, bf16[8,16,640]{2,1,0:T(8,128)(2,1)S(1)} %all-to-all-done.4.got_ref, f32[16,128]{1,0:T(8,128)S(1)} %get-tuple-element.131.cosine_ref, f32[16,128]{1,0:T(8,128)S(1)} %get-tuple-element.117.sine_ref, f32[1,1024]{1,0:T(1,128)S(1)} %reshape.82.span_ref, ...), custom_call_target="tpu_custom_call" | custom-call | flops 100000000 | bytes 2097152 | tf_op jit(solution)/shard_map/attend/pallas_call | solution.py:298
  173.8 3.4 %all-to-all-start.5 = ((bf16[8,16,512]{2,1,0:T(8,128)(2,1)}), bf16[8,16,512]{2,1,0:T(8,128)(2,1)S(1)}, u32[]{:S(2)}, u32[]{:S(2)}) async-start(bf16[8,16,512]{2,1,0:T(8,128)(2,1)} %attend.5), calls=%async_computation.5 | async-start | bytes 262144 | tf_op jit(solution)/shard_map/all_to_all | solution.py:384
  179.3 5.4 %all-to-all-done.5 = bf16[8,16,512]{2,1,0:T(8,128)(2,1)S(1)} async-done(((bf16[8,16,512]{2,1,0:T(8,128)(2,1)}), bf16[8,16,512]{2,1,0:T(8,128)(2,1)S(1)}, u32[]{:S(2)}, u32[]{:S(2)}) %all-to-all-start.5) | async-done | bytes 131104 | tf_op jit(solution)/shard_map/all_to_all | solution.py:384
  184.7 2.7 output.11
  187.4 7.1 %output.10 = bf16[7,128,1024]{2,1,0:T(8,128)(2,1)S(1)} custom-call(s32[8]{0:T(128)S(1)} %fusion.27.table_ref, bf16[128,512]{1,0:T(8,128)(2,1)S(1)} %bitcast.98, bf16[2,512,8192]{2,1,0:T(8,128)(2,1)} %weight_ref.11), custom_call_target="tpu_custom_call" | custom-call | flops 939524096 | bytes 7340032 | tf_op jit(solution)/shard_map/output/pallas_call | solution.py:339
  207.0 2.7 project.21
  209.8 2.7 project.22
  212.5 2.6 project.23
  215.2 2.9 project.24
  218.0 4.4 %all-to-all-start.2 = ((bf16[8,16,640]{2,1,0:T(8,128)(2,1)}), bf16[8,16,640]{2,1,0:T(8,128)(2,1)S(1)}, u32[]{:S(2)}, u32[]{:S(2)}) async-start(bf16[8,16,640]{2,1,0:T(8,128)(2,1)} %bitcast.12), calls=%async_computation.2 | async-start | bytes 327680 | tf_op jit(solution)/shard_map/all_to_all | solution.py:380
  225.2 4.8 %all-to-all-done.2.got_ref = bf16[8,16,640]{2,1,0:T(8,128)(2,1)S(1)} async-done(((bf16[8,16,640]{2,1,0:T(8,128)(2,1)}), bf16[8,16,640]{2,1,0:T(8,128)(2,1)S(1)}, u32[]{:S(2)}, u32[]{:S(2)}) %all-to-all-start.2) | async-done | bytes 163872 | tf_op jit(solution)/shard_map/all_to_all | solution.py:380
  230.0 3.4 %copy-done.6 = bf16[2,32,64,1024]{3,2,1,0:T(8,128)(2,1)S(1)} copy-done((bf16[2,32,64,1024]{3,2,1,0:T(8,128)(2,1)S(1)}, bf16[2,32,64,1024]{3,2,1,0:T(8,128)(2,1)}, u32[]{:S(2)}) %copy-start.6) | copy-done | bytes 8388632
  233.3 5.8 %attend.4 = bf16[8,16,512]{2,1,0:T(8,128)(2,1)} custom-call(s32[16]{0:T(128)S(1)} %get-tuple-element.104.source_ref, bf16[8,16,640]{2,1,0:T(8,128)(2,1)S(1)} %all-to-all-done.2.got_ref, f32[16,128]{1,0:T(8,128)S(1)} %get-tuple-element.130.cosine_ref, f32[16,128]{1,0:T(8,128)S(1)} %get-tuple-element.118.sine_ref, f32[1,1024]{1,0:T(1,128)S(1)} %reshape.77.span_ref, ...), custom_call_target="tpu_custom_call" | custom-call | flops 100000000 | bytes 2097152 | tf_op jit(solution)/shard_map/attend/pallas_call | solution.py:298
  239.1 3.4 %all-to-all-start.3 = ((bf16[8,16,512]{2,1,0:T(8,128)(2,1)}), bf16[8,16,512]{2,1,0:T(8,128)(2,1)S(1)}, u32[]{:S(2)}, u32[]{:S(2)}) async-start(bf16[8,16,512]{2,1,0:T(8,128)(2,1)} %attend.4), calls=%async_computation.3 | async-start | bytes 262144 | tf_op jit(solution)/shard_map/all_to_all | solution.py:384
  245.5 4.4 %all-to-all-done.3 = bf16[8,16,512]{2,1,0:T(8,128)(2,1)S(1)} async-done(((bf16[8,16,512]{2,1,0:T(8,128)(2,1)}), bf16[8,16,512]{2,1,0:T(8,128)(2,1)S(1)}, u32[]{:S(2)}, u32[]{:S(2)}) %all-to-all-start.3) | async-done | bytes 131104 | tf_op jit(solution)/shard_map/all_to_all | solution.py:384
  249.9 6.8 %output.8 = bf16[7,128,1024]{2,1,0:T(8,128)(2,1)S(1)} custom-call(s32[8]{0:T(128)S(1)} %fusion.27.table_ref, bf16[128,512]{1,0:T(8,128)(2,1)S(1)} %bitcast.99, bf16[2,512,8192]{2,1,0:T(8,128)(2,1)} %weight_ref.11), custom_call_target="tpu_custom_call" | custom-call | flops 939524096 | bytes 7340032 | tf_op jit(solution)/shard_map/output/pallas_call | solution.py:339
  261.0 3.8 %collective-permute-done.27 = bf16[128,512]{1,0:T(8,128)(2,1)S(1)} collective-permute-done((bf16[128,512]{1,0:T(8,128)(2,1)S(1)}, bf16[128,512]{1,0:T(8,128)(2,1)S(1)}, u32[]{:S(2)}, u32[]{:S(2)}) %collective-permute-start.27) | collective-permute-done | bytes 131104 | tf_op jit(solution)/shard_map/ppermute | solution.py:366
  267.6 4.7 %collective-permute-done.28 = bf16[128,1024]{1,0:T(8,128)(2,1)S(1)} collective-permute-done((bf16[128,1024]{1,0:T(8,128)(2,1)S(1)}, bf16[128,1024]{1,0:T(8,128)(2,1)S(1)}, u32[]{:S(2)}, u32[]{:S(2)}) %collective-permute-start.28) | collective-permute-done | bytes 262176 | tf_op jit(solution)/shard_map/ppermute | solution.py:366
  275.6 3.2 %collective-permute-done.29 = bf16[128,1024]{1,0:T(8,128)(2,1)S(1)} collective-permute-done((bf16[128,1024]{1,0:T(8,128)(2,1)S(1)}, bf16[128,1024]{1,0:T(8,128)(2,1)S(1)}, u32[]{:S(2)}, u32[]{:S(2)}) %collective-permute-start.29) | collective-permute-done | bytes 262176 | tf_op jit(solution)/shard_map/ppermute | solution.py:366
  288.7 3.2 %collective-permute-done.34 = bf16[128,1024]{1,0:T(8,128)(2,1)S(1)} collective-permute-done((bf16[128,1024]{1,0:T(8,128)(2,1)S(1)}, bf16[128,1024]{1,0:T(8,128)(2,1)S(1)}, u32[]{:S(2)}, u32[]{:S(2)}) %collective-permute-start.34) | collective-permute-done | bytes 262176 | tf_op jit(solution)/shard_map/ppermute | solution.py:366
  (181 shorter events, 86.5 us)
Async XLA Ops:
  0.0 73.2 %collective-permute-start.10 = (bf16[2,32,64,1024]{3,2,1,0:T(8,128)(2,1)}, bf16[2,32,64,1024]{3,2,1,0:T(8,128)(2,1)}, u32[]{:S(2)}, u32[]{:S(2)}) collective-permute-start(bf16[2,32,64,1024]{3,2,1,0:T(8,128)(2,1)} %own_ref.7), channel_id=1, source_target_pairs={{0,8},{8,0},{1,9},{9,1},{2,10},{10,2},{3,11},{11,3},{4,12},{12,4},... | collective-permute-start | bytes 25165832 | tf_op jit(solution)/shard_map/ppermute | solution.py:424
  1.2 11.6 %collective-permute-start = (s32[2,256]{1,0:T(2,128)S(1)}, s32[2,256]{1,0:T(2,128)S(1)}, u32[]{:S(2)}, u32[]{:S(2)}) collective-permute-start(s32[2,256]{1,0:T(2,128)S(1)} %pad_add_fusion), channel_id=1, source_target_pairs={{0,8},{8,0},{1,9},{9,1},{2,10},{10,2},{3,11},{11,3},{4,12},{12,4},... | collective-permute-start | bytes 6152 | tf_op jit(solution)/shard_map/ppermute | solution.py:422
  1.2 13.7 %collective-permute-start.1 = (bf16[256,1024]{1,0:T(8,128)(2,1)}, bf16[256,1024]{1,0:T(8,128)(2,1)S(1)}, u32[]{:S(2)}, u32[]{:S(2)}) collective-permute-start(bf16[256,1024]{1,0:T(8,128)(2,1)} %own_ref.4), channel_id=1, source_target_pairs={{0,8},{8,0},{1,9},{9,1},{2,10},{10,2},{3,11},{11,3},{4,12},{12,4},... | collective-permute-start | bytes 1572872 | tf_op jit(solution)/shard_map/ppermute | solution.py:423
  17.2 9.9 %collective-permute-start.2 = (bf16[128,1024]{1,0:T(8,128)(2,1)S(1)}, bf16[128,1024]{1,0:T(8,128)(2,1)S(1)}, u32[]{:S(2)}, u32[]{:S(2)}) collective-permute-start(bf16[128,1024]{1,0:T(8,128)(2,1)S(1)} %get-tuple-element.55.refs_0_), channel_id=1, source_target_pairs={{0,2},{2,4},{4,6},{6,7},{7,5},{5,3},{3,1},{1,0},{8,10},{10,12},{12... | collective-permute-start | bytes 786440 | tf_op jit(solution)/shard_map/ppermute | solution.py:366
  20.3 8.6 %collective-permute-start.6 = (bf16[128,1024]{1,0:T(8,128)(2,1)S(1)}, bf16[128,1024]{1,0:T(8,128)(2,1)S(1)}, u32[]{:S(2)}, u32[]{:S(2)}) collective-permute-start(bf16[128,1024]{1,0:T(8,128)(2,1)S(1)} %get-tuple-element.55.refs_0_), channel_id=1, source_target_pairs={{0,1},{2,0},{4,2},{6,4},{7,6},{5,7},{3,5},{1,3},{8,9},{10,8},{12,1... | collective-permute-start | bytes 786440 | tf_op jit(solution)/shard_map/ppermute | solution.py:366
  27.1 8.0 %collective-permute-start.3 = (bf16[128,1024]{1,0:T(8,128)(2,1)S(1)}, bf16[128,1024]{1,0:T(8,128)(2,1)S(1)}, u32[]{:S(2)}, u32[]{:S(2)}) collective-permute-start(bf16[128,1024]{1,0:T(8,128)(2,1)S(1)} %collective-permute-done.2.refs_0_), channel_id=1, source_target_pairs={{0,2},{2,4},{4,6},{6,7},{7,5},{5,3},{3,1},{1,0},{8,10},{10,12},{12... | collective-permute-start | bytes 786440 | tf_op jit(solution)/shard_map/ppermute | solution.py:366
  28.9 7.8 %collective-permute-start.7 = (bf16[128,1024]{1,0:T(8,128)(2,1)S(1)}, bf16[128,1024]{1,0:T(8,128)(2,1)S(1)}, u32[]{:S(2)}, u32[]{:S(2)}) collective-permute-start(bf16[128,1024]{1,0:T(8,128)(2,1)S(1)} %collective-permute-done.6.refs_4_), channel_id=1, source_target_pairs={{0,1},{2,0},{4,2},{6,4},{7,6},{5,7},{3,5},{1,3},{8,9},{10,8},{12,1... | collective-permute-start | bytes 786440 | tf_op jit(solution)/shard_map/ppermute | solution.py:366
  35.1 7.1 %collective-permute-start.4 = (bf16[128,1024]{1,0:T(8,128)(2,1)S(1)}, bf16[128,1024]{1,0:T(8,128)(2,1)S(1)}, u32[]{:S(2)}, u32[]{:S(2)}) collective-permute-start(bf16[128,1024]{1,0:T(8,128)(2,1)S(1)} %collective-permute-done.3.refs_0_), channel_id=1, source_target_pairs={{0,2},{2,4},{4,6},{6,7},{7,5},{5,3},{3,1},{1,0},{8,10},{10,12},{12... | collective-permute-start | bytes 786440 | tf_op jit(solution)/shard_map/ppermute | solution.py:366
  36.7 6.9 %collective-permute-start.8 = (bf16[128,1024]{1,0:T(8,128)(2,1)S(1)}, bf16[128,1024]{1,0:T(8,128)(2,1)S(1)}, u32[]{:S(2)}, u32[]{:S(2)}) collective-permute-start(bf16[128,1024]{1,0:T(8,128)(2,1)S(1)} %collective-permute-done.7.refs_4_), channel_id=1, source_target_pairs={{0,1},{2,0},{4,2},{6,4},{7,6},{5,7},{3,5},{1,3},{8,9},{10,8},{12,1... | collective-permute-start | bytes 786440 | tf_op jit(solution)/shard_map/ppermute | solution.py:366
  42.2 14.9 %collective-permute-start.5 = (bf16[128,512]{1,0:T(8,128)(2,1)S(1)}, bf16[128,512]{1,0:T(8,128)(2,1)S(1)}, u32[]{:S(2)}, u32[]{:S(2)}) collective-permute-start(bf16[128,512]{1,0:T(8,128)(2,1)S(1)} %slice.212), channel_id=1, source_target_pairs={{0,2},{2,4},{4,6},{6,7},{7,5},{5,3},{3,1},{1,0},{8,10},{10,12},{12... | collective-permute-start | bytes 393224 | tf_op jit(solution)/shard_map/ppermute | solution.py:366
  43.6 13.6 %collective-permute-start.9 = (bf16[128,512]{1,0:T(8,128)(2,1)S(1)}, bf16[128,512]{1,0:T(8,128)(2,1)S(1)}, u32[]{:S(2)}, u32[]{:S(2)}) collective-permute-start(bf16[128,512]{1,0:T(8,128)(2,1)S(1)} %slice.213), channel_id=1, source_target_pairs={{0,1},{2,0},{4,2},{6,4},{7,6},{5,7},{3,5},{1,3},{8,9},{10,8},{12,1... | collective-permute-start | bytes 393224 | tf_op jit(solution)/shard_map/ppermute | solution.py:366
  60.1 13.1 %all-to-all-start = ((bf16[8,16,640]{2,1,0:T(8,128)(2,1)}), bf16[8,16,640]{2,1,0:T(8,128)(2,1)S(1)}, u32[]{:S(2)}, u32[]{:S(2)}) async-start(bf16[8,16,640]{2,1,0:T(8,128)(2,1)} %bitcast.3), calls=%async_computation | async-start | bytes 327680 | tf_op jit(solution)/shard_map/all_to_all | solution.py:380
  82.3 10.7 %all-to-all-start.1 = ((bf16[8,16,512]{2,1,0:T(8,128)(2,1)}), bf16[8,16,512]{2,1,0:T(8,128)(2,1)S(1)}, u32[]{:S(2)}, u32[]{:S(2)}) async-start(bf16[8,16,512]{2,1,0:T(8,128)(2,1)} %attend.3), calls=%async_computation.1 | async-start | bytes 262144 | tf_op jit(solution)/shard_map/all_to_all | solution.py:384
  85.7 31.9 %collective-permute-start.35 = (bf16[128,1024]{1,0:T(8,128)(2,1)S(1)}, bf16[128,1024]{1,0:T(8,128)(2,1)S(1)}, u32[]{:S(2)}, u32[]{:S(2)}) collective-permute-start(bf16[128,1024]{1,0:T(8,128)(2,1)S(1)} %get-tuple-element.86.refs_0_), channel_id=1, source_target_pairs={{0,2},{2,4},{4,6},{6,7},{7,5},{5,3},{3,1},{1,0},{8,10},{10,12},{12... | collective-permute-start | bytes 786440 | tf_op jit(solution)/shard_map/ppermute | solution.py:366
  87.7 30.6 %collective-permute-start.39 = (bf16[128,1024]{1,0:T(8,128)(2,1)S(1)}, bf16[128,1024]{1,0:T(8,128)(2,1)}, u32[]{:S(2)}, u32[]{:S(2)}) collective-permute-start(bf16[128,1024]{1,0:T(8,128)(2,1)S(1)} %get-tuple-element.86.refs_0_), channel_id=1, source_target_pairs={{0,1},{2,0},{4,2},{6,4},{7,6},{5,7},{3,5},{1,3},{8,9},{10,8},{12,1... | collective-permute-start | bytes 786440 | tf_op jit(solution)/shard_map/ppermute | solution.py:366
  107.9 9.3 %collective-permute-start.12 = (bf16[128,1024]{1,0:T(8,128)(2,1)S(1)}, bf16[128,1024]{1,0:T(8,128)(2,1)S(1)}, u32[]{:S(2)}, u32[]{:S(2)}) collective-permute-start(bf16[128,1024]{1,0:T(8,128)(2,1)S(1)} %pad_maximum_fusion), channel_id=1, source_target_pairs={{0,2},{2,4},{4,6},{6,7},{7,5},{5,3},{3,1},{1,0},{8,10},{10,12},{12... | collective-permute-start | bytes 786440 | tf_op jit(solution)/shard_map/ppermute | solution.py:366
  108.4 11.3 %collective-permute-start.16 = (bf16[128,1024]{1,0:T(8,128)(2,1)S(1)}, bf16[128,1024]{1,0:T(8,128)(2,1)S(1)}, u32[]{:S(2)}, u32[]{:S(2)}) collective-permute-start(bf16[128,1024]{1,0:T(8,128)(2,1)S(1)} %pad_maximum_fusion.1), channel_id=1, source_target_pairs={{0,1},{2,0},{4,2},{6,4},{7,6},{5,7},{3,5},{1,3},{8,9},{10,8},{12,1... | collective-permute-start | bytes 786440 | tf_op jit(solution)/shard_map/ppermute | solution.py:366
  117.3 9.2 %collective-permute-start.13 = (bf16[128,1024]{1,0:T(8,128)(2,1)S(1)}, bf16[128,1024]{1,0:T(8,128)(2,1)S(1)}, u32[]{:S(2)}, u32[]{:S(2)}) collective-permute-start(bf16[128,1024]{1,0:T(8,128)(2,1)S(1)} %fusion.14), channel_id=1, source_target_pairs={{0,2},{2,4},{4,6},{6,7},{7,5},{5,3},{3,1},{1,0},{8,10},{10,12},{12... | collective-permute-start | bytes 786440 | tf_op jit(solution)/shard_map/ppermute | solution.py:366
  117.6 14.5 %collective-permute-start.36 = (bf16[128,1024]{1,0:T(8,128)(2,1)S(1)}, bf16[128,1024]{1,0:T(8,128)(2,1)S(1)}, u32[]{:S(2)}, u32[]{:S(2)}) collective-permute-start(bf16[128,1024]{1,0:T(8,128)(2,1)S(1)} %collective-permute-done.35.refs_0_), channel_id=1, source_target_pairs={{0,2},{2,4},{4,6},{6,7},{7,5},{5,3},{3,1},{1,0},{8,10},{10,12},{12... | collective-permute-start | bytes 786440 | tf_op jit(solution)/shard_map/ppermute | solution.py:366
  118.3 13.8 %collective-permute-start.40 = (bf16[128,1024]{1,0:T(8,128)(2,1)}, bf16[128,1024]{1,0:T(8,128)(2,1)S(1)}, u32[]{:S(2)}, u32[]{:S(2)}) collective-permute-start(bf16[128,1024]{1,0:T(8,128)(2,1)} %collective-permute-done.39.refs_4_), channel_id=1, source_target_pairs={{0,1},{2,0},{4,2},{6,4},{7,6},{5,7},{3,5},{1,3},{8,9},{10,8},{12,1... | collective-permute-start | bytes 786440 | tf_op jit(solution)/shard_map/ppermute | solution.py:366
  127.4 6.8 %collective-permute-start.17 = (bf16[128,1024]{1,0:T(8,128)(2,1)S(1)}, bf16[128,1024]{1,0:T(8,128)(2,1)S(1)}, u32[]{:S(2)}, u32[]{:S(2)}) collective-permute-start(bf16[128,1024]{1,0:T(8,128)(2,1)S(1)} %get-tuple-element.114), channel_id=1, source_target_pairs={{0,1},{2,0},{4,2},{6,4},{7,6},{5,7},{3,5},{1,3},{8,9},{10,8},{12,1... | collective-permute-start | bytes 786440 | tf_op jit(solution)/shard_map/ppermute | solution.py:366
  134.1 23.0 %collective-permute-start.14 = (bf16[128,1024]{1,0:T(8,128)(2,1)}, bf16[128,1024]{1,0:T(8,128)(2,1)S(1)}, u32[]{:S(2)}, u32[]{:S(2)}) collective-permute-start(bf16[128,1024]{1,0:T(8,128)(2,1)} %get-tuple-element.113), channel_id=1, source_target_pairs={{0,2},{2,4},{4,6},{6,7},{7,5},{5,3},{3,1},{1,0},{8,10},{10,12},{12... | collective-permute-start | bytes 786440 | tf_op jit(solution)/shard_map/ppermute | solution.py:366
  134.9 22.2 %collective-permute-start.18 = (bf16[128,1024]{1,0:T(8,128)(2,1)}, bf16[128,1024]{1,0:T(8,128)(2,1)}, u32[]{:S(2)}, u32[]{:S(2)}) collective-permute-start(bf16[128,1024]{1,0:T(8,128)(2,1)} %fusion.13), channel_id=1, source_target_pairs={{0,1},{2,0},{4,2},{6,4},{7,6},{5,7},{3,5},{1,3},{8,9},{10,8},{12,1... | collective-permute-start | bytes 786440 | tf_op jit(solution)/shard_map/ppermute | solution.py:366
  138.5 12.4 %collective-permute-start.38 = (bf16[128,512]{1,0:T(8,128)(2,1)S(1)}, bf16[128,512]{1,0:T(8,128)(2,1)S(1)}, u32[]{:S(2)}, u32[]{:S(2)}) collective-permute-start(bf16[128,512]{1,0:T(8,128)(2,1)S(1)} %slice.242), channel_id=1, source_target_pairs={{0,2},{2,4},{4,6},{6,7},{7,5},{5,3},{3,1},{1,0},{8,10},{10,12},{12... | collective-permute-start | bytes 393224 | tf_op jit(solution)/shard_map/ppermute | solution.py:366
  138.6 12.3 %collective-permute-start.42 = (bf16[128,512]{1,0:T(8,128)(2,1)S(1)}, bf16[128,512]{1,0:T(8,128)(2,1)S(1)}, u32[]{:S(2)}, u32[]{:S(2)}) collective-permute-start(bf16[128,512]{1,0:T(8,128)(2,1)S(1)} %slice.243), channel_id=1, source_target_pairs={{0,1},{2,0},{4,2},{6,4},{7,6},{5,7},{3,5},{1,3},{8,9},{10,8},{12,1... | collective-permute-start | bytes 393224 | tf_op jit(solution)/shard_map/ppermute | solution.py:366
  153.8 11.0 %all-to-all-start.4 = ((bf16[8,16,640]{2,1,0:T(8,128)(2,1)}), bf16[8,16,640]{2,1,0:T(8,128)(2,1)S(1)}, u32[]{:S(2)}, u32[]{:S(2)}) async-start(bf16[8,16,640]{2,1,0:T(8,128)(2,1)} %bitcast.21), calls=%async_computation.4 | async-start | bytes 327680 | tf_op jit(solution)/shard_map/all_to_all | solution.py:380
  158.3 18.9 %collective-permute-start.19 = (bf16[128,1024]{1,0:T(8,128)(2,1)S(1)}, bf16[128,1024]{1,0:T(8,128)(2,1)S(1)}, u32[]{:S(2)}, u32[]{:S(2)}) collective-permute-start(bf16[128,1024]{1,0:T(8,128)(2,1)S(1)} %fusion.17.refs_0_), channel_id=1, source_target_pairs={{0,2},{2,4},{4,6},{6,7},{7,5},{5,3},{3,1},{1,0},{8,10},{10,12},{12... | collective-permute-start | bytes 786440 | tf_op jit(solution)/shard_map/ppermute | solution.py:366
  160.2 18.9 %collective-permute-start.23 = (bf16[128,1024]{1,0:T(8,128)(2,1)S(1)}, bf16[128,1024]{1,0:T(8,128)(2,1)}, u32[]{:S(2)}, u32[]{:S(2)}) collective-permute-start(bf16[128,1024]{1,0:T(8,128)(2,1)S(1)} %fusion.17.refs_0_), channel_id=1, source_target_pairs={{0,1},{2,0},{4,2},{6,4},{7,6},{5,7},{3,5},{1,3},{8,9},{10,8},{12,1... | collective-permute-start | bytes 786440 | tf_op jit(solution)/shard_map/ppermute | solution.py:366
  173.8 10.9 %all-to-all-start.5 = ((bf16[8,16,512]{2,1,0:T(8,128)(2,1)}), bf16[8,16,512]{2,1,0:T(8,128)(2,1)S(1)}, u32[]{:S(2)}, u32[]{:S(2)}) async-start(bf16[8,16,512]{2,1,0:T(8,128)(2,1)} %attend.5), calls=%async_computation.5 | async-start | bytes 262144 | tf_op jit(solution)/shard_map/all_to_all | solution.py:384
  177.2 17.4 %collective-permute-start.20 = (bf16[128,1024]{1,0:T(8,128)(2,1)S(1)}, bf16[128,1024]{1,0:T(8,128)(2,1)}, u32[]{:S(2)}, u32[]{:S(2)}) collective-permute-start(bf16[128,1024]{1,0:T(8,128)(2,1)S(1)} %collective-permute-done.19.refs_0_), channel_id=1, source_target_pairs={{0,2},{2,4},{4,6},{6,7},{7,5},{5,3},{3,1},{1,0},{8,10},{10,12},{12... | collective-permute-start | bytes 786440 | tf_op jit(solution)/shard_map/ppermute | solution.py:366
  179.1 16.2 %collective-permute-start.24 = (bf16[128,1024]{1,0:T(8,128)(2,1)}, bf16[128,1024]{1,0:T(8,128)(2,1)}, u32[]{:S(2)}, u32[]{:S(2)}) collective-permute-start(bf16[128,1024]{1,0:T(8,128)(2,1)} %collective-permute-done.23.refs_4_), channel_id=1, source_target_pairs={{0,1},{2,0},{4,2},{6,4},{7,6},{5,7},{3,5},{1,3},{8,9},{10,8},{12,1... | collective-permute-start | bytes 786440 | tf_op jit(solution)/shard_map/ppermute | solution.py:366
  187.4 11.4 %collective-permute-start.43 = (bf16[128,512]{1,0:T(8,128)(2,1)S(1)}, bf16[128,512]{1,0:T(8,128)(2,1)S(1)}, u32[]{:S(2)}, u32[]{:S(2)}) collective-permute-start(bf16[128,512]{1,0:T(8,128)(2,1)S(1)} %get-tuple-element.99), channel_id=1, source_target_pairs={{0,2},{2,4},{4,6},{6,7},{7,5},{5,3},{3,1},{1,0},{8,10},{10,12},{12... | collective-permute-start | bytes 393224 | tf_op jit(solution)/shard_map/ppermute | solution.py:366
  194.5 6.6 %collective-permute-start.21 = (bf16[128,1024]{1,0:T(8,128)(2,1)}, bf16[128,1024]{1,0:T(8,128)(2,1)S(1)}, u32[]{:S(2)}, u32[]{:S(2)}) collective-permute-start(bf16[128,1024]{1,0:T(8,128)(2,1)} %collective-permute-done.20.refs_0_), channel_id=1, source_target_pairs={{0,2},{2,4},{4,6},{6,7},{7,5},{5,3},{3,1},{1,0},{8,10},{10,12},{12... | collective-permute-start | bytes 786440 | tf_op jit(solution)/shard_map/ppermute | solution.py:366
  195.3 6.6 %collective-permute-start.25 = (bf16[128,1024]{1,0:T(8,128)(2,1)}, bf16[128,1024]{1,0:T(8,128)(2,1)S(1)}, u32[]{:S(2)}, u32[]{:S(2)}) collective-permute-start(bf16[128,1024]{1,0:T(8,128)(2,1)} %collective-permute-done.24.refs_4_), channel_id=1, source_target_pairs={{0,1},{2,0},{4,2},{6,4},{7,6},{5,7},{3,5},{1,3},{8,9},{10,8},{12,1... | collective-permute-start | bytes 786440 | tf_op jit(solution)/shard_map/ppermute | solution.py:366
  196.8 25.6 %collective-permute-start.47 = (bf16[128,512]{1,0:T(8,128)(2,1)}, bf16[128,512]{1,0:T(8,128)(2,1)S(1)}, u32[]{:S(2)}, u32[]{:S(2)}) collective-permute-start(bf16[128,512]{1,0:T(8,128)(2,1)} %get-tuple-element.100), channel_id=1, source_target_pairs={{0,1},{2,0},{4,2},{6,4},{7,6},{5,7},{3,5},{1,3},{8,9},{10,8},{12,1... | collective-permute-start | bytes 393224 | tf_op jit(solution)/shard_map/ppermute | solution.py:366
  201.2 13.9 %collective-permute-start.22 = (bf16[128,512]{1,0:T(8,128)(2,1)S(1)}, bf16[128,512]{1,0:T(8,128)(2,1)S(1)}, u32[]{:S(2)}, u32[]{:S(2)}) collective-permute-start(bf16[128,512]{1,0:T(8,128)(2,1)S(1)} %slice.229), channel_id=1, source_target_pairs={{0,2},{2,4},{4,6},{6,7},{7,5},{5,3},{3,1},{1,0},{8,10},{10,12},{12... | collective-permute-start | bytes 393224 | tf_op jit(solution)/shard_map/ppermute | solution.py:366
  202.0 13.2 %collective-permute-start.26 = (bf16[128,512]{1,0:T(8,128)(2,1)S(1)}, bf16[128,512]{1,0:T(8,128)(2,1)S(1)}, u32[]{:S(2)}, u32[]{:S(2)}) collective-permute-start(bf16[128,512]{1,0:T(8,128)(2,1)S(1)} %slice.230), channel_id=1, source_target_pairs={{0,1},{2,0},{4,2},{6,4},{7,6},{5,7},{3,5},{1,3},{8,9},{10,8},{12,1... | collective-permute-start | bytes 393224 | tf_op jit(solution)/shard_map/ppermute | solution.py:366
  204.1 38.4 %collective-permute-start.44 = (bf16[128,1024]{1,0:T(8,128)(2,1)}, bf16[128,1024]{1,0:T(8,128)(2,1)}, u32[]{:S(2)}, u32[]{:S(2)}) collective-permute-start(bf16[128,1024]{1,0:T(8,128)(2,1)} %pad_maximum_fusion.4), channel_id=1, source_target_pairs={{0,2},{2,4},{4,6},{6,7},{7,5},{5,3},{3,1},{1,0},{8,10},{10,12},{12... | collective-permute-start | bytes 786440 | tf_op jit(solution)/shard_map/ppermute | solution.py:366
  218.0 11.9 %all-to-all-start.2 = ((bf16[8,16,640]{2,1,0:T(8,128)(2,1)}), bf16[8,16,640]{2,1,0:T(8,128)(2,1)S(1)}, u32[]{:S(2)}, u32[]{:S(2)}) async-start(bf16[8,16,640]{2,1,0:T(8,128)(2,1)} %bitcast.12), calls=%async_computation.2 | async-start | bytes 327680 | tf_op jit(solution)/shard_map/all_to_all | solution.py:380
  223.2 49.2 %collective-permute-start.48 = (bf16[128,1024]{1,0:T(8,128)(2,1)}, bf16[128,1024]{1,0:T(8,128)(2,1)S(1)}, u32[]{:S(2)}, u32[]{:S(2)}) collective-permute-start(bf16[128,1024]{1,0:T(8,128)(2,1)} %pad_maximum_fusion.5), channel_id=1, source_target_pairs={{0,1},{2,0},{4,2},{6,4},{7,6},{5,7},{3,5},{1,3},{8,9},{10,8},{12,1... | collective-permute-start | bytes 786440 | tf_op jit(solution)/shard_map/ppermute | solution.py:366
  239.1 10.8 %all-to-all-start.3 = ((bf16[8,16,512]{2,1,0:T(8,128)(2,1)}), bf16[8,16,512]{2,1,0:T(8,128)(2,1)S(1)}, u32[]{:S(2)}, u32[]{:S(2)}) async-start(bf16[8,16,512]{2,1,0:T(8,128)(2,1)} %attend.4), calls=%async_computation.3 | async-start | bytes 262144 | tf_op jit(solution)/shard_map/all_to_all | solution.py:384
  243.5 28.9 %collective-permute-start.45 = (bf16[128,1024]{1,0:T(8,128)(2,1)S(1)}, bf16[128,1024]{1,0:T(8,128)(2,1)}, u32[]{:S(2)}, u32[]{:S(2)}) collective-permute-start(bf16[128,1024]{1,0:T(8,128)(2,1)S(1)} %fusion.2), channel_id=1, source_target_pairs={{0,2},{2,4},{4,6},{6,7},{7,5},{5,3},{3,1},{1,0},{8,10},{10,12},{12... | collective-permute-start | bytes 786440 | tf_op jit(solution)/shard_map/ppermute | solution.py:366
  264.9 7.4 %collective-permute-start.28 = (bf16[128,1024]{1,0:T(8,128)(2,1)S(1)}, bf16[128,1024]{1,0:T(8,128)(2,1)S(1)}, u32[]{:S(2)}, u32[]{:S(2)}) collective-permute-start(bf16[128,1024]{1,0:T(8,128)(2,1)S(1)} %pad_maximum_fusion.2), channel_id=1, source_target_pairs={{0,2},{2,4},{4,6},{6,7},{7,5},{5,3},{3,1},{1,0},{8,10},{10,12},{12... | collective-permute-start | bytes 786440 | tf_op jit(solution)/shard_map/ppermute | solution.py:366
  265.5 10.1 %collective-permute-start.32 = (bf16[128,1024]{1,0:T(8,128)(2,1)S(1)}, bf16[128,1024]{1,0:T(8,128)(2,1)S(1)}, u32[]{:S(2)}, u32[]{:S(2)}) collective-permute-start(bf16[128,1024]{1,0:T(8,128)(2,1)S(1)} %pad_maximum_fusion.3), channel_id=1, source_target_pairs={{0,1},{2,0},{4,2},{6,4},{7,6},{5,7},{3,5},{1,3},{8,9},{10,8},{12,1... | collective-permute-start | bytes 786440 | tf_op jit(solution)/shard_map/ppermute | solution.py:366
  273.5 7.5 %collective-permute-start.49 = (bf16[128,1024]{1,0:T(8,128)(2,1)S(1)}, bf16[128,1024]{1,0:T(8,128)(2,1)S(1)}, u32[]{:S(2)}, u32[]{:S(2)}) collective-permute-start(bf16[128,1024]{1,0:T(8,128)(2,1)S(1)} %get-tuple-element.106), channel_id=1, source_target_pairs={{0,1},{2,0},{4,2},{6,4},{7,6},{5,7},{3,5},{1,3},{8,9},{10,8},{12,1... | collective-permute-start | bytes 786440 | tf_op jit(solution)/shard_map/ppermute | solution.py:366
  279.5 6.5 %collective-permute-start.46 = (bf16[128,1024]{1,0:T(8,128)(2,1)S(1)}, bf16[128,1024]{1,0:T(8,128)(2,1)S(1)}, u32[]{:S(2)}, u32[]{:S(2)}) collective-permute-start(bf16[128,1024]{1,0:T(8,128)(2,1)S(1)} %get-tuple-element.105), channel_id=1, source_target_pairs={{0,2},{2,4},{4,6},{6,7},{7,5},{5,3},{3,1},{1,0},{8,10},{10,12},{12... | collective-permute-start | bytes 786440 | tf_op jit(solution)/shard_map/ppermute | solution.py:366
  281.1 7.1 %collective-permute-start.50 = (bf16[128,1024]{1,0:T(8,128)(2,1)S(1)}, bf16[128,1024]{1,0:T(8,128)(2,1)S(1)}, u32[]{:S(2)}, u32[]{:S(2)}) collective-permute-start(bf16[128,1024]{1,0:T(8,128)(2,1)S(1)} %fusion.1), channel_id=1, source_target_pairs={{0,1},{2,0},{4,2},{6,4},{7,6},{5,7},{3,5},{1,3},{8,9},{10,8},{12,1... | collective-permute-start | bytes 786440 | tf_op jit(solution)/shard_map/ppermute | solution.py:366
  282.1 6.6 %collective-permute-start.30 = (bf16[128,1024]{1,0:T(8,128)(2,1)S(1)}, bf16[128,1024]{1,0:T(8,128)(2,1)S(1)}, u32[]{:S(2)}, u32[]{:S(2)}) collective-permute-start(bf16[128,1024]{1,0:T(8,128)(2,1)S(1)} %get-tuple-element.109), channel_id=1, source_target_pairs={{0,2},{2,4},{4,6},{6,7},{7,5},{5,3},{3,1},{1,0},{8,10},{10,12},{12... | collective-permute-start | bytes 786440 | tf_op jit(solution)/shard_map/ppermute | solution.py:366
  (24 other events, 202.8 us)

commit v2 on v1

v2 whole, which is shorter than its diff:
```python
import functools

import jax
import jax.numpy as jnp
from jax import lax
from jax.experimental import pallas as pl
from jax.experimental.pallas import tpu as pltpu
from jax.sharding import PartitionSpec as P

QH = 32
KVH = 4
HEAD_DIM = 128

EPS = 1e-05
ROPE_BASE = 500000.0
NEGATIVE = -1e30
VMEM_LIMIT = 50 * 1024 * 1024
ATTEND_LIMIT = 57 * 1024 * 1024


def ring_order(mesh):
    count = mesh.shape["tensor"]
    natural = list(range(count))
    if count % 2 or count < 4:
        return natural
    axis = mesh.axis_names.index("tensor")
    places = [getattr(d, "coords", None) for d in jnp_line(mesh, axis)]
    if all(place is not None for place in places):
        steps = [sum(abs(a - b) for a, b in zip(p, q)) for p, q in zip(places, places[1:])]
        if max(steps) <= 1:
            return natural
    return natural[0::2] + natural[1::2][::-1]


def jnp_line(mesh, axis):
    devices = mesh.devices
    index = [0] * devices.ndim
    index[axis] = slice(None)
    return list(devices[tuple(index)])


def params(limit=None):
    return pltpu.CompilerParams(vmem_limit_bytes=limit or VMEM_LIMIT)


def after(value, *others):
    return lax.optimization_barrier((value, *others))[0]


IN_VMEM = pl.BlockSpec(memory_space=pltpu.VMEM)
IN_SMEM = pl.BlockSpec(memory_space=pltpu.SMEM)
IN_HBM = pl.BlockSpec(memory_space=pltpu.HBM)


def deal_kernel(block_rows, exits_ref, other_exits_ref, spans_ref, other_spans_ref, own_ref, other_ref, first_ref, second_ref, place_ref, span_ref, facts_ref):
    rows = own_ref.shape[0]
    half = block_rows // 2
    part = rows // 2
    own = (exits_ref[...] == 2).astype(jnp.float32)
    other = (other_exits_ref[...] == 2).astype(jnp.float32)
    line = lax.broadcasted_iota(jnp.int32, (8, rows), 0)
    marks = jnp.where(line == 0, own, jnp.where(line == 1, other, 0.0))
    marks = jnp.where(line == 2, 1.0 - own, jnp.where(line == 3, 1.0 - other, marks))
    down = lax.broadcasted_iota(jnp.int32, (rows, rows), 0)
    across = lax.broadcasted_iota(jnp.int32, (rows, rows), 1)
    same = (down // block_rows) == (across // block_rows)
    before = same & (down < across)
    marks16 = marks.astype(jnp.bfloat16)
    ranks = jnp.dot(marks16, before.astype(jnp.bfloat16), preferred_element_type=jnp.float32)
    totals = jnp.dot(marks16, same.astype(jnp.bfloat16), preferred_element_type=jnp.float32)

    def listed(which):
        count = totals[which : which + 1]
        place = jnp.where(marks[which : which + 1] > 0.5, ranks[which : which + 1], count + ranks[which + 2 : which + 3])
        low = jnp.minimum(count, float(half))
        high = jnp.maximum(count, float(half))
        return place, low, (place >= low) & (place < high)

    place, low, goes = listed(0)
    other_place, other_low, comes = listed(1)
    group = (lax.broadcasted_iota(jnp.int32, (1, rows), 1) // block_rows).astype(jnp.float32) * float(half)

    def slot(position):
        return jnp.where(position < float(half), group + position, group + position + float(part - half))

    stays_at = jnp.where(goes, -1.0, slot(place))
    comes_to = jnp.where(comes, slot(low + other_place - other_low), -1.0)
    leaves_to = jnp.where(goes, slot(other_low + place - low), -1.0)
    slots = down.astype(jnp.float32)
    stay = slots == stays_at
    come = slots == comes_to
    moved = jnp.dot(stay.astype(jnp.bfloat16), own_ref[...], preferred_element_type=jnp.float32) + jnp.dot(
        come.astype(jnp.bfloat16), other_ref[...], preferred_element_type=jnp.float32
    )
    moved = moved.astype(jnp.bfloat16)
    first_ref[...] = moved[:part]
    second_ref[...] = moved[part:]
    place_ref[0:1, :] = stays_at
    place_ref[1:2, :] = leaves_to
    spans = spans_ref[...].astype(jnp.float32)
    other_spans = other_spans_ref[...].astype(jnp.float32)
    span_ref[...] = jnp.sum(jnp.where(stay, spans, 0.0) + jnp.where(come, other_spans, 0.0), axis=1, keepdims=True)
    local = (lax.broadcasted_iota(jnp.int32, (1, rows), 1) % block_rows).astype(jnp.float32)

    def along(chosen, lengths, places):
        told = jnp.where(line == 0, lengths, jnp.where(line == 1, places, 0.0)).astype(jnp.bfloat16)
        return lax.dot_general(
            told, chosen.astype(jnp.bfloat16), (((1,), (1,)), ((), ())), preferred_element_type=jnp.float32
        )

    facts = along(stay, spans, local) + along(come, other_spans, local + float(block_rows))
    facts_ref[...] = facts[0:2].astype(jnp.int32)


def deal(block_rows, exits, other_exits, spans, other_spans, own, other):
    rows, width = own.shape
    shapes = [
        ((rows // 2, width), jnp.bfloat16),
        ((rows // 2, width), jnp.bfloat16),
        ((2, rows), jnp.float32),
        ((rows, 1), jnp.float32),
        ((2, rows), jnp.int32),
    ]
    lines = [v.reshape(1, rows) for v in (exits, other_exits, spans, other_spans)]
    return pl.pallas_call(
        functools.partial(deal_kernel, block_rows),
        out_shape=[jax.ShapeDtypeStruct(*s) for s in shapes],
        compiler_params=params(),
        name="deal",
    )(*lines, own, other)


def restore_kernel(place_ref, first_ref, second_ref, other_first_ref, other_second_ref, out_ref):
    part = first_ref.shape[0]
    rows = out_ref.shape[0]
    slots = lax.broadcasted_iota(jnp.int32, (rows, rows), 0).astype(jnp.float32)

    def back(chosen, values):
        return lax.dot_general(chosen, values, (((0,), (0,)), ((), ())), preferred_element_type=jnp.float32)

    stay = (slots == place_ref[0:1, :]).astype(jnp.bfloat16)
    leave = (slots == place_ref[1:2, :]).astype(jnp.bfloat16)
    total = back(stay[:part], first_ref[...]) + back(stay[part:], second_ref[...])
    total = total + back(leave[:part], other_first_ref[...]) + back(leave[part:], other_second_ref[...])
    out_ref[...] = total.astype(jnp.bfloat16)


def restore(places, first, second, other_first, other_second):
    return pl.pallas_call(
        restore_kernel,
        out_shape=jax.ShapeDtypeStruct((places.shape[1], first.shape[1]), jnp.bfloat16),
        compiler_params=params(),
        name="restore",
    )(places, first, second, other_first, other_second)


def project_kernel(level, kinds, depth, has_sum, finish, table_ref, *refs):
    refs = list(refs)
    parts = table_ref.shape[0]
    width = depth // parts
    blocks = []
    for pieces, place in kinds:
        blocks.append((refs[:pieces], place))
        refs = refs[pieces:]
    gain_ref, query_weight_ref, fresh_weight_ref = refs[:3]
    *refs, query_held, fresh_held, sems = refs[3:]
    rows = blocks[0][0][0].shape[0]
    copies = []
    for index, (_, place) in enumerate(blocks):
        at = pl.ds(pl.multiple_of(table_ref[place] * width, width), width)
        pair = (
            pltpu.make_async_copy(query_weight_ref.at[level, at, :], query_held.at[index], sems.at[index, 0]),
            pltpu.make_async_copy(fresh_weight_ref.at[level, at, :], fresh_held.at[index], sems.at[index, 1]),
        )
        for copy in pair:
            copy.start()
        copies.append(pair)
    if has_sum:
        query, fresh, square = (ref[...] for ref in refs[:3])
        refs = refs[3:]
    else:
        query = jnp.zeros((rows, query_weight_ref.shape[2]), jnp.float32)
        fresh = jnp.zeros((rows, fresh_weight_ref.shape[2]), jnp.float32)
        square = jnp.zeros((rows, HEAD_DIM), jnp.float32)
    for index, (value_refs, place) in enumerate(blocks):
        at = pl.multiple_of(table_ref[place] * width, width)
        for copy in copies[index]:
            copy.wait()
        row = 0
        for value_ref in value_refs:
            span = value_ref.shape[1]
            values = value_ref[...].astype(jnp.float32)
            scaled = (values * gain_ref[level : level + 1, pl.ds(at, span)]).astype(jnp.bfloat16)
            query = query + jnp.dot(scaled, query_held[index, row : row + span], preferred_element_type=jnp.float32)
            fresh = fresh + jnp.dot(scaled, fresh_held[index, row : row + span], preferred_element_type=jnp.float32)
            squares = values * values
            for column in range(0, span, HEAD_DIM):
                square = square + squares[:, column : column + HEAD_DIM]
            at = at + span
            row += span
    if not finish:
        refs[0][...] = query
        refs[1][...] = fresh
        refs[2][...] = square
        return
    cosine_ref, sine_ref, out_ref = refs
    factor = lax.rsqrt(jnp.sum(square, axis=1, keepdims=True) / depth + EPS)
    cosine = cosine_ref[...]
    sine = sine_ref[...]
    columns = query.shape[1]
    for column in range(0, columns, HEAD_DIM):
        head = query[:, column : column + HEAD_DIM] * factor
        turned = head * cosine + pltpu.roll(head, HEAD_DIM // 2, 1) * sine
        out_ref[:, column : column + HEAD_DIM] = turned.astype(jnp.bfloat16)
    out_ref[:, columns:] = (fresh * factor).astype(jnp.bfloat16)


def project(level, table, gain, query_weight, fresh_weight, blocks, sums=None, rope=None):
    rows = blocks[0][0][0].shape[0]
    parts = table.shape[0]
    depth = query_weight.shape[1]
    columns = query_weight.shape[2]
    fresh_columns = fresh_weight.shape[2]
    operands = [table]
    for values, _ in blocks:
        operands += list(values)
    operands += [gain, query_weight, fresh_weight]
    if sums is not None:
        operands += list(sums)
    if rope is not None:
        operands += list(rope)
        out_shape = jax.ShapeDtypeStruct((rows, columns + fresh_columns), jnp.bfloat16)
    else:
        out_shape = [jax.ShapeDtypeStruct((rows, n), jnp.float32) for n in (columns, fresh_columns, HEAD_DIM)]
    kinds = [(len(values), place) for values, place in blocks]
    body = functools.partial(project_kernel, level, kinds, depth, sums is not None, rope is not None)
    flops = 2 * rows * (depth // table.shape[0]) * len(blocks) * (columns + fresh_columns)
    return pl.pallas_call(
        body,
        out_shape=out_shape,
        in_specs=[IN_SMEM] + [IN_HBM if v is query_weight or v is fresh_weight else IN_VMEM for v in operands[1:]],
        out_specs=jax.tree.map(lambda _: IN_VMEM, out_shape),
        scratch_shapes=[
            pltpu.VMEM((len(blocks), depth // parts, columns), jnp.bfloat16),
            pltpu.VMEM((len(blocks), depth // parts, fresh_columns), jnp.bfloat16),
            pltpu.SemaphoreType.DMA((len(blocks), 2)),
        ],
        compiler_params=params(),
        cost_estimate=pl.CostEstimate(flops=flops, bytes_accessed=flops // rows, transcendentals=0),
        name="project",
    )(*operands)


def attend_kernel(level, start, columns, table_ref, facts_ref, got_ref, cosine_ref, sine_ref, own_ref, other_ref, out_ref, held, sems):
    parts, rows, _ = got_ref.shape
    block_rows = own_ref.shape[1]
    slots = held.shape[1]
    first = start + table_ref[0] * rows
    for row in range(rows):
        source = facts_ref[1, first + row]

        @pl.when(source < block_rows)
        def _():
            pltpu.make_async_copy(own_ref.at[level, source], held.at[row], sems.at[row]).start()

        @pl.when(source >= block_rows)
        def _():
            pltpu.make_async_copy(other_ref.at[level, source - block_rows], held.at[row], sems.at[row]).start()

    heads_dev = columns // HEAD_DIM
    group = QH // KVH
    fresh = jnp.concatenate([got_ref[s, :, columns:].astype(jnp.float32) for s in range(parts)], axis=1)
    mine = pl.ds(pl.multiple_of(first, rows), rows)
    cosine = cosine_ref[mine, :]
    sine = sine_ref[mine, :]
    scale = HEAD_DIM ** (-0.5)
    total_rows = group * rows
    across = lax.broadcasted_iota(jnp.int32, (1, rows * slots), 1)
    owner = across // slots
    span = jnp.zeros_like(across)
    for row in range(rows):
        span = jnp.where(owner == row, facts_ref[0, first + row], span)
    owner = jnp.where(across % slots < span, owner, -1)
    down = lax.broadcasted_iota(jnp.int32, (total_rows, 1), 0) % rows
    valid = down == owner
    for row in range(rows):
        pltpu.make_async_copy(own_ref.at[level, 0], held.at[row], sems.at[row]).wait()
    for j in range(KVH):
        tiles = []
        for head in range(j * group, (j + 1) * group):
            at = head % heads_dev * HEAD_DIM
            tiles.append(got_ref[head // heads_dev, :, at : at + HEAD_DIM].astype(jnp.float32))
        query = jnp.concatenate(tiles, axis=0)
        new_key = fresh[:, j * HEAD_DIM : (j + 1) * HEAD_DIM]
        new_key = new_key * cosine + pltpu.roll(new_key, HEAD_DIM // 2, 1) * sine
        new_key = new_key.astype(jnp.bfloat16).astype(jnp.float32)
        new_value = fresh[:, (KVH + j) * HEAD_DIM : (KVH + j + 1) * HEAD_DIM]
        keys = held[:, :, 2 * j * HEAD_DIM : (2 * j + 1) * HEAD_DIM].reshape(rows * slots, HEAD_DIM)
        values = held[:, :, (2 * j + 1) * HEAD_DIM : (2 * j + 2) * HEAD_DIM].reshape(rows * slots, HEAD_DIM)
        scores = lax.dot_general(
            query.astype(jnp.bfloat16), keys, (((1,), (1,)), ((), ())), preferred_element_type=jnp.float32
        )
        scores = jnp.where(valid, scores * scale, NEGATIVE)
        own = jnp.sum(query * jnp.concatenate([new_key] * group, axis=0), axis=1, keepdims=True) * scale
        highest = jnp.maximum(jnp.max(scores, axis=1, keepdims=True), own)
        weights = jnp.where(valid, jnp.exp(scores - highest), 0.0)
        own_weight = jnp.exp(own - highest)
        total = jnp.sum(weights, axis=1, keepdims=True) + own_weight
        mixed = jnp.dot(weights.astype(jnp.bfloat16), values, preferred_element_type=jnp.float32)
        mixed = (mixed + own_weight * jnp.concatenate([new_value] * group, axis=0)) / total
        for head in range(j * group, (j + 1) * group):
            at = head % heads_dev * HEAD_DIM
            tile = mixed[(head - j * group) * rows : (head - j * group + 1) * rows]
            out_ref[head // heads_dev, :, at : at + HEAD_DIM] = tile.astype(jnp.bfloat16)


def attend(level, start, table, got, columns, facts, cosine, sine, own, other):
    parts, rows, _ = got.shape
    _, _, slots, depth = own.shape
    return pl.pallas_call(
        functools.partial(attend_kernel, level, start, columns),
        out_shape=jax.ShapeDtypeStruct((parts, rows, columns), jnp.bfloat16),
        in_specs=[IN_SMEM, IN_SMEM, IN_VMEM, IN_VMEM, IN_VMEM, IN_HBM, IN_HBM],
        out_specs=IN_VMEM,
        scratch_shapes=[pltpu.VMEM((rows, slots, depth), jnp.bfloat16), pltpu.SemaphoreType.DMA((rows,))],
        compiler_params=params(ATTEND_LIMIT),
        cost_estimate=pl.CostEstimate(flops=10**8, bytes_accessed=rows * slots * depth * 2, transcendentals=0),
        name="attend",
    )(table, facts, got, cosine, sine, own, other)


def output_kernel(level, table_ref, value_ref, weight_ref, front_ref, back_ref, *refs):
    parts = table_ref.shape[0]
    width = weight_ref.shape[2] // parts
    *out_refs, held, sems = refs
    copies = []
    order = sorted(range(parts), key=lambda place: -abs(place - parts // 2))[::-1]
    for place in order:
        at = pl.ds(pl.multiple_of(table_ref[place] * width, width), width)
        copies.append(pltpu.make_async_copy(weight_ref.at[level, :, at], held.at[place], sems.at[place]))
        copies[-1].start()
    values = value_ref[...]
    for place, copy in zip(order, copies):
        copy.wait()
        product = jnp.dot(values, held[place], preferred_element_type=jnp.float32).astype(jnp.bfloat16)
        if place == parts // 2:
            front_ref[...] = product[:, : width // 2]
            back_ref[...] = product[:, width // 2 :]
        else:
            out_refs[place - (place > parts // 2)][...] = product


def output_blocks(level, table, values, weight):
    rows, depth = values.shape
    parts = table.shape[0]
    width = weight.shape[2] // parts
    shapes = [(rows, width // 2)] * 2 + [(rows, width)] * (parts - 1)
    flops = 2 * rows * depth * width * parts
    return pl.pallas_call(
        functools.partial(output_kernel, level),
        out_shape=[jax.ShapeDtypeStruct(s, jnp.bfloat16) for s in shapes],
        in_specs=[IN_SMEM, IN_VMEM, IN_HBM],
        out_specs=[IN_VMEM] * (parts + 1),
        scratch_shapes=[pltpu.VMEM((parts, depth, width), jnp.bfloat16), pltpu.SemaphoreType.DMA((parts,))],
        compiler_params=params(),
        cost_estimate=pl.CostEstimate(flops=flops, bytes_accessed=flops // rows, transcendentals=0),
        name="output",
    )(table, values, weight)


class Layer:
    def __init__(self, level, start, ring, table, share, told, weights):
        self.level, self.start, self.ring, self.table, self.share = level, start, ring, table, share
        self.facts, self.cosine, self.sine, self.own, self.other = told
        self.gain, self.query_weight, self.fresh_weight, self.out_weight = weights
        self.half = len(ring) // 2
        self.ahead = self.behind = share
        self.blocks = [((share,), 0)]
        self.sums = None

    def hop(self, to_front, to_back, held):
        parts = len(self.ring)
        forward = [(self.ring[i], self.ring[(i + 1) % parts]) for i in range(parts)]
        backward = [(self.ring[i], self.ring[(i - 1) % parts]) for i in range(parts)]
        to_front, to_back = lax.optimization_barrier((to_front, to_back, held))[:2]
        self.last = lax.ppermute(to_front, "tensor", forward), lax.ppermute(to_back, "tensor", backward)
        return self.last

    def gather(self, step, *held):
        width = self.share.shape[1] // 2
        if step < self.half:
            self.behind, self.ahead = self.hop(self.behind, self.ahead, held)
            self.blocks += [((self.behind,), -step % len(self.ring)), ((self.ahead,), step)]
        else:
            halves = self.hop(self.behind[:, :width], self.ahead[:, width:], held)
            self.blocks.append((halves, self.half))

    def project(self, places=None, final=False, held=()):
        weights = (self.gain, self.query_weight, self.fresh_weight)
        rope = None
        if final:
            rows = slice(self.start, self.start + self.share.shape[0])
            rope = self.cosine[rows], self.sine[rows]
        if places is None:
            blocks, self.blocks = self.blocks, []
        else:
            near = [min(place, len(self.ring) - place) <= places for _, place in self.blocks]
            blocks = [block for block, is_near in zip(self.blocks, near) if is_near]
            self.blocks = [block for block, is_near in zip(self.blocks, near) if not is_near]
        (values, place), *others = blocks
        values = (after(values[0], held), *values[1:])
        blocks = [(values, place), *others]
        self.sums = project(self.level, self.table, *weights, blocks, self.sums, rope)
        return self.sums

    def project_ring(self, steps, *held):
        first = 1 + sum(len(values) == 1 for values, _ in self.blocks) // 2
        for step in range(first, steps + 1):
            ready = self.sums if step > 2 else None
            self.gather(step, ready, *(held if step == first + 1 else ()))
            if 2 <= step < steps:
                self.project(step - 1)

    def ask(self, *held):
        parts = len(self.ring)
        mine = after(self.sums, held)
        mine = mine.reshape(parts, mine.shape[0] // parts, mine.shape[1])
        self.got = lax.all_to_all(mine, "tensor", split_axis=0, concat_axis=0, tiled=True)

    def attend(self, *held):
        columns = self.query_weight.shape[2]
        got = after(self.got, held)
        self.mixed = attend(
            self.level, self.start, self.table, got, columns, self.facts, self.cosine, self.sine, self.own, self.other
        )

    def answer(self, *held):
        mixed = after(self.mixed, held)
        back = lax.all_to_all(mixed, "tensor", split_axis=0, concat_axis=0, tiled=True)
        self.attended = back.reshape(self.share.shape[0], self.query_weight.shape[2])

    def output(self, *held):
        attended = after(self.attended, held)
        made = output_blocks(self.level, self.table, attended, self.out_weight)
        self.halves, self.products = made[:2], made[2:]

    def product(self, place):
        place = place % len(self.ring)
        return self.products[place - (place > self.half)].astype(jnp.float32)

    def scatter(self, step, *held):
        width = self.share.shape[1] // 2
        if step == 1:
            self.last = self.hop(*self.halves, held)
            return
        from_back, from_front = (v.astype(jnp.float32) for v in self.last)
        to_front = self.product(self.half + 1 - step)
        to_back = self.product(step - 1 - self.half)
        if step == 2:
            to_front = jnp.concatenate([to_front[:, :width] + from_back, to_front[:, width:]], axis=1)
            to_back = jnp.concatenate([to_back[:, :width], to_back[:, width:] + from_front], axis=1)
        else:
            to_front = to_front + from_back
            to_back = to_back + from_front
        self.hop(to_front.astype(jnp.bfloat16), to_back.astype(jnp.bfloat16), held)

    def result(self):
        from_back, from_front = (v.astype(jnp.float32) for v in self.last)
        total = self.product(0) + (from_back + from_front)
        return (self.share.astype(jnp.float32) + total).astype(jnp.bfloat16)


def local(ring, hidden, norm_gain, w_query, w_kv, w_out, cache, lengths, exits):
    parts = len(ring)
    rows, width = hidden.shape
    block_rows = rows // parts
    half = block_rows // 2
    part = rows // 2
    me = lax.axis_index("tensor")
    swap = [(0, 1), (1, 0)]
    places = [ring.index(i) for i in range(parts)]
    tables = jnp.array([[ring[(places[i] + r) % parts] for r in range(parts)] for i in range(parts)], jnp.int32)
    table = lax.dynamic_index_in_dim(tables, me, 0, False)

    other_exits = lax.ppermute(exits, "dp", swap)
    other_lengths = lax.ppermute(lengths, "dp", swap)
    other_hidden = lax.ppermute(hidden, "dp", swap)
    first, second, restored, span, facts = deal(
        block_rows, exits, other_exits, lengths, other_lengths, hidden, other_hidden
    )
    other_cache = lax.ppermute(after(cache, facts), "dp", swap)

    turns = HEAD_DIM // 2
    freqs = ROPE_BASE ** (-jnp.arange(turns, dtype=jnp.float32) / turns)
    angle = span * freqs[None, :]
    cosine = jnp.cos(angle)
    sine = jnp.sin(angle)
    cosine = jnp.concatenate([cosine, cosine], axis=1)
    sine = jnp.concatenate([-sine, sine], axis=1)

    told = facts, cosine, sine, cache, other_cache
    weights = (norm_gain, w_query, w_kv, w_out)
    steps = parts // 2
    a = Layer(0, 0, ring, table, first, told, weights)
    b = Layer(0, part, ring, table, second, told, weights)

    a.gather(1)
    a.project_ring(steps)
    b.gather(1, a.last)
    a.project(final=True)
    a.ask()
    for step in range(2, steps - 1):
        b.gather(step, a.sums)
    a.attend(b.last)
    a.answer()
    b.gather(steps - 1, a.got)
    b.project(2)
    a.output(b.last, b.sums)
    b.gather(steps, a.attended)
    a.scatter(1, b.last)
    a.scatter(2, a.products)
    b.project(final=True, held=a.products)
    for step in range(3, steps + 1):
        a.scatter(step, b.sums)
    b.ask()
    first = a.result()
    a = Layer(1, 0, ring, table, first, told, weights)
    a.gather(1, b.got)
    b.attend()
    b.answer()
    a.gather(2, b.mixed)
    b.output()
    a.project_ring(steps, b.products)
    b.scatter(1, a.last)
    a.project(final=True)
    a.ask()
    for step in range(2, steps - 1):
        b.scatter(step, a.sums)
    a.attend(b.last)
    a.answer()
    b.scatter(steps - 1, a.got)
    a.output(b.last)
    b.scatter(steps, a.attended)
    a.scatter(1, b.last)
    second = b.result()
    other_second = lax.ppermute(second, "dp", swap)
    for step in range(2, steps + 1):
        a.scatter(step)
    first = a.result()
    other_first = lax.ppermute(first, "dp", swap)
    return restore(restored, first, second, other_first, other_second)


def solution(mesh):
    in_specs = (
        P(("group", "dp"), "tensor"),
        P(),
        P(None, None, "tensor"),
        P(None, None, "tensor"),
        P(None, "tensor", None),
        P(None, ("group", "dp", "tensor"), None, None),
        P(("group", "dp")),
        P(("group", "dp")),
    )
    out_specs = P(("group", "dp"), "tensor")
    body = functools.partial(local, ring_order(mesh))
    return jax.shard_map(body, mesh=mesh, in_specs=in_specs, out_specs=out_specs, check_vma=False)
```

time: 298 us -> 246 us (0.83)
  Pallas kernels: 86.6 us -> 56.3 us
  local copies, waits for them, and re-layouts: 15.4 us -> 4.79 us
  other arithmetic: 11.3 us -> 3.27 us
  waiting for transfers between devices: 106 us -> 103 us
    pallas_call x25 -> x14, Pallas kernels: 85.9 us -> 55.7 us  [the longest x7 25.3 us: project(): pl.pallas_call(body, out_shape=out_shape, in_specs=[IN_SMEM] + [IN_HBM if...]
    unnamed x26 -> x30, local copies, waits for them, and re-layouts: 14 us -> 3.98 us
    convert_element_type x15, other arithmetic: 7.17 us -> 1.32 us  [the longest x12 0.8 us: scatter(): self.hop(to_front.astype(jnp.bfloat16), to_back.astype(jnp.bfloat16), held)]
    ppermute x50 -> x51, waiting for transfers between devices: 73.4 us -> 67.7 us  [the longest x24 47.8 us: hop(): lax.ppermute(to_front, 'tensor', forward)]
    ppermute x50 -> x51, starting transfers between devices: 51.1 us -> 52.8 us  [the longest x24 27.9 us: hop(): lax.ppermute(to_back, 'tensor', backward)]
  transfers between devices with their start and end apart: 59 -> 60, of which waited for: 25 -> 38; matrix products, arithmetic and copies ran while one was open for 4% -> 1% of each run, Pallas kernels for 27% -> 22%
where the time goes in v2:
time: 246 us; the launch traced here: 245 us
  waiting for transfers between devices  103 us (42%)
  starting transfers between devices  77.3 us (31%)
  Pallas kernels  56.3 us (23%)
  local copies, waits for them, and re-layouts  4.79 us (2%)
  other arithmetic  3.27 us (1%)
    ppermute x24, waiting for transfers between devices, hop(): lax.ppermute(to_front, 'tensor', forward)  47.8 us
    ppermute x24, starting transfers between devices, hop(): lax.ppermute(to_back, 'tensor', backward)  27.9 us
    pallas_call x7, Pallas kernels, project(): pl.pallas_call(body, out_shape=out_shape, in_specs=[IN_SMEM] + [IN_HBM if...  25.3 us
    ppermute x24, starting transfers between devices, hop(): lax.ppermute(to_front, 'tensor', forward)  23.9 us
    ppermute x24, waiting for transfers between devices, hop(): lax.ppermute(to_back, 'tensor', backward)  18.6 us
    all_to_all x3, waiting for transfers between devices, answer(): lax.all_to_all(mixed, 'tensor', split_axis=0, concat_axis=0, tiled=True)  17.8 us
    all_to_all x3, waiting for transfers between devices, ask(): lax.all_to_all(mine, 'tensor', split_axis=0, concat_axis=0, tiled=True)  16 us
    pallas_call x3, Pallas kernels, attend(): pl.pallas_call(functools.partial(attend_kernel, level, start, columns), o...  15.7 us
  transfers between devices with their start and end apart: 60, of which 38 were waited for; matrix products, arithmetic and copies ran while one was open for 1% of the time, Pallas kernels for 22%

profile of v2, /device:TPU:0, one launch (start us, length us, event | category | flops | bytes accessed | tf_op | source)
XLA Modules:
  0.0 245.2 jit_solution(2208666816719962400)
XLA Ops:
  5.7 2.7 %collective-permute-start.3 = (bf16[128,1024]{1,0:T(8,128)(2,1)S(1)}, bf16[128,1024]{1,0:T(8,128)(2,1)S(1)}, u32[]{:S(2)}, u32[]{:S(2)}) collective-permute-start(bf16[128,1024]{1,0:T(8,128)(2,1)S(1)} %get-tuple-element.107.refs_0_), channel_id=1, source_target_pairs={{0,2},{2,4},{4,6},{6,7},{7,5},{5,3},{3,1},{1,0},{8,10},{10,12},{12... | collective-permute-start | bytes 786440 | tf_op jit(solution)/shard_map/ppermute | solution.py:386
  8.4 6.8 %collective-permute-done.3.refs_1_ = bf16[128,1024]{1,0:T(8,128)(2,1)S(1)} collective-permute-done((bf16[128,1024]{1,0:T(8,128)(2,1)S(1)}, bf16[128,1024]{1,0:T(8,128)(2,1)S(1)}, u32[]{:S(2)}, u32[]{:S(2)}) %collective-permute-start.3) | collective-permute-done | bytes 262176 | tf_op jit(solution)/shard_map/ppermute | solution.py:386
  20.2 3.2 %project.7 = (f32[128,512]{1,0:T(8,128)S(1)}, f32[128,128]{1,0:T(8,128)S(1)}, f32[128,128]{1,0:T(8,128)S(1)}) custom-call(s32[8]{0:T(128)S(1)} %dynamic-slice_bitcast_fusion.table_ref, bf16[128,1024]{1,0:T(8,128)(2,1)S(1)} %get-tuple-element.107.refs_0_, bf16[128,1024]{1,0:T(8,128)(2,1)S(1)} %collective-permute-done.3.refs_1_, ...), custom_call_target="tpu_custom_call" | custom-call | flops 503316480 | bytes 3932160 | tf_op jit(solution)/shard_map/project/pallas_call | solution.py:238
  27.5 2.6 %project.8 = (f32[128,512]{1,0:T(8,128)S(1)}, f32[128,128]{1,0:T(8,128)S(1)}, f32[128,128]{1,0:T(8,128)S(1)}) custom-call(s32[8]{0:T(128)S(1)} %dynamic-slice_bitcast_fusion.table_ref, bf16[128,1024]{1,0:T(8,128)(2,1)S(1)} %collective-permute-done.5.refs_0_, bf16[128,1024]{1,0:T(8,128)(2,1)S(1)} %collective-permute-done.6.refs_1_, f32[2,8192]{1,0:T(2,128)S(1)} %copy-done.1, ...), custom_call_target="tpu_custom_call" | custom-call | flops 335544320 | bytes 2621440 | tf_op jit(solution)/shard_map/project/pallas_call | solution.py:238
  35.6 3.2 %collective-permute-done.9.refs_2_ = bf16[128,512]{1,0:T(8,128)(2,1)S(1)} collective-permute-done((bf16[128,512]{1,0:T(8,128)(2,1)S(1)}, bf16[128,512]{1,0:T(8,128)(2,1)S(1)}, u32[]{:S(2)}, u32[]{:S(2)}) %collective-permute-start.9) | collective-permute-done | bytes 131104 | tf_op jit(solution)/shard_map/ppermute | solution.py:386
  38.8 2.5 %collective-permute-done.10.refs_3_ = bf16[128,512]{1,0:T(8,128)(2,1)S(1)} collective-permute-done((bf16[128,512]{1,0:T(8,128)(2,1)S(1)}, bf16[128,512]{1,0:T(8,128)(2,1)S(1)}, u32[]{:S(2)}, u32[]{:S(2)}) %collective-permute-start.10) | collective-permute-done | bytes 131104 | tf_op jit(solution)/shard_map/ppermute | solution.py:386
  44.0 3.8 %project.9 = bf16[128,640]{1,0:T(8,128)(2,1)} custom-call(s32[8]{0:T(128)S(1)} %dynamic-slice_bitcast_fusion.table_ref, bf16[128,1024]{1,0:T(8,128)(2,1)S(1)} %collective-permute-done.7.refs_0_, bf16[128,1024]{1,0:T(8,128)(2,1)S(1)} %collective-permute-done.8.refs_1_, bf16[128,512]{1,0:T(8,128)(2,1)S(1)} %collective-permute-done.9.refs_2_, ...), custom_call_target="tpu_custom_call" | custom-call | flops 503316480 | bytes 3932160 | tf_op jit(solution)/shard_map/project/pallas_call | solution.py:238
  47.8 3.4 %all-to-all-start = ((bf16[8,16,640]{2,1,0:T(8,128)(2,1)}), bf16[8,16,640]{2,1,0:T(8,128)(2,1)S(1)}, u32[]{:S(2)}, u32[]{:S(2)}) async-start(bf16[8,16,640]{2,1,0:T(8,128)(2,1)} %bitcast.5), calls=%async_computation | async-start | bytes 327680 | tf_op jit(solution)/shard_map/all_to_all | solution.py:428
  53.3 6.5 %all-to-all-done.got_ref = bf16[8,16,640]{2,1,0:T(8,128)(2,1)S(1)} async-done(((bf16[8,16,640]{2,1,0:T(8,128)(2,1)}), bf16[8,16,640]{2,1,0:T(8,128)(2,1)S(1)}, u32[]{:S(2)}, u32[]{:S(2)}) %all-to-all-start) | async-done | bytes 163872 | tf_op jit(solution)/shard_map/all_to_all | solution.py:428
  65.3 5.2 %attend.3 = bf16[8,16,512]{2,1,0:T(8,128)(2,1)} custom-call(s32[8]{0:T(128)} %copy-done.5, s32[2,256]{1,0:T(2,128)} %copy-done.9, bf16[8,16,640]{2,1,0:T(8,128)(2,1)} %copy-done.12, f32[256,128]{1,0:T(8,128)} %get-tuple-element.208.cosine_ref, f32[256,128]{1,0:T(8,128)} %get-tuple-element.209.sine_ref, bf16[2,32,64,1024]{3,2,1,0:T(8,128)(2,1)} %own_ref.7, ...), custom_call_target="tpu_custom_call" | custom-call | flops 100000000 | bytes 2097152 | tf_op jit(solution)/shard_map/attend/pallas_call | solution.py:320
  70.5 4.0 %all-to-all-start.1 = ((bf16[8,16,512]{2,1,0:T(8,128)(2,1)}), bf16[8,16,512]{2,1,0:T(8,128)(2,1)S(1)}, u32[]{:S(2)}, u32[]{:S(2)}) async-start(bf16[8,16,512]{2,1,0:T(8,128)(2,1)} %attend.3), calls=%async_computation.1 | async-start | bytes 262144 | tf_op jit(solution)/shard_map/all_to_all | solution.py:439
  74.6 7.3 %all-to-all-done.1 = bf16[8,16,512]{2,1,0:T(8,128)(2,1)S(1)} async-done(((bf16[8,16,512]{2,1,0:T(8,128)(2,1)}), bf16[8,16,512]{2,1,0:T(8,128)(2,1)S(1)}, u32[]{:S(2)}, u32[]{:S(2)}) %all-to-all-start.1) | async-done | bytes 131104 | tf_op jit(solution)/shard_map/all_to_all | solution.py:439
  81.9 2.0 collective-permute-start.19
  83.9 4.1 %project.10 = (f32[128,512]{1,0:T(8,128)S(1)}, f32[128,128]{1,0:T(8,128)S(1)}, f32[128,128]{1,0:T(8,128)S(1)}) custom-call(s32[8]{0:T(128)S(1)} %copy-done.6, bf16[128,1024]{1,0:T(8,128)(2,1)S(1)} %get-tuple-element.123.refs_0_, bf16[128,1024]{1,0:T(8,128)(2,1)S(1)} %collective-permute-done.11.refs_1_, ...), custom_call_target="tpu_custom_call" | custom-call | flops 838860800 | bytes 6553600 | tf_op jit(solution)/shard_map/project/pallas_call | solution.py:238
  88.0 4.4 %output.3 = (bf16[128,512]{1,0:T(8,128)(2,1)S(1)}, bf16[128,512]{1,0:T(8,128)(2,1)S(1)}, bf16[128,1024]{1,0:T(8,128)(2,1)S(1)}, bf16[128,1024]{1,0:T(8,128)(2,1)...) custom-call(s32[8]{0:T(128)S(1)} %copy-done.6, ...), custom_call_target="tpu_custom_call" | custom-call | flops 1073741824 | bytes 8388608 | tf_op jit(solution)/shard_map/output/pallas_call | solution.py:359
  92.5 2.1 collective-permute-start.21
  94.5 2.9 %collective-permute-done.20 = bf16[128,512]{1,0:T(8,128)(2,1)S(1)} collective-permute-done((bf16[128,512]{1,0:T(8,128)(2,1)S(1)}, bf16[128,512]{1,0:T(8,128)(2,1)S(1)}, u32[]{:S(2)}, u32[]{:S(2)}) %collective-permute-start.20) | collective-permute-done | bytes 131104 | tf_op jit(solution)/shard_map/ppermute | solution.py:386
  99.9 3.8 %project.11 = bf16[128,640]{1,0:T(8,128)(2,1)} custom-call(s32[8]{0:T(128)S(1)} %copy-done.6, bf16[128,1024]{1,0:T(8,128)(2,1)S(1)} %collective-permute-done.16.refs_0_, bf16[128,1024]{1,0:T(8,128)(2,1)S(1)} %collective-permute-done.17.refs_1_, bf16[128,512]{1,0:T(8,128)(2,1)S(1)} %collective-permute-done.18.refs_2_, ...), custom_call_target="tpu_custom_call" | custom-call | flops 503316480 | bytes 3932160 | tf_op jit(solution)/shard_map/project/pallas_call | solution.py:238
  103.7 2.1 collective-permute-done.22
  105.9 2.3 collective-permute-start.24
  108.3 5.2 %collective-permute-done.24 = bf16[128,1024]{1,0:T(8,128)(2,1)S(1)} collective-permute-done((bf16[128,1024]{1,0:T(8,128)(2,1)S(1)}, bf16[128,1024]{1,0:T(8,128)(2,1)S(1)}, u32[]{:S(2)}, u32[]{:S(2)}) %collective-permute-start.24) | collective-permute-done | bytes 262176 | tf_op jit(solution)/shard_map/ppermute | solution.py:386
  113.5 2.7 %collective-permute-done.25 = bf16[128,1024]{1,0:T(8,128)(2,1)S(1)} collective-permute-done((bf16[128,1024]{1,0:T(8,128)(2,1)S(1)}, bf16[128,1024]{1,0:T(8,128)(2,1)S(1)}, u32[]{:S(2)}, u32[]{:S(2)}) %collective-permute-start.25) | collective-permute-done | bytes 262176 | tf_op jit(solution)/shard_map/ppermute | solution.py:386
  116.3 3.1 %collective-permute-start.26 = (bf16[128,1024]{1,0:T(8,128)(2,1)S(1)}, bf16[128,1024]{1,0:T(8,128)(2,1)S(1)}, u32[]{:S(2)}, u32[]{:S(2)}) collective-permute-start(bf16[128,1024]{1,0:T(8,128)(2,1)S(1)} %add_convert_fusion.12), channel_id=1, source_target_pairs={{0,2},{2,4},{4,6},{6,7},{7,5},{5,3},{3,1},{1,0},{8,10},{10,12},{12... | collective-permute-start | bytes 786440 | tf_op jit(solution)/shard_map/ppermute | solution.py:386
  119.4 4.6 %all-to-all-start.2 = ((bf16[8,16,640]{2,1,0:T(8,128)(2,1)}), bf16[8,16,640]{2,1,0:T(8,128)(2,1)S(1)}, u32[]{:S(2)}, u32[]{:S(2)}) async-start(bf16[8,16,640]{2,1,0:T(8,128)(2,1)} %bitcast.7), calls=%async_computation.2 | async-start | bytes 327680 | tf_op jit(solution)/shard_map/all_to_all | solution.py:428
  124.1 2.1 collective-permute-done.26
  128.1 4.6 %all-to-all-done.2.got_ref = bf16[8,16,640]{2,1,0:T(8,128)(2,1)S(1)} async-done(((bf16[8,16,640]{2,1,0:T(8,128)(2,1)}), bf16[8,16,640]{2,1,0:T(8,128)(2,1)S(1)}, u32[]{:S(2)}, u32[]{:S(2)}) %all-to-all-start.2) | async-done | bytes 163872 | tf_op jit(solution)/shard_map/all_to_all | solution.py:428
  132.7 2.0 collective-permute-start.29
  134.7 5.2 %attend.4 = bf16[8,16,512]{2,1,0:T(8,128)(2,1)} custom-call(s32[8]{0:T(128)} %copy-done.5, s32[2,256]{1,0:T(2,128)} %copy-done.9, bf16[8,16,640]{2,1,0:T(8,128)(2,1)} %copy-done.14, f32[256,128]{1,0:T(8,128)} %get-tuple-element.208.cosine_ref, f32[256,128]{1,0:T(8,128)} %get-tuple-element.209.sine_ref, bf16[2,32,64,1024]{3,2,1,0:T(8,128)(2,1)} %own_ref.7, ...), custom_call_target="tpu_custom_call" | custom-call | flops 100000000 | bytes 2097152 | tf_op jit(solution)/shard_map/attend/pallas_call | solution.py:320
  142.1 3.4 %all-to-all-start.3 = ((bf16[8,16,512]{2,1,0:T(8,128)(2,1)}), bf16[8,16,512]{2,1,0:T(8,128)(2,1)S(1)}, u32[]{:S(2)}, u32[]{:S(2)}) async-start(bf16[8,16,512]{2,1,0:T(8,128)(2,1)} %attend.4), calls=%async_computation.3 | async-start | bytes 262144 | tf_op jit(solution)/shard_map/all_to_all | solution.py:439
  145.4 2.1 collective-permute-done.30.refs_3_
  147.6 2.2 collective-permute-start.33
  149.8 3.5 %all-to-all-done.3 = bf16[8,16,512]{2,1,0:T(8,128)(2,1)S(1)} async-done(((bf16[8,16,512]{2,1,0:T(8,128)(2,1)}), bf16[8,16,512]{2,1,0:T(8,128)(2,1)S(1)}, u32[]{:S(2)}, u32[]{:S(2)}) %all-to-all-start.3) | async-done | bytes 131104 | tf_op jit(solution)/shard_map/all_to_all | solution.py:439
  153.3 4.4 %output.4 = (bf16[128,512]{1,0:T(8,128)(2,1)S(1)}, bf16[128,512]{1,0:T(8,128)(2,1)S(1)}, bf16[128,1024]{1,0:T(8,128)(2,1)S(1)}, bf16[128,1024]{1,0:T(8,128)(2,1)...) custom-call(s32[8]{0:T(128)S(1)} %copy-done.7, ...), custom_call_target="tpu_custom_call" | custom-call | flops 1073741824 | bytes 8388608 | tf_op jit(solution)/shard_map/output/pallas_call | solution.py:359
  158.4 4.0 %project.12 = (f32[128,512]{1,0:T(8,128)S(1)}, f32[128,128]{1,0:T(8,128)S(1)}, f32[128,128]{1,0:T(8,128)S(1)}) custom-call(s32[8]{0:T(128)S(1)} %copy-done.7, bf16[128,1024]{1,0:T(8,128)(2,1)S(1)} %add_convert_fusion.10.refs_0_, bf16[128,1024]{1,0:T(8,128)(2,1)S(1)} %collective-permute-done.28.refs_1_, ...), custom_call_target="tpu_custom_call" | custom-call | flops 838860800 | bytes 6553600 | tf_op jit(solution)/shard_map/project/pallas_call | solution.py:238
  164.6 2.9 %collective-permute-done.34.refs_2_ = bf16[128,512]{1,0:T(8,128)(2,1)S(1)} collective-permute-done((bf16[128,512]{1,0:T(8,128)(2,1)S(1)}, bf16[128,512]{1,0:T(8,128)(2,1)S(1)}, u32[]{:S(2)}, u32[]{:S(2)}) %collective-permute-start.34) | collective-permute-done | bytes 131104 | tf_op jit(solution)/shard_map/ppermute | solution.py:386
  169.7 3.8 %project.13 = bf16[128,640]{1,0:T(8,128)(2,1)} custom-call(s32[8]{0:T(128)S(1)} %copy-done.7, bf16[128,1024]{1,0:T(8,128)(2,1)S(1)} %collective-permute-done.32.refs_0_, bf16[128,1024]{1,0:T(8,128)(2,1)S(1)} %collective-permute-done.33.refs_1_, bf16[128,512]{1,0:T(8,128)(2,1)S(1)} %collective-permute-done.34.refs_2_, ...), custom_call_target="tpu_custom_call" | custom-call | flops 503316480 | bytes 3932160 | tf_op jit(solution)/shard_map/project/pallas_call | solution.py:238
  175.8 4.9 %all-to-all-start.4 = ((bf16[8,16,640]{2,1,0:T(8,128)(2,1)}), bf16[8,16,640]{2,1,0:T(8,128)(2,1)S(1)}, u32[]{:S(2)}, u32[]{:S(2)}) async-start(bf16[8,16,640]{2,1,0:T(8,128)(2,1)} %bitcast.9), calls=%async_computation.4 | async-start | bytes 327680 | tf_op jit(solution)/shard_map/all_to_all | solution.py:428
  181.7 2.6 %collective-permute-done.39 = bf16[128,1024]{1,0:T(8,128)(2,1)S(1)} collective-permute-done((bf16[128,1024]{1,0:T(8,128)(2,1)S(1)}, bf16[128,1024]{1,0:T(8,128)(2,1)S(1)}, u32[]{:S(2)}, u32[]{:S(2)}) %collective-permute-start.39) | collective-permute-done | bytes 262176 | tf_op jit(solution)/shard_map/ppermute | solution.py:386
  184.4 4.9 %all-to-all-done.4.got_ref = bf16[8,16,640]{2,1,0:T(8,128)(2,1)S(1)} async-done(((bf16[8,16,640]{2,1,0:T(8,128)(2,1)}), bf16[8,16,640]{2,1,0:T(8,128)(2,1)S(1)}, u32[]{:S(2)}, u32[]{:S(2)}) %all-to-all-start.4) | async-done | bytes 163872 | tf_op jit(solution)/shard_map/all_to_all | solution.py:428
  189.3 2.0 collective-permute-start.41
  191.4 5.2 %attend.5 = bf16[8,16,512]{2,1,0:T(8,128)(2,1)} custom-call(s32[8]{0:T(128)} %copy-done.5, s32[2,256]{1,0:T(2,128)} %copy-done.9, bf16[8,16,640]{2,1,0:T(8,128)(2,1)} %copy-done.13, f32[256,128]{1,0:T(8,128)} %get-tuple-element.208.cosine_ref, f32[256,128]{1,0:T(8,128)} %get-tuple-element.209.sine_ref, bf16[2,32,64,1024]{3,2,1,0:T(8,128)(2,1)} %own_ref.7, ...), custom_call_target="tpu_custom_call" | custom-call | flops 100000000 | bytes 2097152 | tf_op jit(solution)/shard_map/attend/pallas_call | solution.py:320
  196.6 3.6 %all-to-all-start.5 = ((bf16[8,16,512]{2,1,0:T(8,128)(2,1)}), bf16[8,16,512]{2,1,0:T(8,128)(2,1)S(1)}, u32[]{:S(2)}, u32[]{:S(2)}) async-start(bf16[8,16,512]{2,1,0:T(8,128)(2,1)} %attend.5), calls=%async_computation.5 | async-start | bytes 262144 | tf_op jit(solution)/shard_map/all_to_all | solution.py:439
  200.4 7.0 %all-to-all-done.5 = bf16[8,16,512]{2,1,0:T(8,128)(2,1)S(1)} async-done(((bf16[8,16,512]{2,1,0:T(8,128)(2,1)}), bf16[8,16,512]{2,1,0:T(8,128)(2,1)S(1)}, u32[]{:S(2)}, u32[]{:S(2)}) %all-to-all-start.5) | async-done | bytes 131104 | tf_op jit(solution)/shard_map/all_to_all | solution.py:439
  209.4 4.4 %output.5 = (bf16[128,512]{1,0:T(8,128)(2,1)S(1)}, bf16[128,512]{1,0:T(8,128)(2,1)S(1)}, bf16[128,1024]{1,0:T(8,128)(2,1)S(1)}, bf16[128,1024]{1,0:T(8,128)(2,1)...) custom-call(s32[8]{0:T(128)S(1)} %copy-done.8, ...), custom_call_target="tpu_custom_call" | custom-call | flops 1073741824 | bytes 8388608 | tf_op jit(solution)/shard_map/output/pallas_call | solution.py:359
  216.0 2.9 %collective-permute-done.44 = bf16[128,512]{1,0:T(8,128)(2,1)S(1)} collective-permute-done((bf16[128,512]{1,0:T(8,128)(2,1)S(1)}, bf16[128,512]{1,0:T(8,128)(2,1)S(1)}, u32[]{:S(2)}, u32[]{:S(2)}) %collective-permute-start.44) | collective-permute-done | bytes 131104 | tf_op jit(solution)/shard_map/ppermute | solution.py:386
  221.8 4.3 %collective-permute-done.46 = bf16[128,1024]{1,0:T(8,128)(2,1)S(1)} collective-permute-done((bf16[128,1024]{1,0:T(8,128)(2,1)S(1)}, bf16[128,1024]{1,0:T(8,128)(2,1)S(1)}, u32[]{:S(2)}, u32[]{:S(2)}) %collective-permute-start.46) | collective-permute-done | bytes 262176 | tf_op jit(solution)/shard_map/ppermute | solution.py:386
  229.0 4.3 %collective-permute-done.48 = bf16[128,1024]{1,0:T(8,128)(2,1)S(1)} collective-permute-done((bf16[128,1024]{1,0:T(8,128)(2,1)S(1)}, bf16[128,1024]{1,0:T(8,128)(2,1)S(1)}, u32[]{:S(2)}, u32[]{:S(2)}) %collective-permute-start.48) | collective-permute-done | bytes 262176 | tf_op jit(solution)/shard_map/ppermute | solution.py:386
  236.9 4.1 %collective-permute-done.50 = bf16[128,1024]{1,0:T(8,128)(2,1)S(1)} collective-permute-done((bf16[128,1024]{1,0:T(8,128)(2,1)S(1)}, bf16[128,1024]{1,0:T(8,128)(2,1)S(1)}, u32[]{:S(2)}, u32[]{:S(2)}) %collective-permute-start.50) | collective-permute-done | bytes 262176 | tf_op jit(solution)/shard_map/ppermute | solution.py:386
  (162 shorter events, 63.4 us)
Async XLA Ops:
  5.2 60.0 %collective-permute-start.15 = (bf16[2,32,64,1024]{3,2,1,0:T(8,128)(2,1)}, bf16[2,32,64,1024]{3,2,1,0:T(8,128)(2,1)}, u32[]{:S(2)}, u32[]{:S(2)}) collective-permute-start(bf16[2,32,64,1024]{3,2,1,0:T(8,128)(2,1)} %own_ref.7), channel_id=1, source_target_pairs={{0,8},{8,0},{1,9},{9,1},{2,10},{10,2},{3,11},{11,3},{4,12},{12,4},... | collective-permute-start | bytes 25165832 | tf_op jit(solution)/shard_map/ppermute | solution.py:491
  5.7 9.5 %collective-permute-start.3 = (bf16[128,1024]{1,0:T(8,128)(2,1)S(1)}, bf16[128,1024]{1,0:T(8,128)(2,1)S(1)}, u32[]{:S(2)}, u32[]{:S(2)}) collective-permute-start(bf16[128,1024]{1,0:T(8,128)(2,1)S(1)} %get-tuple-element.107.refs_0_), channel_id=1, source_target_pairs={{0,2},{2,4},{4,6},{6,7},{7,5},{5,3},{3,1},{1,0},{8,10},{10,12},{12... | collective-permute-start | bytes 786440 | tf_op jit(solution)/shard_map/ppermute | solution.py:386
  8.4 8.3 %collective-permute-start.4 = (bf16[128,1024]{1,0:T(8,128)(2,1)S(1)}, bf16[128,1024]{1,0:T(8,128)(2,1)S(1)}, u32[]{:S(2)}, u32[]{:S(2)}) collective-permute-start(bf16[128,1024]{1,0:T(8,128)(2,1)S(1)} %get-tuple-element.107.refs_0_), channel_id=1, source_target_pairs={{0,1},{2,0},{4,2},{6,4},{7,6},{5,7},{3,5},{1,3},{8,9},{10,8},{12,1... | collective-permute-start | bytes 786440 | tf_op jit(solution)/shard_map/ppermute | solution.py:386
  16.7 7.4 %collective-permute-start.5 = (bf16[128,1024]{1,0:T(8,128)(2,1)S(1)}, bf16[128,1024]{1,0:T(8,128)(2,1)S(1)}, u32[]{:S(2)}, u32[]{:S(2)}) collective-permute-start(bf16[128,1024]{1,0:T(8,128)(2,1)S(1)} %collective-permute-done.3.refs_1_), channel_id=1, source_target_pairs={{0,2},{2,4},{4,6},{6,7},{7,5},{5,3},{3,1},{1,0},{8,10},{10,12},{12... | collective-permute-start | bytes 786440 | tf_op jit(solution)/shard_map/ppermute | solution.py:386
  18.3 7.2 %collective-permute-start.6 = (bf16[128,1024]{1,0:T(8,128)(2,1)S(1)}, bf16[128,1024]{1,0:T(8,128)(2,1)S(1)}, u32[]{:S(2)}, u32[]{:S(2)}) collective-permute-start(bf16[128,1024]{1,0:T(8,128)(2,1)S(1)} %collective-permute-done.4.refs_2_), channel_id=1, source_target_pairs={{0,1},{2,0},{4,2},{6,4},{7,6},{5,7},{3,5},{1,3},{8,9},{10,8},{12,1... | collective-permute-start | bytes 786440 | tf_op jit(solution)/shard_map/ppermute | solution.py:386
  25.4 6.4 %collective-permute-start.7 = (bf16[128,1024]{1,0:T(8,128)(2,1)S(1)}, bf16[128,1024]{1,0:T(8,128)(2,1)S(1)}, u32[]{:S(2)}, u32[]{:S(2)}) collective-permute-start(bf16[128,1024]{1,0:T(8,128)(2,1)S(1)} %collective-permute-done.5.refs_0_), channel_id=1, source_target_pairs={{0,2},{2,4},{4,6},{6,7},{7,5},{5,3},{3,1},{1,0},{8,10},{10,12},{12... | collective-permute-start | bytes 786440 | tf_op jit(solution)/shard_map/ppermute | solution.py:386
  27.0 6.4 %collective-permute-start.8 = (bf16[128,1024]{1,0:T(8,128)(2,1)S(1)}, bf16[128,1024]{1,0:T(8,128)(2,1)S(1)}, u32[]{:S(2)}, u32[]{:S(2)}) collective-permute-start(bf16[128,1024]{1,0:T(8,128)(2,1)S(1)} %collective-permute-done.6.refs_1_), channel_id=1, source_target_pairs={{0,1},{2,0},{4,2},{6,4},{7,6},{5,7},{3,5},{1,3},{8,9},{10,8},{12,1... | collective-permute-start | bytes 786440 | tf_op jit(solution)/shard_map/ppermute | solution.py:386
  33.4 5.4 %collective-permute-start.9 = (bf16[128,512]{1,0:T(8,128)(2,1)S(1)}, bf16[128,512]{1,0:T(8,128)(2,1)S(1)}, u32[]{:S(2)}, u32[]{:S(2)}) collective-permute-start(bf16[128,512]{1,0:T(8,128)(2,1)S(1)} %slice.120), channel_id=1, source_target_pairs={{0,2},{2,4},{4,6},{6,7},{7,5},{5,3},{3,1},{1,0},{8,10},{10,12},{12... | collective-permute-start | bytes 393224 | tf_op jit(solution)/shard_map/ppermute | solution.py:386
  35.0 6.4 %collective-permute-start.10 = (bf16[128,512]{1,0:T(8,128)(2,1)S(1)}, bf16[128,512]{1,0:T(8,128)(2,1)S(1)}, u32[]{:S(2)}, u32[]{:S(2)}) collective-permute-start(bf16[128,512]{1,0:T(8,128)(2,1)S(1)} %slice.121), channel_id=1, source_target_pairs={{0,1},{2,0},{4,2},{6,4},{7,6},{5,7},{3,5},{1,3},{8,9},{10,8},{12,1... | collective-permute-start | bytes 393224 | tf_op jit(solution)/shard_map/ppermute | solution.py:386
  41.3 9.9 %collective-permute-start.11 = (bf16[128,1024]{1,0:T(8,128)(2,1)S(1)}, bf16[128,1024]{1,0:T(8,128)(2,1)S(1)}, u32[]{:S(2)}, u32[]{:S(2)}) collective-permute-start(bf16[128,1024]{1,0:T(8,128)(2,1)S(1)} %get-tuple-element.123.refs_0_), channel_id=1, source_target_pairs={{0,2},{2,4},{4,6},{6,7},{7,5},{5,3},{3,1},{1,0},{8,10},{10,12},{12... | collective-permute-start | bytes 786440 | tf_op jit(solution)/shard_map/ppermute | solution.py:386
  41.9 9.3 %collective-permute-start.12 = (bf16[128,1024]{1,0:T(8,128)(2,1)S(1)}, bf16[128,1024]{1,0:T(8,128)(2,1)S(1)}, u32[]{:S(2)}, u32[]{:S(2)}) collective-permute-start(bf16[128,1024]{1,0:T(8,128)(2,1)S(1)} %get-tuple-element.123.refs_0_), channel_id=1, source_target_pairs={{0,1},{2,0},{4,2},{6,4},{7,6},{5,7},{3,5},{1,3},{8,9},{10,8},{12,1... | collective-permute-start | bytes 786440 | tf_op jit(solution)/shard_map/ppermute | solution.py:386
  47.8 12.0 %all-to-all-start = ((bf16[8,16,640]{2,1,0:T(8,128)(2,1)}), bf16[8,16,640]{2,1,0:T(8,128)(2,1)S(1)}, u32[]{:S(2)}, u32[]{:S(2)}) async-start(bf16[8,16,640]{2,1,0:T(8,128)(2,1)} %bitcast.5), calls=%async_computation | async-start | bytes 327680 | tf_op jit(solution)/shard_map/all_to_all | solution.py:428
  51.3 10.1 %collective-permute-start.13 = (bf16[128,1024]{1,0:T(8,128)(2,1)S(1)}, bf16[128,1024]{1,0:T(8,128)(2,1)S(1)}, u32[]{:S(2)}, u32[]{:S(2)}) collective-permute-start(bf16[128,1024]{1,0:T(8,128)(2,1)S(1)} %collective-permute-done.11.refs_1_), channel_id=1, source_target_pairs={{0,2},{2,4},{4,6},{6,7},{7,5},{5,3},{3,1},{1,0},{8,10},{10,12},{12... | collective-permute-start | bytes 786440 | tf_op jit(solution)/shard_map/ppermute | solution.py:386
  53.2 9.2 %collective-permute-start.14 = (bf16[128,1024]{1,0:T(8,128)(2,1)S(1)}, bf16[128,1024]{1,0:T(8,128)(2,1)S(1)}, u32[]{:S(2)}, u32[]{:S(2)}) collective-permute-start(bf16[128,1024]{1,0:T(8,128)(2,1)S(1)} %collective-permute-done.12.refs_2_), channel_id=1, source_target_pairs={{0,1},{2,0},{4,2},{6,4},{7,6},{5,7},{3,5},{1,3},{8,9},{10,8},{12,1... | collective-permute-start | bytes 786440 | tf_op jit(solution)/shard_map/ppermute | solution.py:386
  62.4 12.2 %collective-permute-start.16 = (bf16[128,1024]{1,0:T(8,128)(2,1)S(1)}, bf16[128,1024]{1,0:T(8,128)(2,1)S(1)}, u32[]{:S(2)}, u32[]{:S(2)}) collective-permute-start(bf16[128,1024]{1,0:T(8,128)(2,1)S(1)} %collective-permute-done.13.refs_3_), channel_id=1, source_target_pairs={{0,2},{2,4},{4,6},{6,7},{7,5},{5,3},{3,1},{1,0},{8,10},{10,12},{12... | collective-permute-start | bytes 786440 | tf_op jit(solution)/shard_map/ppermute | solution.py:386
  63.8 10.8 %collective-permute-start.17 = (bf16[128,1024]{1,0:T(8,128)(2,1)S(1)}, bf16[128,1024]{1,0:T(8,128)(2,1)S(1)}, u32[]{:S(2)}, u32[]{:S(2)}) collective-permute-start(bf16[128,1024]{1,0:T(8,128)(2,1)S(1)} %collective-permute-done.14.refs_4_), channel_id=1, source_target_pairs={{0,1},{2,0},{4,2},{6,4},{7,6},{5,7},{3,5},{1,3},{8,9},{10,8},{12,1... | collective-permute-start | bytes 786440 | tf_op jit(solution)/shard_map/ppermute | solution.py:386
  70.5 11.4 %all-to-all-start.1 = ((bf16[8,16,512]{2,1,0:T(8,128)(2,1)}), bf16[8,16,512]{2,1,0:T(8,128)(2,1)S(1)}, u32[]{:S(2)}, u32[]{:S(2)}) async-start(bf16[8,16,512]{2,1,0:T(8,128)(2,1)} %attend.3), calls=%async_computation.1 | async-start | bytes 262144 | tf_op jit(solution)/shard_map/all_to_all | solution.py:439
  81.9 10.5 %collective-permute-start.18 = (bf16[128,512]{1,0:T(8,128)(2,1)S(1)}, bf16[128,512]{1,0:T(8,128)(2,1)S(1)}, u32[]{:S(2)}, u32[]{:S(2)}) collective-permute-start(bf16[128,512]{1,0:T(8,128)(2,1)S(1)} %slice.126), channel_id=1, source_target_pairs={{0,2},{2,4},{4,6},{6,7},{7,5},{5,3},{3,1},{1,0},{8,10},{10,12},{12... | collective-permute-start | bytes 393224 | tf_op jit(solution)/shard_map/ppermute | solution.py:386
  81.9 10.5 %collective-permute-start.19 = (bf16[128,512]{1,0:T(8,128)(2,1)S(1)}, bf16[128,512]{1,0:T(8,128)(2,1)S(1)}, u32[]{:S(2)}, u32[]{:S(2)}) collective-permute-start(bf16[128,512]{1,0:T(8,128)(2,1)S(1)} %slice.127), channel_id=1, source_target_pairs={{0,1},{2,0},{4,2},{6,4},{7,6},{5,7},{3,5},{1,3},{8,9},{10,8},{12,1... | collective-permute-start | bytes 393224 | tf_op jit(solution)/shard_map/ppermute | solution.py:386
  97.6 8.2 %collective-permute-start.22 = (bf16[128,1024]{1,0:T(8,128)(2,1)S(1)}, bf16[128,1024]{1,0:T(8,128)(2,1)S(1)}, u32[]{:S(2)}, u32[]{:S(2)}) collective-permute-start(bf16[128,1024]{1,0:T(8,128)(2,1)S(1)} %pad_maximum_fusion), channel_id=1, source_target_pairs={{0,2},{2,4},{4,6},{6,7},{7,5},{5,3},{3,1},{1,0},{8,10},{10,12},{12... | collective-permute-start | bytes 786440 | tf_op jit(solution)/shard_map/ppermute | solution.py:386
  98.6 7.3 %collective-permute-start.23 = (bf16[128,1024]{1,0:T(8,128)(2,1)S(1)}, bf16[128,1024]{1,0:T(8,128)(2,1)S(1)}, u32[]{:S(2)}, u32[]{:S(2)}) collective-permute-start(bf16[128,1024]{1,0:T(8,128)(2,1)S(1)} %pad_maximum_fusion.1), channel_id=1, source_target_pairs={{0,1},{2,0},{4,2},{6,4},{7,6},{5,7},{3,5},{1,3},{8,9},{10,8},{12,1... | collective-permute-start | bytes 786440 | tf_op jit(solution)/shard_map/ppermute | solution.py:386
  105.9 7.5 %collective-permute-start.24 = (bf16[128,1024]{1,0:T(8,128)(2,1)S(1)}, bf16[128,1024]{1,0:T(8,128)(2,1)S(1)}, u32[]{:S(2)}, u32[]{:S(2)}) collective-permute-start(bf16[128,1024]{1,0:T(8,128)(2,1)S(1)} %add_convert_fusion.14), channel_id=1, source_target_pairs={{0,2},{2,4},{4,6},{6,7},{7,5},{5,3},{3,1},{1,0},{8,10},{10,12},{12... | collective-permute-start | bytes 786440 | tf_op jit(solution)/shard_map/ppermute | solution.py:386
  108.2 8.0 %collective-permute-start.25 = (bf16[128,1024]{1,0:T(8,128)(2,1)S(1)}, bf16[128,1024]{1,0:T(8,128)(2,1)S(1)}, u32[]{:S(2)}, u32[]{:S(2)}) collective-permute-start(bf16[128,1024]{1,0:T(8,128)(2,1)S(1)} %add_convert_fusion.13), channel_id=1, source_target_pairs={{0,1},{2,0},{4,2},{6,4},{7,6},{5,7},{3,5},{1,3},{8,9},{10,8},{12,1... | collective-permute-start | bytes 786440 | tf_op jit(solution)/shard_map/ppermute | solution.py:386
  116.3 9.8 %collective-permute-start.26 = (bf16[128,1024]{1,0:T(8,128)(2,1)S(1)}, bf16[128,1024]{1,0:T(8,128)(2,1)S(1)}, u32[]{:S(2)}, u32[]{:S(2)}) collective-permute-start(bf16[128,1024]{1,0:T(8,128)(2,1)S(1)} %add_convert_fusion.12), channel_id=1, source_target_pairs={{0,2},{2,4},{4,6},{6,7},{7,5},{5,3},{3,1},{1,0},{8,10},{10,12},{12... | collective-permute-start | bytes 786440 | tf_op jit(solution)/shard_map/ppermute | solution.py:386
  119.4 8.4 %collective-permute-start.27 = (bf16[128,1024]{1,0:T(8,128)(2,1)S(1)}, bf16[128,1024]{1,0:T(8,128)(2,1)S(1)}, u32[]{:S(2)}, u32[]{:S(2)}) collective-permute-start(bf16[128,1024]{1,0:T(8,128)(2,1)S(1)} %add_convert_fusion.11), channel_id=1, source_target_pairs={{0,1},{2,0},{4,2},{6,4},{7,6},{5,7},{3,5},{1,3},{8,9},{10,8},{12,1... | collective-permute-start | bytes 786440 | tf_op jit(solution)/shard_map/ppermute | solution.py:386
  119.4 13.2 %all-to-all-start.2 = ((bf16[8,16,640]{2,1,0:T(8,128)(2,1)}), bf16[8,16,640]{2,1,0:T(8,128)(2,1)S(1)}, u32[]{:S(2)}, u32[]{:S(2)}) async-start(bf16[8,16,640]{2,1,0:T(8,128)(2,1)} %bitcast.7), calls=%async_computation.2 | async-start | bytes 327680 | tf_op jit(solution)/shard_map/all_to_all | solution.py:428
  132.7 7.3 %collective-permute-start.28 = (bf16[128,1024]{1,0:T(8,128)(2,1)S(1)}, bf16[128,1024]{1,0:T(8,128)(2,1)S(1)}, u32[]{:S(2)}, u32[]{:S(2)}) collective-permute-start(bf16[128,1024]{1,0:T(8,128)(2,1)S(1)} %add_convert_fusion.10.refs_0_), channel_id=1, source_target_pairs={{0,2},{2,4},{4,6},{6,7},{7,5},{5,3},{3,1},{1,0},{8,10},{10,12},{12... | collective-permute-start | bytes 786440 | tf_op jit(solution)/shard_map/ppermute | solution.py:386
  132.7 7.3 %collective-permute-start.29 = (bf16[128,1024]{1,0:T(8,128)(2,1)S(1)}, bf16[128,1024]{1,0:T(8,128)(2,1)S(1)}, u32[]{:S(2)}, u32[]{:S(2)}) collective-permute-start(bf16[128,1024]{1,0:T(8,128)(2,1)S(1)} %add_convert_fusion.10.refs_0_), channel_id=1, source_target_pairs={{0,1},{2,0},{4,2},{6,4},{7,6},{5,7},{3,5},{1,3},{8,9},{10,8},{12,1... | collective-permute-start | bytes 786440 | tf_op jit(solution)/shard_map/ppermute | solution.py:386
  140.0 7.6 %collective-permute-start.30 = (bf16[128,1024]{1,0:T(8,128)(2,1)S(1)}, bf16[128,1024]{1,0:T(8,128)(2,1)S(1)}, u32[]{:S(2)}, u32[]{:S(2)}) collective-permute-start(bf16[128,1024]{1,0:T(8,128)(2,1)S(1)} %collective-permute-done.28.refs_1_), channel_id=1, source_target_pairs={{0,2},{2,4},{4,6},{6,7},{7,5},{5,3},{3,1},{1,0},{8,10},{10,12},{12... | collective-permute-start | bytes 786440 | tf_op jit(solution)/shard_map/ppermute | solution.py:386
  140.0 7.5 %collective-permute-start.31 = (bf16[128,1024]{1,0:T(8,128)(2,1)S(1)}, bf16[128,1024]{1,0:T(8,128)(2,1)S(1)}, u32[]{:S(2)}, u32[]{:S(2)}) collective-permute-start(bf16[128,1024]{1,0:T(8,128)(2,1)S(1)} %collective-permute-done.29.refs_2_), channel_id=1, source_target_pairs={{0,1},{2,0},{4,2},{6,4},{7,6},{5,7},{3,5},{1,3},{8,9},{10,8},{12,1... | collective-permute-start | bytes 786440 | tf_op jit(solution)/shard_map/ppermute | solution.py:386
  142.1 11.2 %all-to-all-start.3 = ((bf16[8,16,512]{2,1,0:T(8,128)(2,1)}), bf16[8,16,512]{2,1,0:T(8,128)(2,1)S(1)}, u32[]{:S(2)}, u32[]{:S(2)}) async-start(bf16[8,16,512]{2,1,0:T(8,128)(2,1)} %attend.4), calls=%async_computation.3 | async-start | bytes 262144 | tf_op jit(solution)/shard_map/all_to_all | solution.py:439
  147.6 14.9 %collective-permute-start.32 = (bf16[128,1024]{1,0:T(8,128)(2,1)S(1)}, bf16[128,1024]{1,0:T(8,128)(2,1)S(1)}, u32[]{:S(2)}, u32[]{:S(2)}) collective-permute-start(bf16[128,1024]{1,0:T(8,128)(2,1)S(1)} %collective-permute-done.30.refs_3_), channel_id=1, source_target_pairs={{0,2},{2,4},{4,6},{6,7},{7,5},{5,3},{3,1},{1,0},{8,10},{10,12},{12... | collective-permute-start | bytes 786440 | tf_op jit(solution)/shard_map/ppermute | solution.py:386
  147.6 14.9 %collective-permute-start.33 = (bf16[128,1024]{1,0:T(8,128)(2,1)S(1)}, bf16[128,1024]{1,0:T(8,128)(2,1)S(1)}, u32[]{:S(2)}, u32[]{:S(2)}) collective-permute-start(bf16[128,1024]{1,0:T(8,128)(2,1)S(1)} %collective-permute-done.31.refs_4_), channel_id=1, source_target_pairs={{0,1},{2,0},{4,2},{6,4},{7,6},{5,7},{3,5},{1,3},{8,9},{10,8},{12,1... | collective-permute-start | bytes 786440 | tf_op jit(solution)/shard_map/ppermute | solution.py:386
  167.6 5.9 %collective-permute-start.36 = (bf16[128,512]{1,0:T(8,128)(2,1)S(1)}, bf16[128,512]{1,0:T(8,128)(2,1)S(1)}, u32[]{:S(2)}, u32[]{:S(2)}) collective-permute-start(bf16[128,512]{1,0:T(8,128)(2,1)S(1)} %get-tuple-element.174), channel_id=1, source_target_pairs={{0,2},{2,4},{4,6},{6,7},{7,5},{5,3},{3,1},{1,0},{8,10},{10,12},{12... | collective-permute-start | bytes 393224 | tf_op jit(solution)/shard_map/ppermute | solution.py:386
  173.8 7.9 %collective-permute-start.38 = (bf16[128,1024]{1,0:T(8,128)(2,1)S(1)}, bf16[128,1024]{1,0:T(8,128)(2,1)S(1)}, u32[]{:S(2)}, u32[]{:S(2)}) collective-permute-start(bf16[128,1024]{1,0:T(8,128)(2,1)S(1)} %pad_maximum_fusion.2), channel_id=1, source_target_pairs={{0,2},{2,4},{4,6},{6,7},{7,5},{5,3},{3,1},{1,0},{8,10},{10,12},{12... | collective-permute-start | bytes 786440 | tf_op jit(solution)/shard_map/ppermute | solution.py:386
  175.2 9.1 %collective-permute-start.39 = (bf16[128,1024]{1,0:T(8,128)(2,1)S(1)}, bf16[128,1024]{1,0:T(8,128)(2,1)S(1)}, u32[]{:S(2)}, u32[]{:S(2)}) collective-permute-start(bf16[128,1024]{1,0:T(8,128)(2,1)S(1)} %pad_maximum_fusion.3), channel_id=1, source_target_pairs={{0,1},{2,0},{4,2},{6,4},{7,6},{5,7},{3,5},{1,3},{8,9},{10,8},{12,1... | collective-permute-start | bytes 786440 | tf_op jit(solution)/shard_map/ppermute | solution.py:386
  175.8 13.5 %all-to-all-start.4 = ((bf16[8,16,640]{2,1,0:T(8,128)(2,1)}), bf16[8,16,640]{2,1,0:T(8,128)(2,1)S(1)}, u32[]{:S(2)}, u32[]{:S(2)}) async-start(bf16[8,16,640]{2,1,0:T(8,128)(2,1)} %bitcast.9), calls=%async_computation.4 | async-start | bytes 327680 | tf_op jit(solution)/shard_map/all_to_all | solution.py:428
  189.3 10.9 %collective-permute-start.40 = (bf16[128,1024]{1,0:T(8,128)(2,1)S(1)}, bf16[128,1024]{1,0:T(8,128)(2,1)S(1)}, u32[]{:S(2)}, u32[]{:S(2)}) collective-permute-start(bf16[128,1024]{1,0:T(8,128)(2,1)S(1)} %add_convert_fusion.9), channel_id=1, source_target_pairs={{0,2},{2,4},{4,6},{6,7},{7,5},{5,3},{3,1},{1,0},{8,10},{10,12},{12... | collective-permute-start | bytes 786440 | tf_op jit(solution)/shard_map/ppermute | solution.py:386
  189.3 11.0 %collective-permute-start.41 = (bf16[128,1024]{1,0:T(8,128)(2,1)S(1)}, bf16[128,1024]{1,0:T(8,128)(2,1)S(1)}, u32[]{:S(2)}, u32[]{:S(2)}) collective-permute-start(bf16[128,1024]{1,0:T(8,128)(2,1)S(1)} %add_convert_fusion.8), channel_id=1, source_target_pairs={{0,1},{2,0},{4,2},{6,4},{7,6},{5,7},{3,5},{1,3},{8,9},{10,8},{12,1... | collective-permute-start | bytes 786440 | tf_op jit(solution)/shard_map/ppermute | solution.py:386
  196.6 10.8 %all-to-all-start.5 = ((bf16[8,16,512]{2,1,0:T(8,128)(2,1)}), bf16[8,16,512]{2,1,0:T(8,128)(2,1)S(1)}, u32[]{:S(2)}, u32[]{:S(2)}) async-start(bf16[8,16,512]{2,1,0:T(8,128)(2,1)} %attend.5), calls=%async_computation.5 | async-start | bytes 262144 | tf_op jit(solution)/shard_map/all_to_all | solution.py:439
  207.4 6.4 %collective-permute-start.42 = (bf16[128,1024]{1,0:T(8,128)(2,1)S(1)}, bf16[128,1024]{1,0:T(8,128)(2,1)S(1)}, u32[]{:S(2)}, u32[]{:S(2)}) collective-permute-start(bf16[128,1024]{1,0:T(8,128)(2,1)S(1)} %add_convert_fusion.7), channel_id=1, source_target_pairs={{0,2},{2,4},{4,6},{6,7},{7,5},{5,3},{3,1},{1,0},{8,10},{10,12},{12... | collective-permute-start | bytes 786440 | tf_op jit(solution)/shard_map/ppermute | solution.py:386
  207.4 6.4 %collective-permute-start.43 = (bf16[128,1024]{1,0:T(8,128)(2,1)S(1)}, bf16[128,1024]{1,0:T(8,128)(2,1)S(1)}, u32[]{:S(2)}, u32[]{:S(2)}) collective-permute-start(bf16[128,1024]{1,0:T(8,128)(2,1)S(1)} %add_convert_fusion.6), channel_id=1, source_target_pairs={{0,1},{2,0},{4,2},{6,4},{7,6},{5,7},{3,5},{1,3},{8,9},{10,8},{12,1... | collective-permute-start | bytes 786440 | tf_op jit(solution)/shard_map/ppermute | solution.py:386
  219.7 6.4 %collective-permute-start.46 = (bf16[128,1024]{1,0:T(8,128)(2,1)S(1)}, bf16[128,1024]{1,0:T(8,128)(2,1)S(1)}, u32[]{:S(2)}, u32[]{:S(2)}) collective-permute-start(bf16[128,1024]{1,0:T(8,128)(2,1)S(1)} %pad_maximum_fusion.4), channel_id=1, source_target_pairs={{0,2},{2,4},{4,6},{6,7},{7,5},{5,3},{3,1},{1,0},{8,10},{10,12},{12... | collective-permute-start | bytes 786440 | tf_op jit(solution)/shard_map/ppermute | solution.py:386
  220.5 6.4 %collective-permute-start.47 = (bf16[128,1024]{1,0:T(8,128)(2,1)S(1)}, bf16[128,1024]{1,0:T(8,128)(2,1)S(1)}, u32[]{:S(2)}, u32[]{:S(2)}) collective-permute-start(bf16[128,1024]{1,0:T(8,128)(2,1)S(1)} %pad_maximum_fusion.5), channel_id=1, source_target_pairs={{0,1},{2,0},{4,2},{6,4},{7,6},{5,7},{3,5},{1,3},{8,9},{10,8},{12,1... | collective-permute-start | bytes 786440 | tf_op jit(solution)/shard_map/ppermute | solution.py:386
  226.9 6.4 %collective-permute-start.48 = (bf16[128,1024]{1,0:T(8,128)(2,1)S(1)}, bf16[128,1024]{1,0:T(8,128)(2,1)S(1)}, u32[]{:S(2)}, u32[]{:S(2)}) collective-permute-start(bf16[128,1024]{1,0:T(8,128)(2,1)S(1)} %add_convert_fusion.5), channel_id=1, source_target_pairs={{0,2},{2,4},{4,6},{6,7},{7,5},{5,3},{3,1},{1,0},{8,10},{10,12},{12... | collective-permute-start | bytes 786440 | tf_op jit(solution)/shard_map/ppermute | solution.py:386
  228.1 6.4 %collective-permute-start.49 = (bf16[128,1024]{1,0:T(8,128)(2,1)S(1)}, bf16[128,1024]{1,0:T(8,128)(2,1)S(1)}, u32[]{:S(2)}, u32[]{:S(2)}) collective-permute-start(bf16[128,1024]{1,0:T(8,128)(2,1)S(1)} %add_convert_fusion.4), channel_id=1, source_target_pairs={{0,1},{2,0},{4,2},{6,4},{7,6},{5,7},{3,5},{1,3},{8,9},{10,8},{12,1... | collective-permute-start | bytes 786440 | tf_op jit(solution)/shard_map/ppermute | solution.py:386
  234.5 6.4 %collective-permute-start.50 = (bf16[128,1024]{1,0:T(8,128)(2,1)S(1)}, bf16[128,1024]{1,0:T(8,128)(2,1)S(1)}, u32[]{:S(2)}, u32[]{:S(2)}) collective-permute-start(bf16[128,1024]{1,0:T(8,128)(2,1)S(1)} %add_convert_fusion.3), channel_id=1, source_target_pairs={{0,2},{2,4},{4,6},{6,7},{7,5},{5,3},{3,1},{1,0},{8,10},{10,12},{12... | collective-permute-start | bytes 786440 | tf_op jit(solution)/shard_map/ppermute | solution.py:386
  235.5 6.4 %collective-permute-start.51 = (bf16[128,1024]{1,0:T(8,128)(2,1)S(1)}, bf16[128,1024]{1,0:T(8,128)(2,1)S(1)}, u32[]{:S(2)}, u32[]{:S(2)}) collective-permute-start(bf16[128,1024]{1,0:T(8,128)(2,1)S(1)} %add_convert_fusion.2), channel_id=1, source_target_pairs={{0,1},{2,0},{4,2},{6,4},{7,6},{5,7},{3,5},{1,3},{8,9},{10,8},{12,1... | collective-permute-start | bytes 786440 | tf_op jit(solution)/shard_map/ppermute | solution.py:386
  (27 other events, 186.3 us)

commit v3 on v2

--- a/solution.py
+++ b/solution.py
@@ -16,6 +16,7 @@
 NEGATIVE = -1e30
 VMEM_LIMIT = 50 * 1024 * 1024
 ATTEND_LIMIT = 57 * 1024 * 1024
+DEAL_LIMIT = 61 * 1024 * 1024
 
 
 def ring_order(mesh):
@@ -52,8 +53,16 @@
 IN_HBM = pl.BlockSpec(memory_space=pltpu.HBM)
 
 
-def deal_kernel(block_rows, exits_ref, other_exits_ref, spans_ref, other_spans_ref, own_ref, other_ref, first_ref, second_ref, place_ref, span_ref, facts_ref):
+def deal_kernel(block_rows, exits_ref, other_exits_ref, spans_ref, other_spans_ref, own_ref, other_ref, first_ref, second_ref, place_ref, span_ref, facts_ref, *refs):
+    *held, sems = refs
     rows = own_ref.shape[0]
+    copies = []
+    for index, ref in enumerate((exits_ref, other_exits_ref, spans_ref, other_spans_ref, own_ref, other_ref)):
+        copies.append(pltpu.make_async_copy(ref, held[index], sems.at[index]))
+        copies[-1].start()
+    exits_ref, other_exits_ref, spans_ref, other_spans_ref, own_ref, other_ref = held
+    for copy in copies[:4]:
+        copy.wait()
     half = block_rows // 2
     part = rows // 2
     own = (exits_ref[...] == 2).astype(jnp.float32)
@@ -89,6 +98,8 @@
     slots = down.astype(jnp.float32)
     stay = slots == stays_at
     come = slots == comes_to
+    for copy in copies[4:]:
+        copy.wait()
     moved = jnp.dot(stay.astype(jnp.bfloat16), own_ref[...], preferred_element_type=jnp.float32) + jnp.dot(
         come.astype(jnp.bfloat16), other_ref[...], preferred_element_type=jnp.float32
     )
@@ -125,7 +136,10 @@
     return pl.pallas_call(
         functools.partial(deal_kernel, block_rows),
         out_shape=[jax.ShapeDtypeStruct(*s) for s in shapes],
-        compiler_params=params(),
+        in_specs=[IN_HBM] * 6,
+        out_specs=[IN_VMEM] * 5,
+        scratch_shapes=[pltpu.VMEM(v.shape, v.dtype) for v in (*lines, own, other)] + [pltpu.SemaphoreType.DMA((6,))],
+        compiler_params=params(DEAL_LIMIT),
         name="deal",
     )(*lines, own, other)
 
@@ -303,7 +317,7 @@
         scores = jnp.where(valid, scores * scale, NEGATIVE)
         own = jnp.sum(query * jnp.concatenate([new_key] * group, axis=0), axis=1, keepdims=True) * scale
         highest = jnp.maximum(jnp.max(scores, axis=1, keepdims=True), own)
-        weights = jnp.where(valid, jnp.exp(scores - highest), 0.0)
+        weights = jnp.exp(scores - highest)
         own_weight = jnp.exp(own - highest)
         total = jnp.sum(weights, axis=1, keepdims=True) + own_weight
         mixed = jnp.dot(weights.astype(jnp.bfloat16), values, preferred_element_type=jnp.float32)
@@ -378,21 +392,23 @@
         self.blocks = [((share,), 0)]
         self.sums = None
 
-    def hop(self, to_front, to_back, held):
+    def hop(self, to_front, to_back, held, first):
         parts = len(self.ring)
         forward = [(self.ring[i], self.ring[(i + 1) % parts]) for i in range(parts)]
         backward = [(self.ring[i], self.ring[(i - 1) % parts]) for i in range(parts)]
         to_front, to_back = lax.optimization_barrier((to_front, to_back, held))[:2]
         self.last = lax.ppermute(to_front, "tensor", forward), lax.ppermute(to_back, "tensor", backward)
+        if first:
+            self.first_hop = self.last
         return self.last
 
     def gather(self, step, *held):
         width = self.share.shape[1] // 2
         if step < self.half:
-            self.behind, self.ahead = self.hop(self.behind, self.ahead, held)
+            self.behind, self.ahead = self.hop(self.behind, self.ahead, held, step == 1)
             self.blocks += [((self.behind,), -step % len(self.ring)), ((self.ahead,), step)]
         else:
-            halves = self.hop(self.behind[:, :width], self.ahead[:, width:], held)
+            halves = self.hop(self.behind[:, :width], self.ahead[:, width:], held, False)
             self.blocks.append((halves, self.half))
 
     def project(self, places=None, final=False, held=()):
@@ -451,7 +467,7 @@
     def scatter(self, step, *held):
         width = self.share.shape[1] // 2
         if step == 1:
-            self.last = self.hop(*self.halves, held)
+            self.hop(*self.halves, held, True)
             return
         from_back, from_front = (v.astype(jnp.float32) for v in self.last)
         to_front = self.product(self.half + 1 - step)
@@ -462,7 +478,7 @@
         else:
             to_front = to_front + from_back
             to_back = to_back + from_front
-        self.hop(to_front.astype(jnp.bfloat16), to_back.astype(jnp.bfloat16), held)
+        self.hop(to_front.astype(jnp.bfloat16), to_back.astype(jnp.bfloat16), held, False)
 
     def result(self):
         from_back, from_front = (v.astype(jnp.float32) for v in self.last)
@@ -505,46 +521,49 @@
     b = Layer(0, part, ring, table, second, told, weights)
 
     a.gather(1)
-    a.project_ring(steps)
-    b.gather(1, a.last)
+    a.project_ring(steps, cosine, sine)
+    a.project(steps - 1)
+    b.gather(1, a.last, a.sums)
     a.project(final=True)
     a.ask()
     for step in range(2, steps - 1):
         b.gather(step, a.sums)
-    a.attend(b.last)
+    a.attend(b.first_hop)
+    b.gather(steps - 1, a.mixed)
     a.answer()
-    b.gather(steps - 1, a.got)
-    b.project(2)
-    a.output(b.last, b.sums)
-    b.gather(steps, a.attended)
-    a.scatter(1, b.last)
-    a.scatter(2, a.products)
-    b.project(final=True, held=a.products)
+    b.gather(steps)
+    a.output(b.last)
+    a.scatter(1)
+    b.project(steps - 2, held=a.products)
+    a.scatter(2, b.sums)
+    b.project(final=True)
     for step in range(3, steps + 1):
         a.scatter(step, b.sums)
     b.ask()
     first = a.result()
     a = Layer(1, 0, ring, table, first, told, weights)
-    a.gather(1, b.got)
-    b.attend()
+    a.gather(1)
+    b.attend(first)
     b.answer()
     a.gather(2, b.mixed)
+    for step in range(3, steps):
+        a.gather(step)
     b.output()
-    a.project_ring(steps, b.products)
-    b.scatter(1, a.last)
+    a.project(steps - 2)
+    a.gather(steps, b.products)
+    b.scatter(1, a.last, a.sums)
     a.project(final=True)
-    a.ask()
+    a.ask(b.last)
     for step in range(2, steps - 1):
         b.scatter(step, a.sums)
-    a.attend(b.last)
-    a.answer()
+    a.attend()
     b.scatter(steps - 1, a.got)
+    a.answer(b.last)
+    b.scatter(steps, a.mixed)
     a.output(b.last)
-    b.scatter(steps, a.attended)
-    a.scatter(1, b.last)
     second = b.result()
     other_second = lax.ppermute(second, "dp", swap)
-    for step in range(2, steps + 1):
+    for step in range(1, steps + 1):
         a.scatter(step)
     first = a.result()
     other_first = lax.ppermute(first, "dp", swap)

time: 246 us -> 226 us (0.919)
  waiting for transfers between devices: 103 us -> 75.5 us
  blocking collectives: 0 us -> 10.8 us
  starting transfers between devices: 77.3 us -> 69.4 us
  Pallas kernels: 56.3 us -> 59.6 us
    all_to_all x3 -> x2, waiting for transfers between devices: 17.8 us -> 6.73 us  [answer(): lax.all_to_all(mixed, 'tensor', split_axis=0, concat_axis=0, tiled=True)]
    all_to_all x0 -> x1, blocking collectives: none -> 10.8 us  [answer(): lax.all_to_all(mixed, 'tensor', split_axis=0, concat_axis=0, tiled=True)]
    ppermute x24, waiting for transfers between devices: 47.8 us -> 38 us  [hop(): lax.ppermute(to_front, 'tensor', forward)]
    all_to_all x3, waiting for transfers between devices: 16 us -> 10.7 us  [ask(): lax.all_to_all(mine, 'tensor', split_axis=0, concat_axis=0, tiled=True)]
    all_to_all x3 -> x2, starting transfers between devices: 11 us -> 6.74 us  [answer(): lax.all_to_all(mixed, 'tensor', split_axis=0, concat_axis=0, tiled=True)]
    all_to_all x3, starting transfers between devices: 12.9 us -> 10.2 us  [ask(): lax.all_to_all(mine, 'tensor', split_axis=0, concat_axis=0, tiled=True)]
    pallas_call x7 -> x8, Pallas kernels: 25.3 us -> 27.1 us  [project(): pl.pallas_call(body, out_shape=out_shape, in_specs=[IN_SMEM] + [IN_HBM if...]
  transfers between devices with their start and end apart: 60 -> 59, of which waited for: 38 -> 39; matrix products, arithmetic and copies ran while one was open for 1% -> 2% of each run, Pallas kernels for 22% -> 21%
where the time goes in v3:
time: 226 us; the launch traced here: 225 us
  waiting for transfers between devices  75.5 us (33%)
  starting transfers between devices  69.4 us (31%)
  Pallas kernels  59.6 us (26%)
  blocking collectives  10.8 us (5%)
  local copies, waits for them, and re-layouts  4.77 us (2%)
  other arithmetic  4.16 us (2%)
    ppermute x24, waiting for transfers between devices, hop(): lax.ppermute(to_front, 'tensor', forward)  38 us
    ppermute x24, starting transfers between devices, hop(): lax.ppermute(to_back, 'tensor', backward)  29.4 us
    pallas_call x8, Pallas kernels, project(): pl.pallas_call(body, out_shape=out_shape, in_specs=[IN_SMEM] + [IN_HBM if...  27.1 us
    ppermute x24, starting transfers between devices, hop(): lax.ppermute(to_front, 'tensor', forward)  21.5 us
    ppermute x24, waiting for transfers between devices, hop(): lax.ppermute(to_back, 'tensor', backward)  17.3 us
    pallas_call x3, Pallas kernels, attend(): pl.pallas_call(functools.partial(attend_kernel, level, start, columns), o...  15.2 us
    pallas_call x3, Pallas kernels, output_blocks(): pl.pallas_call(functools.partial(output_kernel, level), out_shape=[jax.Sh...  13.1 us
    all_to_all x1, blocking collectives, answer(): lax.all_to_all(mixed, 'tensor', split_axis=0, concat_axis=0, tiled=True)  10.8 us
  transfers between devices with their start and end apart: 59, of which 39 were waited for; matrix products, arithmetic and copies ran while one was open for 2% of the time, Pallas kernels for 21%

profile of v3, /device:TPU:0, one launch (start us, length us, event | category | flops | bytes accessed | tf_op | source)
XLA Modules:
  0.0 224.8 jit_solution(13327709266373190061)
XLA Ops:
  3.0 2.5 %deal.1 = (bf16[128,1024]{1,0:T(8,128)(2,1)}, bf16[128,1024]{1,0:T(8,128)(2,1)}, f32[2,256]{1,0:T(2,128)}, f32[256,1]{1,0:T(8,128)}, s32[2,256]{1,0:T(2,128)}) custom-call(s32[1,256]{1,0:T(1,128)} %bitcast.15, s32[1,256]{1,0:T(1,128)} %bitcast.18, s32[1,256]{1,0:T(1,128)} %bitcast.16, s32[1,256]{1,0:T(1,128)} %bitcast.17, bf16[256,1024]{1,0:T(8,128)(2,1)} %own_ref.4, ...), custom_call_target="tpu_custom_call" | custom-call | tf_op jit(solution)/shard_map/deal/pallas_call | solution.py:136
  6.0 2.7 %collective-permute-start.3 = (bf16[128,1024]{1,0:T(8,128)(2,1)}, bf16[128,1024]{1,0:T(8,128)(2,1)S(1)}, u32[]{:S(2)}, u32[]{:S(2)}) collective-permute-start(bf16[128,1024]{1,0:T(8,128)(2,1)} %get-tuple-element.112.refs_0_), channel_id=1, source_target_pairs={{0,2},{2,4},{4,6},{6,7},{7,5},{5,3},{3,1},{1,0},{8,10},{10,12},{12... | collective-permute-start | bytes 786440 | tf_op jit(solution)/shard_map/ppermute | solution.py:400
  10.4 5.2 %collective-permute-done.3.refs_1_ = bf16[128,1024]{1,0:T(8,128)(2,1)S(1)} collective-permute-done((bf16[128,1024]{1,0:T(8,128)(2,1)}, bf16[128,1024]{1,0:T(8,128)(2,1)S(1)}, u32[]{:S(2)}, u32[]{:S(2)}) %collective-permute-start.3) | collective-permute-done | bytes 262176 | tf_op jit(solution)/shard_map/ppermute | solution.py:400
  22.4 3.2 %project.8 = (f32[128,512]{1,0:T(8,128)S(1)}, f32[128,128]{1,0:T(8,128)S(1)}, f32[128,128]{1,0:T(8,128)S(1)}) custom-call(s32[8]{0:T(128)S(1)} %dynamic-slice_bitcast_fusion.table_ref, bf16[128,1024]{1,0:T(8,128)(2,1)S(1)} %copy-done.3, bf16[128,1024]{1,0:T(8,128)(2,1)S(1)} %collective-permute-done.3.refs_1_, ...), custom_call_target="tpu_custom_call" | custom-call | flops 503316480 | bytes 3932160 | tf_op jit(solution)/shard_map/project/pallas_call | solution.py:252
  28.0 2.6 %project.9 = (f32[128,512]{1,0:T(8,128)S(1)}, f32[128,128]{1,0:T(8,128)S(1)}, f32[128,128]{1,0:T(8,128)S(1)}) custom-call(s32[8]{0:T(128)S(1)} %dynamic-slice_bitcast_fusion.table_ref, bf16[128,1024]{1,0:T(8,128)(2,1)S(1)} %collective-permute-done.5.refs_0_, bf16[128,1024]{1,0:T(8,128)(2,1)S(1)} %collective-permute-done.6.refs_1_, f32[2,8192]{1,0:T(2,128)S(1)} %copy-done.1, ...), custom_call_target="tpu_custom_call" | custom-call | flops 335544320 | bytes 2621440 | tf_op jit(solution)/shard_map/project/pallas_call | solution.py:252
  30.6 2.0 collective-permute-done.7.refs_0_
  36.0 2.6 %project.10 = (f32[128,512]{1,0:T(8,128)S(1)}, f32[128,128]{1,0:T(8,128)S(1)}, f32[128,128]{1,0:T(8,128)S(1)}) custom-call(s32[8]{0:T(128)S(1)} %dynamic-slice_bitcast_fusion.table_ref, bf16[128,1024]{1,0:T(8,128)(2,1)S(1)} %collective-permute-done.7.refs_0_, bf16[128,1024]{1,0:T(8,128)(2,1)S(1)} %collective-permute-done.8.refs_1_, f32[2,8192]{1,0:T(2,128)S(1)} %copy-done.1, ...), custom_call_target="tpu_custom_call" | custom-call | flops 335544320 | bytes 2621440 | tf_op jit(solution)/shard_map/project/pallas_call | solution.py:252
  40.6 2.4 %collective-permute-start.11 = (bf16[128,1024]{1,0:T(8,128)(2,1)S(1)}, bf16[128,1024]{1,0:T(8,128)(2,1)S(1)}, u32[]{:S(2)}, u32[]{:S(2)}) collective-permute-start(bf16[128,1024]{1,0:T(8,128)(2,1)S(1)} %copy-done.2), channel_id=1, source_target_pairs={{0,2},{2,4},{4,6},{6,7},{7,5},{5,3},{3,1},{1,0},{8,10},{10,12},{12... | collective-permute-start | bytes 786440 | tf_op jit(solution)/shard_map/ppermute | solution.py:400
  43.2 2.9 %project.11 = bf16[128,640]{1,0:T(8,128)(2,1)} custom-call(s32[8]{0:T(128)S(1)} %dynamic-slice_bitcast_fusion.table_ref, bf16[128,512]{1,0:T(8,128)(2,1)S(1)} %collective-permute-done.9.refs_0_, bf16[128,512]{1,0:T(8,128)(2,1)S(1)} %collective-permute-done.10.refs_1_, f32[2,8192]{1,0:T(2,128)S(1)} %copy-done.1, bf16[2,8192,512]{2,1,0:T(8,128)(2,1)} %refs_5_.9, ...), custom_call_target="tpu_custom_call" | custom-call | flops 167772160 | bytes 1310720 | tf_op jit(solution)/shard_map/project/pallas_call | solution.py:252
  46.1 3.4 %all-to-all-start = ((bf16[8,16,640]{2,1,0:T(8,128)(2,1)}), bf16[8,16,640]{2,1,0:T(8,128)(2,1)S(1)}, u32[]{:S(2)}, u32[]{:S(2)}) async-start(bf16[8,16,640]{2,1,0:T(8,128)(2,1)} %bitcast.5), calls=%async_computation | async-start | bytes 327680 | tf_op jit(solution)/shard_map/all_to_all | solution.py:444
  49.6 2.5 %collective-permute-done.12.refs_2_ = bf16[128,1024]{1,0:T(8,128)(2,1)S(1)} collective-permute-done((bf16[128,1024]{1,0:T(8,128)(2,1)S(1)}, bf16[128,1024]{1,0:T(8,128)(2,1)S(1)}, u32[]{:S(2)}, u32[]{:S(2)}) %collective-permute-start.12) | collective-permute-done | bytes 262176 | tf_op jit(solution)/shard_map/ppermute | solution.py:400
  52.2 1.9 collective-permute-start.15
  54.1 3.1 %all-to-all-done.got_ref = bf16[8,16,640]{2,1,0:T(8,128)(2,1)S(1)} async-done(((bf16[8,16,640]{2,1,0:T(8,128)(2,1)}), bf16[8,16,640]{2,1,0:T(8,128)(2,1)S(1)}, u32[]{:S(2)}, u32[]{:S(2)}) %all-to-all-start) | async-done | bytes 163872 | tf_op jit(solution)/shard_map/all_to_all | solution.py:444
  57.8 5.1 %attend.3 = bf16[8,16,512]{2,1,0:T(8,128)(2,1)} custom-call(s32[8]{0:T(128)} %copy-done.7, s32[2,256]{1,0:T(2,128)} %get-tuple-element.110.facts_ref, bf16[8,16,640]{2,1,0:T(8,128)(2,1)} %copy-done.14, f32[256,128]{1,0:T(8,128)} %get-tuple-element.218.cosine_ref, f32[256,128]{1,0:T(8,128)} %get-tuple-element.219.sine_ref, bf16[2,32,64,1024]{3,2,1,0:T(8,128)(2,1)} %own_ref.7, ...), custom_call_target="tpu_custom_call" | custom-call | flops 100000000 | bytes 2097152 | tf_op jit(solution)/shard_map/attend/pallas_call | solution.py:334
  63.0 2.0 collective-permute-start.17
  65.0 3.4 %all-to-all-start.1 = ((bf16[8,16,512]{2,1,0:T(8,128)(2,1)}), bf16[8,16,512]{2,1,0:T(8,128)(2,1)S(1)}, u32[]{:S(2)}, u32[]{:S(2)}) async-start(bf16[8,16,512]{2,1,0:T(8,128)(2,1)} %attend.3), calls=%async_computation.1 | async-start | bytes 262144 | tf_op jit(solution)/shard_map/all_to_all | solution.py:455
  72.4 3.3 %all-to-all-done.1 = bf16[8,16,512]{2,1,0:T(8,128)(2,1)S(1)} async-done(((bf16[8,16,512]{2,1,0:T(8,128)(2,1)}), bf16[8,16,512]{2,1,0:T(8,128)(2,1)S(1)}, u32[]{:S(2)}, u32[]{:S(2)}) %all-to-all-start.1) | async-done | bytes 131104 | tf_op jit(solution)/shard_map/all_to_all | solution.py:455
  76.8 4.4 %output.3 = (bf16[128,512]{1,0:T(8,128)(2,1)S(1)}, bf16[128,512]{1,0:T(8,128)(2,1)S(1)}, bf16[128,1024]{1,0:T(8,128)(2,1)S(1)}, bf16[128,1024]{1,0:T(8,128)(2,1)...) custom-call(s32[8]{0:T(128)S(1)} %copy-done.8, ...), custom_call_target="tpu_custom_call" | custom-call | flops 1073741824 | bytes 8388608 | tf_op jit(solution)/shard_map/output/pallas_call | solution.py:373
  83.3 4.1 %project.12 = (f32[128,512]{1,0:T(8,128)S(1)}, f32[128,128]{1,0:T(8,128)S(1)}, f32[128,128]{1,0:T(8,128)S(1)}) custom-call(s32[8]{0:T(128)S(1)} %copy-done.8, bf16[128,1024]{1,0:T(8,128)(2,1)S(1)} %copy-done.2, bf16[128,1024]{1,0:T(8,128)(2,1)S(1)} %collective-permute-done.11.refs_1_, bf16[128,1024]{1,0:T(8,128)(2,1)S(1)} %collective-permute-done.12.refs_2_, ...), custom_call_target="tpu_custom_call" | custom-call | flops 838860800 | bytes 6553600 | tf_op jit(solution)/shard_map/project/pallas_call | solution.py:252
  89.6 3.8 %project.13 = bf16[128,640]{1,0:T(8,128)(2,1)} custom-call(s32[8]{0:T(128)S(1)} %copy-done.8, bf16[128,1024]{1,0:T(8,128)(2,1)S(1)} %collective-permute-done.16.refs_0_, bf16[128,1024]{1,0:T(8,128)(2,1)S(1)} %collective-permute-done.17.refs_1_, bf16[128,512]{1,0:T(8,128)(2,1)S(1)} %collective-permute-done.18.refs_2_, ...), custom_call_target="tpu_custom_call" | custom-call | flops 503316480 | bytes 3932160 | tf_op jit(solution)/shard_map/project/pallas_call | solution.py:252
  95.0 1.7 collective-permute-start.24
  97.1 5.5 %collective-permute-done.24 = bf16[128,1024]{1,0:T(8,128)(2,1)S(1)} collective-permute-done((bf16[128,1024]{1,0:T(8,128)(2,1)S(1)}, bf16[128,1024]{1,0:T(8,128)(2,1)S(1)}, u32[]{:S(2)}, u32[]{:S(2)}) %collective-permute-start.24) | collective-permute-done | bytes 262176 | tf_op jit(solution)/shard_map/ppermute | solution.py:400
  102.7 2.5 %collective-permute-done.25 = bf16[128,1024]{1,0:T(8,128)(2,1)S(1)} collective-permute-done((bf16[128,1024]{1,0:T(8,128)(2,1)S(1)}, bf16[128,1024]{1,0:T(8,128)(2,1)S(1)}, u32[]{:S(2)}, u32[]{:S(2)}) %collective-permute-start.25) | collective-permute-done | bytes 262176 | tf_op jit(solution)/shard_map/ppermute | solution.py:400
  107.4 3.4 %all-to-all-start.2 = ((bf16[8,16,640]{2,1,0:T(8,128)(2,1)}), bf16[8,16,640]{2,1,0:T(8,128)(2,1)S(1)}, u32[]{:S(2)}, u32[]{:S(2)}) async-start(bf16[8,16,640]{2,1,0:T(8,128)(2,1)} %bitcast.7), calls=%async_computation.2 | async-start | bytes 327680 | tf_op jit(solution)/shard_map/all_to_all | solution.py:444
  114.8 3.6 %all-to-all-done.2.got_ref = bf16[8,16,640]{2,1,0:T(8,128)(2,1)S(1)} async-done(((bf16[8,16,640]{2,1,0:T(8,128)(2,1)}), bf16[8,16,640]{2,1,0:T(8,128)(2,1)S(1)}, u32[]{:S(2)}, u32[]{:S(2)}) %all-to-all-start.2) | async-done | bytes 163872 | tf_op jit(solution)/shard_map/all_to_all | solution.py:444
  119.1 5.1 %attend.4 = bf16[8,16,512]{2,1,0:T(8,128)(2,1)} custom-call(s32[8]{0:T(128)} %copy-done.7, s32[2,256]{1,0:T(2,128)} %get-tuple-element.110.facts_ref, bf16[8,16,640]{2,1,0:T(8,128)(2,1)} %copy-done.13, f32[256,128]{1,0:T(8,128)} %get-tuple-element.218.cosine_ref, f32[256,128]{1,0:T(8,128)} %get-tuple-element.219.sine_ref, bf16[2,32,64,1024]{3,2,1,0:T(8,128)(2,1)} %own_ref.7, ...), custom_call_target="tpu_custom_call" | custom-call | flops 100000000 | bytes 2097152 | tf_op jit(solution)/shard_map/attend/pallas_call | solution.py:334
  124.4 1.8 collective-permute-start.31
  126.3 3.4 %all-to-all-start.3 = ((bf16[8,16,512]{2,1,0:T(8,128)(2,1)}), bf16[8,16,512]{2,1,0:T(8,128)(2,1)S(1)}, u32[]{:S(2)}, u32[]{:S(2)}) async-start(bf16[8,16,512]{2,1,0:T(8,128)(2,1)} %attend.4), calls=%async_computation.3 | async-start | bytes 262144 | tf_op jit(solution)/shard_map/all_to_all | solution.py:455
  129.6 2.3 %collective-permute-done.30.refs_3_ = bf16[128,1024]{1,0:T(8,128)(2,1)S(1)} collective-permute-done((bf16[128,1024]{1,0:T(8,128)(2,1)S(1)}, bf16[128,1024]{1,0:T(8,128)(2,1)S(1)}, u32[]{:S(2)}, u32[]{:S(2)}) %collective-permute-start.30) | collective-permute-done | bytes 262176 | tf_op jit(solution)/shard_map/ppermute | solution.py:400
  134.2 3.4 %all-to-all-done.3 = bf16[8,16,512]{2,1,0:T(8,128)(2,1)S(1)} async-done(((bf16[8,16,512]{2,1,0:T(8,128)(2,1)}), bf16[8,16,512]{2,1,0:T(8,128)(2,1)S(1)}, u32[]{:S(2)}, u32[]{:S(2)}) %all-to-all-start.3) | async-done | bytes 131104 | tf_op jit(solution)/shard_map/all_to_all | solution.py:455
  137.6 4.4 %output.4 = (bf16[128,512]{1,0:T(8,128)(2,1)S(1)}, bf16[128,512]{1,0:T(8,128)(2,1)S(1)}, bf16[128,1024]{1,0:T(8,128)(2,1)S(1)}, bf16[128,1024]{1,0:T(8,128)(2,1)...) custom-call(s32[8]{0:T(128)S(1)} %copy-done.9, ...), custom_call_target="tpu_custom_call" | custom-call | flops 1073741824 | bytes 8388608 | tf_op jit(solution)/shard_map/output/pallas_call | solution.py:373
  142.1 2.0 collective-permute-start.35
  144.2 4.1 %project.14 = (f32[128,512]{1,0:T(8,128)S(1)}, f32[128,128]{1,0:T(8,128)S(1)}, f32[128,128]{1,0:T(8,128)S(1)}) custom-call(s32[8]{0:T(128)S(1)} %copy-done.9, bf16[128,1024]{1,0:T(8,128)(2,1)S(1)} %add_convert_fusion.10.refs_0_, bf16[128,1024]{1,0:T(8,128)(2,1)S(1)} %collective-permute-done.28.refs_1_, ...), custom_call_target="tpu_custom_call" | custom-call | flops 838860800 | bytes 6553600 | tf_op jit(solution)/shard_map/project/pallas_call | solution.py:252
  150.5 3.8 %project.15 = bf16[128,640]{1,0:T(8,128)(2,1)} custom-call(s32[8]{0:T(128)S(1)} %copy-done.9, bf16[128,1024]{1,0:T(8,128)(2,1)S(1)} %collective-permute-done.32.refs_0_, bf16[128,1024]{1,0:T(8,128)(2,1)S(1)} %collective-permute-done.33.refs_1_, bf16[128,512]{1,0:T(8,128)(2,1)S(1)} %collective-permute-done.34.refs_2_, ...), custom_call_target="tpu_custom_call" | custom-call | flops 503316480 | bytes 3932160 | tf_op jit(solution)/shard_map/project/pallas_call | solution.py:252
  156.2 1.9 collective-permute-start.39
  158.1 3.4 %all-to-all-start.4 = ((bf16[8,16,640]{2,1,0:T(8,128)(2,1)}), bf16[8,16,640]{2,1,0:T(8,128)(2,1)S(1)}, u32[]{:S(2)}, u32[]{:S(2)}) async-start(bf16[8,16,640]{2,1,0:T(8,128)(2,1)} %bitcast.9), calls=%async_computation.4 | async-start | bytes 327680 | tf_op jit(solution)/shard_map/all_to_all | solution.py:444
  161.5 3.2 %collective-permute-done.38 = bf16[128,1024]{1,0:T(8,128)(2,1)S(1)} collective-permute-done((bf16[128,1024]{1,0:T(8,128)(2,1)S(1)}, bf16[128,1024]{1,0:T(8,128)(2,1)S(1)}, u32[]{:S(2)}, u32[]{:S(2)}) %collective-permute-start.38) | collective-permute-done | bytes 262176 | tf_op jit(solution)/shard_map/ppermute | solution.py:400
  165.1 4.0 %all-to-all-done.4.got_ref = bf16[8,16,640]{2,1,0:T(8,128)(2,1)S(1)} async-done(((bf16[8,16,640]{2,1,0:T(8,128)(2,1)}), bf16[8,16,640]{2,1,0:T(8,128)(2,1)S(1)}, u32[]{:S(2)}, u32[]{:S(2)}) %all-to-all-start.4) | async-done | bytes 163872 | tf_op jit(solution)/shard_map/all_to_all | solution.py:444
  169.2 1.9 collective-permute-start.41
  171.1 5.1 %attend.5 = bf16[8,16,512]{2,1,0:T(8,128)(2,1)} custom-call(s32[8]{0:T(128)} %copy-done.7, s32[2,256]{1,0:T(2,128)} %get-tuple-element.110.facts_ref, bf16[8,16,640]{2,1,0:T(8,128)(2,1)} %copy-done.12, f32[256,128]{1,0:T(8,128)} %get-tuple-element.218.cosine_ref, f32[256,128]{1,0:T(8,128)} %get-tuple-element.219.sine_ref, bf16[2,32,64,1024]{3,2,1,0:T(8,128)(2,1)} %own_ref.7, ...), custom_call_target="tpu_custom_call" | custom-call | flops 100000000 | bytes 2097152 | tf_op jit(solution)/shard_map/attend/pallas_call | solution.py:334
  176.7 2.1 collective-permute-start.43
  178.8 10.8 %all_to_all.30 = bf16[8,16,512]{2,1,0:T(8,128)(2,1)S(1)} all-to-all(bf16[8,16,512]{2,1,0:T(8,128)(2,1)} %attend.5), channel_id=1, replica_groups=mesh['group'=2,'dp'=2,'tensor'=8] {'tensor'}, dimensions={0} | all-to-all | bytes 262144 | tf_op jit(solution)/shard_map/all_to_all | solution.py:455
  189.7 4.4 %output.5 = (bf16[128,512]{1,0:T(8,128)(2,1)S(1)}, bf16[128,512]{1,0:T(8,128)(2,1)S(1)}, bf16[128,1024]{1,0:T(8,128)(2,1)S(1)}, bf16[128,1024]{1,0:T(8,128)(2,1)...) custom-call(s32[8]{0:T(128)S(1)} %copy-done.10, ...), custom_call_target="tpu_custom_call" | custom-call | flops 1073741824 | bytes 8388608 | tf_op jit(solution)/shard_map/output/pallas_call | solution.py:373
  194.1 2.1 collective-permute-start.45
  196.2 3.1 %collective-permute-done.44 = bf16[128,512]{1,0:T(8,128)(2,1)S(1)} collective-permute-done((bf16[128,512]{1,0:T(8,128)(2,1)S(1)}, bf16[128,512]{1,0:T(8,128)(2,1)S(1)}, u32[]{:S(2)}, u32[]{:S(2)}) %collective-permute-start.44) | collective-permute-done | bytes 131104 | tf_op jit(solution)/shard_map/ppermute | solution.py:400
  201.7 4.3 %collective-permute-done.46 = bf16[128,1024]{1,0:T(8,128)(2,1)S(1)} collective-permute-done((bf16[128,1024]{1,0:T(8,128)(2,1)S(1)}, bf16[128,1024]{1,0:T(8,128)(2,1)S(1)}, u32[]{:S(2)}, u32[]{:S(2)}) %collective-permute-start.46) | collective-permute-done | bytes 262176 | tf_op jit(solution)/shard_map/ppermute | solution.py:400
  209.3 4.3 %collective-permute-done.48 = bf16[128,1024]{1,0:T(8,128)(2,1)S(1)} collective-permute-done((bf16[128,1024]{1,0:T(8,128)(2,1)S(1)}, bf16[128,1024]{1,0:T(8,128)(2,1)S(1)}, u32[]{:S(2)}, u32[]{:S(2)}) %collective-permute-start.48) | collective-permute-done | bytes 262176 | tf_op jit(solution)/shard_map/ppermute | solution.py:400
  216.8 4.1 %collective-permute-done.50 = bf16[128,1024]{1,0:T(8,128)(2,1)S(1)} collective-permute-done((bf16[128,1024]{1,0:T(8,128)(2,1)S(1)}, bf16[128,1024]{1,0:T(8,128)(2,1)S(1)}, u32[]{:S(2)}, u32[]{:S(2)}) %collective-permute-start.50) | collective-permute-done | bytes 262176 | tf_op jit(solution)/shard_map/ppermute | solution.py:400
  (168 shorter events, 59.4 us)
Async XLA Ops:
  5.6 51.6 %collective-permute-start.13 = (bf16[2,32,64,1024]{3,2,1,0:T(8,128)(2,1)}, bf16[2,32,64,1024]{3,2,1,0:T(8,128)(2,1)}, u32[]{:S(2)}, u32[]{:S(2)}) collective-permute-start(bf16[2,32,64,1024]{3,2,1,0:T(8,128)(2,1)} %own_ref.7), channel_id=1, source_target_pairs={{0,8},{8,0},{1,9},{9,1},{2,10},{10,2},{3,11},{11,3},{4,12},{12,4},... | collective-permute-start | bytes 25165832 | tf_op jit(solution)/shard_map/ppermute | solution.py:507
  6.0 9.7 %collective-permute-start.3 = (bf16[128,1024]{1,0:T(8,128)(2,1)}, bf16[128,1024]{1,0:T(8,128)(2,1)S(1)}, u32[]{:S(2)}, u32[]{:S(2)}) collective-permute-start(bf16[128,1024]{1,0:T(8,128)(2,1)} %get-tuple-element.112.refs_0_), channel_id=1, source_target_pairs={{0,2},{2,4},{4,6},{6,7},{7,5},{5,3},{3,1},{1,0},{8,10},{10,12},{12... | collective-permute-start | bytes 786440 | tf_op jit(solution)/shard_map/ppermute | solution.py:400
  8.7 8.5 %collective-permute-start.4 = (bf16[128,1024]{1,0:T(8,128)(2,1)}, bf16[128,1024]{1,0:T(8,128)(2,1)S(1)}, u32[]{:S(2)}, u32[]{:S(2)}) collective-permute-start(bf16[128,1024]{1,0:T(8,128)(2,1)} %get-tuple-element.112.refs_0_), channel_id=1, source_target_pairs={{0,1},{2,0},{4,2},{6,4},{7,6},{5,7},{3,5},{1,3},{8,9},{10,8},{12,1... | collective-permute-start | bytes 786440 | tf_op jit(solution)/shard_map/ppermute | solution.py:400
  17.2 8.5 %collective-permute-start.5 = (bf16[128,1024]{1,0:T(8,128)(2,1)S(1)}, bf16[128,1024]{1,0:T(8,128)(2,1)S(1)}, u32[]{:S(2)}, u32[]{:S(2)}) collective-permute-start(bf16[128,1024]{1,0:T(8,128)(2,1)S(1)} %collective-permute-done.3.refs_1_), channel_id=1, source_target_pairs={{0,2},{2,4},{4,6},{6,7},{7,5},{5,3},{3,1},{1,0},{8,10},{10,12},{12... | collective-permute-start | bytes 786440 | tf_op jit(solution)/shard_map/ppermute | solution.py:400
  18.8 7.2 %collective-permute-start.6 = (bf16[128,1024]{1,0:T(8,128)(2,1)S(1)}, bf16[128,1024]{1,0:T(8,128)(2,1)S(1)}, u32[]{:S(2)}, u32[]{:S(2)}) collective-permute-start(bf16[128,1024]{1,0:T(8,128)(2,1)S(1)} %collective-permute-done.4.refs_2_), channel_id=1, source_target_pairs={{0,1},{2,0},{4,2},{6,4},{7,6},{5,7},{3,5},{1,3},{8,9},{10,8},{12,1... | collective-permute-start | bytes 786440 | tf_op jit(solution)/shard_map/ppermute | solution.py:400
  26.0 6.7 %collective-permute-start.7 = (bf16[128,1024]{1,0:T(8,128)(2,1)S(1)}, bf16[128,1024]{1,0:T(8,128)(2,1)S(1)}, u32[]{:S(2)}, u32[]{:S(2)}) collective-permute-start(bf16[128,1024]{1,0:T(8,128)(2,1)S(1)} %collective-permute-done.5.refs_0_), channel_id=1, source_target_pairs={{0,2},{2,4},{4,6},{6,7},{7,5},{5,3},{3,1},{1,0},{8,10},{10,12},{12... | collective-permute-start | bytes 786440 | tf_op jit(solution)/shard_map/ppermute | solution.py:400
  27.5 6.4 %collective-permute-start.8 = (bf16[128,1024]{1,0:T(8,128)(2,1)S(1)}, bf16[128,1024]{1,0:T(8,128)(2,1)S(1)}, u32[]{:S(2)}, u32[]{:S(2)}) collective-permute-start(bf16[128,1024]{1,0:T(8,128)(2,1)S(1)} %collective-permute-done.6.refs_1_), channel_id=1, source_target_pairs={{0,1},{2,0},{4,2},{6,4},{7,6},{5,7},{3,5},{1,3},{8,9},{10,8},{12,1... | collective-permute-start | bytes 786440 | tf_op jit(solution)/shard_map/ppermute | solution.py:400
  40.6 8.9 %collective-permute-start.11 = (bf16[128,1024]{1,0:T(8,128)(2,1)S(1)}, bf16[128,1024]{1,0:T(8,128)(2,1)S(1)}, u32[]{:S(2)}, u32[]{:S(2)}) collective-permute-start(bf16[128,1024]{1,0:T(8,128)(2,1)S(1)} %copy-done.2), channel_id=1, source_target_pairs={{0,2},{2,4},{4,6},{6,7},{7,5},{5,3},{3,1},{1,0},{8,10},{10,12},{12... | collective-permute-start | bytes 786440 | tf_op jit(solution)/shard_map/ppermute | solution.py:400
  43.0 9.0 %collective-permute-start.12 = (bf16[128,1024]{1,0:T(8,128)(2,1)S(1)}, bf16[128,1024]{1,0:T(8,128)(2,1)S(1)}, u32[]{:S(2)}, u32[]{:S(2)}) collective-permute-start(bf16[128,1024]{1,0:T(8,128)(2,1)S(1)} %copy-done.2), channel_id=1, source_target_pairs={{0,1},{2,0},{4,2},{6,4},{7,6},{5,7},{3,5},{1,3},{8,9},{10,8},{12,1... | collective-permute-start | bytes 786440 | tf_op jit(solution)/shard_map/ppermute | solution.py:400
  46.1 11.0 %all-to-all-start = ((bf16[8,16,640]{2,1,0:T(8,128)(2,1)}), bf16[8,16,640]{2,1,0:T(8,128)(2,1)S(1)}, u32[]{:S(2)}, u32[]{:S(2)}) async-start(bf16[8,16,640]{2,1,0:T(8,128)(2,1)} %bitcast.5), calls=%async_computation | async-start | bytes 327680 | tf_op jit(solution)/shard_map/all_to_all | solution.py:444
  52.1 10.9 %collective-permute-start.14 = (bf16[128,1024]{1,0:T(8,128)(2,1)S(1)}, bf16[128,1024]{1,0:T(8,128)(2,1)S(1)}, u32[]{:S(2)}, u32[]{:S(2)}) collective-permute-start(bf16[128,1024]{1,0:T(8,128)(2,1)S(1)} %collective-permute-done.11.refs_1_), channel_id=1, source_target_pairs={{0,2},{2,4},{4,6},{6,7},{7,5},{5,3},{3,1},{1,0},{8,10},{10,12},{12... | collective-permute-start | bytes 786440 | tf_op jit(solution)/shard_map/ppermute | solution.py:400
  52.2 10.8 %collective-permute-start.15 = (bf16[128,1024]{1,0:T(8,128)(2,1)S(1)}, bf16[128,1024]{1,0:T(8,128)(2,1)S(1)}, u32[]{:S(2)}, u32[]{:S(2)}) collective-permute-start(bf16[128,1024]{1,0:T(8,128)(2,1)S(1)} %collective-permute-done.12.refs_2_), channel_id=1, source_target_pairs={{0,1},{2,0},{4,2},{6,4},{7,6},{5,7},{3,5},{1,3},{8,9},{10,8},{12,1... | collective-permute-start | bytes 786440 | tf_op jit(solution)/shard_map/ppermute | solution.py:400
  62.9 6.6 %collective-permute-start.16 = (bf16[128,1024]{1,0:T(8,128)(2,1)S(1)}, bf16[128,1024]{1,0:T(8,128)(2,1)S(1)}, u32[]{:S(2)}, u32[]{:S(2)}) collective-permute-start(bf16[128,1024]{1,0:T(8,128)(2,1)S(1)} %collective-permute-done.14.refs_3_), channel_id=1, source_target_pairs={{0,2},{2,4},{4,6},{6,7},{7,5},{5,3},{3,1},{1,0},{8,10},{10,12},{12... | collective-permute-start | bytes 786440 | tf_op jit(solution)/shard_map/ppermute | solution.py:400
  63.0 7.3 %collective-permute-start.17 = (bf16[128,1024]{1,0:T(8,128)(2,1)S(1)}, bf16[128,1024]{1,0:T(8,128)(2,1)S(1)}, u32[]{:S(2)}, u32[]{:S(2)}) collective-permute-start(bf16[128,1024]{1,0:T(8,128)(2,1)S(1)} %collective-permute-done.15.refs_4_), channel_id=1, source_target_pairs={{0,1},{2,0},{4,2},{6,4},{7,6},{5,7},{3,5},{1,3},{8,9},{10,8},{12,1... | collective-permute-start | bytes 786440 | tf_op jit(solution)/shard_map/ppermute | solution.py:400
  65.0 10.8 %all-to-all-start.1 = ((bf16[8,16,512]{2,1,0:T(8,128)(2,1)}), bf16[8,16,512]{2,1,0:T(8,128)(2,1)S(1)}, u32[]{:S(2)}, u32[]{:S(2)}) async-start(bf16[8,16,512]{2,1,0:T(8,128)(2,1)} %attend.3), calls=%async_computation.1 | async-start | bytes 262144 | tf_op jit(solution)/shard_map/all_to_all | solution.py:455
  81.1 6.2 %collective-permute-start.20 = (bf16[128,512]{1,0:T(8,128)(2,1)S(1)}, bf16[128,512]{1,0:T(8,128)(2,1)S(1)}, u32[]{:S(2)}, u32[]{:S(2)}) collective-permute-start(bf16[128,512]{1,0:T(8,128)(2,1)S(1)} %get-tuple-element.147), channel_id=1, source_target_pairs={{0,2},{2,4},{4,6},{6,7},{7,5},{5,3},{3,1},{1,0},{8,10},{10,12},{12... | collective-permute-start | bytes 393224 | tf_op jit(solution)/shard_map/ppermute | solution.py:400
  81.9 5.6 %collective-permute-start.21 = (bf16[128,512]{1,0:T(8,128)(2,1)S(1)}, bf16[128,512]{1,0:T(8,128)(2,1)S(1)}, u32[]{:S(2)}, u32[]{:S(2)}) collective-permute-start(bf16[128,512]{1,0:T(8,128)(2,1)S(1)} %get-tuple-element.149), channel_id=1, source_target_pairs={{0,1},{2,0},{4,2},{6,4},{7,6},{5,7},{3,5},{1,3},{8,9},{10,8},{12,1... | collective-permute-start | bytes 393224 | tf_op jit(solution)/shard_map/ppermute | solution.py:400
  87.6 6.7 %collective-permute-start.22 = (bf16[128,1024]{1,0:T(8,128)(2,1)S(1)}, bf16[128,1024]{1,0:T(8,128)(2,1)S(1)}, u32[]{:S(2)}, u32[]{:S(2)}) collective-permute-start(bf16[128,1024]{1,0:T(8,128)(2,1)S(1)} %pad_maximum_fusion), channel_id=1, source_target_pairs={{0,2},{2,4},{4,6},{6,7},{7,5},{5,3},{3,1},{1,0},{8,10},{10,12},{12... | collective-permute-start | bytes 786440 | tf_op jit(solution)/shard_map/ppermute | solution.py:400
  88.3 6.7 %collective-permute-start.23 = (bf16[128,1024]{1,0:T(8,128)(2,1)S(1)}, bf16[128,1024]{1,0:T(8,128)(2,1)S(1)}, u32[]{:S(2)}, u32[]{:S(2)}) collective-permute-start(bf16[128,1024]{1,0:T(8,128)(2,1)S(1)} %pad_maximum_fusion.1), channel_id=1, source_target_pairs={{0,1},{2,0},{4,2},{6,4},{7,6},{5,7},{3,5},{1,3},{8,9},{10,8},{12,1... | collective-permute-start | bytes 786440 | tf_op jit(solution)/shard_map/ppermute | solution.py:400
  95.0 7.6 %collective-permute-start.24 = (bf16[128,1024]{1,0:T(8,128)(2,1)S(1)}, bf16[128,1024]{1,0:T(8,128)(2,1)S(1)}, u32[]{:S(2)}, u32[]{:S(2)}) collective-permute-start(bf16[128,1024]{1,0:T(8,128)(2,1)S(1)} %add_convert_fusion.14), channel_id=1, source_target_pairs={{0,2},{2,4},{4,6},{6,7},{7,5},{5,3},{3,1},{1,0},{8,10},{10,12},{12... | collective-permute-start | bytes 786440 | tf_op jit(solution)/shard_map/ppermute | solution.py:400
  96.8 8.5 %collective-permute-start.25 = (bf16[128,1024]{1,0:T(8,128)(2,1)S(1)}, bf16[128,1024]{1,0:T(8,128)(2,1)S(1)}, u32[]{:S(2)}, u32[]{:S(2)}) collective-permute-start(bf16[128,1024]{1,0:T(8,128)(2,1)S(1)} %add_convert_fusion.13), channel_id=1, source_target_pairs={{0,1},{2,0},{4,2},{6,4},{7,6},{5,7},{3,5},{1,3},{8,9},{10,8},{12,1... | collective-permute-start | bytes 786440 | tf_op jit(solution)/shard_map/ppermute | solution.py:400
  105.3 6.4 %collective-permute-start.26 = (bf16[128,1024]{1,0:T(8,128)(2,1)S(1)}, bf16[128,1024]{1,0:T(8,128)(2,1)S(1)}, u32[]{:S(2)}, u32[]{:S(2)}) collective-permute-start(bf16[128,1024]{1,0:T(8,128)(2,1)S(1)} %add_convert_fusion.12), channel_id=1, source_target_pairs={{0,2},{2,4},{4,6},{6,7},{7,5},{5,3},{3,1},{1,0},{8,10},{10,12},{12... | collective-permute-start | bytes 786440 | tf_op jit(solution)/shard_map/ppermute | solution.py:400
  106.2 6.4 %collective-permute-start.27 = (bf16[128,1024]{1,0:T(8,128)(2,1)S(1)}, bf16[128,1024]{1,0:T(8,128)(2,1)S(1)}, u32[]{:S(2)}, u32[]{:S(2)}) collective-permute-start(bf16[128,1024]{1,0:T(8,128)(2,1)S(1)} %add_convert_fusion.11), channel_id=1, source_target_pairs={{0,1},{2,0},{4,2},{6,4},{7,6},{5,7},{3,5},{1,3},{8,9},{10,8},{12,1... | collective-permute-start | bytes 786440 | tf_op jit(solution)/shard_map/ppermute | solution.py:400
  107.4 11.0 %all-to-all-start.2 = ((bf16[8,16,640]{2,1,0:T(8,128)(2,1)}), bf16[8,16,640]{2,1,0:T(8,128)(2,1)S(1)}, u32[]{:S(2)}, u32[]{:S(2)}) async-start(bf16[8,16,640]{2,1,0:T(8,128)(2,1)} %bitcast.7), calls=%async_computation.2 | async-start | bytes 327680 | tf_op jit(solution)/shard_map/all_to_all | solution.py:444
  112.7 11.4 %collective-permute-start.28 = (bf16[128,1024]{1,0:T(8,128)(2,1)S(1)}, bf16[128,1024]{1,0:T(8,128)(2,1)S(1)}, u32[]{:S(2)}, u32[]{:S(2)}) collective-permute-start(bf16[128,1024]{1,0:T(8,128)(2,1)S(1)} %add_convert_fusion.10.refs_0_), channel_id=1, source_target_pairs={{0,2},{2,4},{4,6},{6,7},{7,5},{5,3},{3,1},{1,0},{8,10},{10,12},{12... | collective-permute-start | bytes 786440 | tf_op jit(solution)/shard_map/ppermute | solution.py:400
  113.4 10.8 %collective-permute-start.29 = (bf16[128,1024]{1,0:T(8,128)(2,1)S(1)}, bf16[128,1024]{1,0:T(8,128)(2,1)S(1)}, u32[]{:S(2)}, u32[]{:S(2)}) collective-permute-start(bf16[128,1024]{1,0:T(8,128)(2,1)S(1)} %add_convert_fusion.10.refs_0_), channel_id=1, source_target_pairs={{0,1},{2,0},{4,2},{6,4},{7,6},{5,7},{3,5},{1,3},{8,9},{10,8},{12,1... | collective-permute-start | bytes 786440 | tf_op jit(solution)/shard_map/ppermute | solution.py:400
  124.2 7.7 %collective-permute-start.30 = (bf16[128,1024]{1,0:T(8,128)(2,1)S(1)}, bf16[128,1024]{1,0:T(8,128)(2,1)S(1)}, u32[]{:S(2)}, u32[]{:S(2)}) collective-permute-start(bf16[128,1024]{1,0:T(8,128)(2,1)S(1)} %collective-permute-done.28.refs_1_), channel_id=1, source_target_pairs={{0,2},{2,4},{4,6},{6,7},{7,5},{5,3},{3,1},{1,0},{8,10},{10,12},{12... | collective-permute-start | bytes 786440 | tf_op jit(solution)/shard_map/ppermute | solution.py:400
  124.4 7.8 %collective-permute-start.31 = (bf16[128,1024]{1,0:T(8,128)(2,1)S(1)}, bf16[128,1024]{1,0:T(8,128)(2,1)S(1)}, u32[]{:S(2)}, u32[]{:S(2)}) collective-permute-start(bf16[128,1024]{1,0:T(8,128)(2,1)S(1)} %collective-permute-done.29.refs_2_), channel_id=1, source_target_pairs={{0,1},{2,0},{4,2},{6,4},{7,6},{5,7},{3,5},{1,3},{8,9},{10,8},{12,1... | collective-permute-start | bytes 786440 | tf_op jit(solution)/shard_map/ppermute | solution.py:400
  126.3 11.4 %all-to-all-start.3 = ((bf16[8,16,512]{2,1,0:T(8,128)(2,1)}), bf16[8,16,512]{2,1,0:T(8,128)(2,1)S(1)}, u32[]{:S(2)}, u32[]{:S(2)}) async-start(bf16[8,16,512]{2,1,0:T(8,128)(2,1)} %attend.4), calls=%async_computation.3 | async-start | bytes 262144 | tf_op jit(solution)/shard_map/all_to_all | solution.py:455
  132.2 9.8 %collective-permute-start.32 = (bf16[128,1024]{1,0:T(8,128)(2,1)S(1)}, bf16[128,1024]{1,0:T(8,128)(2,1)S(1)}, u32[]{:S(2)}, u32[]{:S(2)}) collective-permute-start(bf16[128,1024]{1,0:T(8,128)(2,1)S(1)} %collective-permute-done.30.refs_3_), channel_id=1, source_target_pairs={{0,2},{2,4},{4,6},{6,7},{7,5},{5,3},{3,1},{1,0},{8,10},{10,12},{12... | collective-permute-start | bytes 786440 | tf_op jit(solution)/shard_map/ppermute | solution.py:400
  132.7 9.3 %collective-permute-start.33 = (bf16[128,1024]{1,0:T(8,128)(2,1)S(1)}, bf16[128,1024]{1,0:T(8,128)(2,1)S(1)}, u32[]{:S(2)}, u32[]{:S(2)}) collective-permute-start(bf16[128,1024]{1,0:T(8,128)(2,1)S(1)} %collective-permute-done.31.refs_4_), channel_id=1, source_target_pairs={{0,1},{2,0},{4,2},{6,4},{7,6},{5,7},{3,5},{1,3},{8,9},{10,8},{12,1... | collective-permute-start | bytes 786440 | tf_op jit(solution)/shard_map/ppermute | solution.py:400
  142.1 6.2 %collective-permute-start.34 = (bf16[128,512]{1,0:T(8,128)(2,1)S(1)}, bf16[128,512]{1,0:T(8,128)(2,1)S(1)}, u32[]{:S(2)}, u32[]{:S(2)}) collective-permute-start(bf16[128,512]{1,0:T(8,128)(2,1)S(1)} %slice.132), channel_id=1, source_target_pairs={{0,2},{2,4},{4,6},{6,7},{7,5},{5,3},{3,1},{1,0},{8,10},{10,12},{12... | collective-permute-start | bytes 393224 | tf_op jit(solution)/shard_map/ppermute | solution.py:400
  142.1 6.1 %collective-permute-start.35 = (bf16[128,512]{1,0:T(8,128)(2,1)S(1)}, bf16[128,512]{1,0:T(8,128)(2,1)S(1)}, u32[]{:S(2)}, u32[]{:S(2)}) collective-permute-start(bf16[128,512]{1,0:T(8,128)(2,1)S(1)} %slice.133), channel_id=1, source_target_pairs={{0,1},{2,0},{4,2},{6,4},{7,6},{5,7},{3,5},{1,3},{8,9},{10,8},{12,1... | collective-permute-start | bytes 393224 | tf_op jit(solution)/shard_map/ppermute | solution.py:400
  148.3 6.4 %collective-permute-start.36 = (bf16[128,512]{1,0:T(8,128)(2,1)S(1)}, bf16[128,512]{1,0:T(8,128)(2,1)S(1)}, u32[]{:S(2)}, u32[]{:S(2)}) collective-permute-start(bf16[128,512]{1,0:T(8,128)(2,1)S(1)} %get-tuple-element.183), channel_id=1, source_target_pairs={{0,2},{2,4},{4,6},{6,7},{7,5},{5,3},{3,1},{1,0},{8,10},{10,12},{12... | collective-permute-start | bytes 393224 | tf_op jit(solution)/shard_map/ppermute | solution.py:400
  149.7 6.3 %collective-permute-start.37 = (bf16[128,512]{1,0:T(8,128)(2,1)S(1)}, bf16[128,512]{1,0:T(8,128)(2,1)S(1)}, u32[]{:S(2)}, u32[]{:S(2)}) collective-permute-start(bf16[128,512]{1,0:T(8,128)(2,1)S(1)} %get-tuple-element.184), channel_id=1, source_target_pairs={{0,1},{2,0},{4,2},{6,4},{7,6},{5,7},{3,5},{1,3},{8,9},{10,8},{12,1... | collective-permute-start | bytes 393224 | tf_op jit(solution)/shard_map/ppermute | solution.py:400
  156.0 8.6 %collective-permute-start.38 = (bf16[128,1024]{1,0:T(8,128)(2,1)S(1)}, bf16[128,1024]{1,0:T(8,128)(2,1)S(1)}, u32[]{:S(2)}, u32[]{:S(2)}) collective-permute-start(bf16[128,1024]{1,0:T(8,128)(2,1)S(1)} %pad_maximum_fusion.2), channel_id=1, source_target_pairs={{0,2},{2,4},{4,6},{6,7},{7,5},{5,3},{3,1},{1,0},{8,10},{10,12},{12... | collective-permute-start | bytes 786440 | tf_op jit(solution)/shard_map/ppermute | solution.py:400
  156.2 8.8 %collective-permute-start.39 = (bf16[128,1024]{1,0:T(8,128)(2,1)S(1)}, bf16[128,1024]{1,0:T(8,128)(2,1)S(1)}, u32[]{:S(2)}, u32[]{:S(2)}) collective-permute-start(bf16[128,1024]{1,0:T(8,128)(2,1)S(1)} %pad_maximum_fusion.3), channel_id=1, source_target_pairs={{0,1},{2,0},{4,2},{6,4},{7,6},{5,7},{3,5},{1,3},{8,9},{10,8},{12,1... | collective-permute-start | bytes 786440 | tf_op jit(solution)/shard_map/ppermute | solution.py:400
  158.1 11.0 %all-to-all-start.4 = ((bf16[8,16,640]{2,1,0:T(8,128)(2,1)}), bf16[8,16,640]{2,1,0:T(8,128)(2,1)S(1)}, u32[]{:S(2)}, u32[]{:S(2)}) async-start(bf16[8,16,640]{2,1,0:T(8,128)(2,1)} %bitcast.9), calls=%async_computation.4 | async-start | bytes 327680 | tf_op jit(solution)/shard_map/all_to_all | solution.py:444
  169.0 7.4 %collective-permute-start.40 = (bf16[128,1024]{1,0:T(8,128)(2,1)S(1)}, bf16[128,1024]{1,0:T(8,128)(2,1)S(1)}, u32[]{:S(2)}, u32[]{:S(2)}) collective-permute-start(bf16[128,1024]{1,0:T(8,128)(2,1)S(1)} %add_convert_fusion.9), channel_id=1, source_target_pairs={{0,2},{2,4},{4,6},{6,7},{7,5},{5,3},{3,1},{1,0},{8,10},{10,12},{12... | collective-permute-start | bytes 786440 | tf_op jit(solution)/shard_map/ppermute | solution.py:400
  169.2 7.3 %collective-permute-start.41 = (bf16[128,1024]{1,0:T(8,128)(2,1)S(1)}, bf16[128,1024]{1,0:T(8,128)(2,1)S(1)}, u32[]{:S(2)}, u32[]{:S(2)}) collective-permute-start(bf16[128,1024]{1,0:T(8,128)(2,1)S(1)} %add_convert_fusion.8), channel_id=1, source_target_pairs={{0,1},{2,0},{4,2},{6,4},{7,6},{5,7},{3,5},{1,3},{8,9},{10,8},{12,1... | collective-permute-start | bytes 786440 | tf_op jit(solution)/shard_map/ppermute | solution.py:400
  176.6 13.1 %collective-permute-start.42 = (bf16[128,1024]{1,0:T(8,128)(2,1)S(1)}, bf16[128,1024]{1,0:T(8,128)(2,1)S(1)}, u32[]{:S(2)}, u32[]{:S(2)}) collective-permute-start(bf16[128,1024]{1,0:T(8,128)(2,1)S(1)} %add_convert_fusion.7), channel_id=1, source_target_pairs={{0,2},{2,4},{4,6},{6,7},{7,5},{5,3},{3,1},{1,0},{8,10},{10,12},{12... | collective-permute-start | bytes 786440 | tf_op jit(solution)/shard_map/ppermute | solution.py:400
  176.7 12.9 %collective-permute-start.43 = (bf16[128,1024]{1,0:T(8,128)(2,1)S(1)}, bf16[128,1024]{1,0:T(8,128)(2,1)S(1)}, u32[]{:S(2)}, u32[]{:S(2)}) collective-permute-start(bf16[128,1024]{1,0:T(8,128)(2,1)S(1)} %add_convert_fusion.6), channel_id=1, source_target_pairs={{0,1},{2,0},{4,2},{6,4},{7,6},{5,7},{3,5},{1,3},{8,9},{10,8},{12,1... | collective-permute-start | bytes 786440 | tf_op jit(solution)/shard_map/ppermute | solution.py:400
  199.6 6.4 %collective-permute-start.46 = (bf16[128,1024]{1,0:T(8,128)(2,1)S(1)}, bf16[128,1024]{1,0:T(8,128)(2,1)S(1)}, u32[]{:S(2)}, u32[]{:S(2)}) collective-permute-start(bf16[128,1024]{1,0:T(8,128)(2,1)S(1)} %pad_maximum_fusion.4), channel_id=1, source_target_pairs={{0,2},{2,4},{4,6},{6,7},{7,5},{5,3},{3,1},{1,0},{8,10},{10,12},{12... | collective-permute-start | bytes 786440 | tf_op jit(solution)/shard_map/ppermute | solution.py:400
  200.7 6.4 %collective-permute-start.47 = (bf16[128,1024]{1,0:T(8,128)(2,1)S(1)}, bf16[128,1024]{1,0:T(8,128)(2,1)S(1)}, u32[]{:S(2)}, u32[]{:S(2)}) collective-permute-start(bf16[128,1024]{1,0:T(8,128)(2,1)S(1)} %pad_maximum_fusion.5), channel_id=1, source_target_pairs={{0,1},{2,0},{4,2},{6,4},{7,6},{5,7},{3,5},{1,3},{8,9},{10,8},{12,1... | collective-permute-start | bytes 786440 | tf_op jit(solution)/shard_map/ppermute | solution.py:400
  207.2 6.4 %collective-permute-start.48 = (bf16[128,1024]{1,0:T(8,128)(2,1)S(1)}, bf16[128,1024]{1,0:T(8,128)(2,1)S(1)}, u32[]{:S(2)}, u32[]{:S(2)}) collective-permute-start(bf16[128,1024]{1,0:T(8,128)(2,1)S(1)} %add_convert_fusion.5), channel_id=1, source_target_pairs={{0,2},{2,4},{4,6},{6,7},{7,5},{5,3},{3,1},{1,0},{8,10},{10,12},{12... | collective-permute-start | bytes 786440 | tf_op jit(solution)/shard_map/ppermute | solution.py:400
  208.0 6.4 %collective-permute-start.49 = (bf16[128,1024]{1,0:T(8,128)(2,1)S(1)}, bf16[128,1024]{1,0:T(8,128)(2,1)S(1)}, u32[]{:S(2)}, u32[]{:S(2)}) collective-permute-start(bf16[128,1024]{1,0:T(8,128)(2,1)S(1)} %add_convert_fusion.4), channel_id=1, source_target_pairs={{0,1},{2,0},{4,2},{6,4},{7,6},{5,7},{3,5},{1,3},{8,9},{10,8},{12,1... | collective-permute-start | bytes 786440 | tf_op jit(solution)/shard_map/ppermute | solution.py:400
  214.5 6.4 %collective-permute-start.50 = (bf16[128,1024]{1,0:T(8,128)(2,1)S(1)}, bf16[128,1024]{1,0:T(8,128)(2,1)S(1)}, u32[]{:S(2)}, u32[]{:S(2)}) collective-permute-start(bf16[128,1024]{1,0:T(8,128)(2,1)S(1)} %add_convert_fusion.3), channel_id=1, source_target_pairs={{0,2},{2,4},{4,6},{6,7},{7,5},{5,3},{3,1},{1,0},{8,10},{10,12},{12... | collective-permute-start | bytes 786440 | tf_op jit(solution)/shard_map/ppermute | solution.py:400
  215.1 6.4 %collective-permute-start.51 = (bf16[128,1024]{1,0:T(8,128)(2,1)S(1)}, bf16[128,1024]{1,0:T(8,128)(2,1)S(1)}, u32[]{:S(2)}, u32[]{:S(2)}) collective-permute-start(bf16[128,1024]{1,0:T(8,128)(2,1)S(1)} %add_convert_fusion.2), channel_id=1, source_target_pairs={{0,1},{2,0},{4,2},{6,4},{7,6},{5,7},{3,5},{1,3},{8,9},{10,8},{12,1... | collective-permute-start | bytes 786440 | tf_op jit(solution)/shard_map/ppermute | solution.py:400
  (29 other events, 250.9 us)
